TPU v7x, 32 devices: a whole 2x2x4 slice. The times are simulated.
32 devices in a mesh: sp: 8 (over z, y), dp: 4 (over x, core).
Axes of the slice: x: 2, y: 2, z: 4, core: 2. Of those that a mesh axis runs over, the one named last changes fastest.
Arguments:
- volume: bfloat16 [4, 96, 32, 8, 128], P('dp', None, 'sp'), may hold values from -6 to 6
- cotangent: bfloat16 [4, 96, 32, 8, 128], P('dp', None, 'sp'), may hold values from -6 to 6
- kernels_xy: bfloat16 [2, 96, 3, 3], replicated, may hold values from -2 to 2
- kernels_z: bfloat16 [2, 96, 3], replicated, may hold values from -3.5 to 3.5
- mixing: bfloat16 [2, 96, 96], replicated, may hold values from -0.625 to 0.625
Outputs:
- volume_grad: bfloat16 [4, 96, 32, 8, 128], P('dp', None, 'sp')
- mixing_grad: float32 [2, 96, 96], replicated
- xy_grad: float32 [2, 96, 3, 3], replicated
- z_grad: float32 [2, 96, 3], replicated
All inputs are finite; a program needn't handle non-finite values.
Results may differ from a plain program's by a relative error of at most 0.018.
Values may be sent and summed in bfloat16 or wider, within the bound.
No kernel may reach another device: no remote copies, remote signals or barrier semaphores. Data moves between devices by JAX's collectives and lax.ppermute only.
A program may use at most 64 MiB of HBM per device.

v0:
```python
import math

import jax
import jax.numpy as jnp
from jax import lax
from jax.sharding import PartitionSpec as P


def padded_2(x, sides, width):
    for axis, dim in sides:
        count, length = (lax.axis_size(axis), x.shape[dim])
        up = [(i, (i + 1) % count) for i in range(count - 1)]
        down = [(j, i) for i, j in up]
        last = lax.slice_in_dim(x, length - width, length, axis=dim)
        first = lax.slice_in_dim(x, 0, width, axis=dim)
        before = lax.ppermute(last, axis, up)
        after = lax.ppermute(first, axis, down)
        x = jnp.concatenate([before, x, after], axis=dim)
    return x


def conv_plane(inputs, kernel):
    extent = inputs.shape[1] - 2
    across = inputs.shape[3]
    padded = jnp.pad(inputs, ((0, 0), (0, 0), (0, 0), (1, 1)))
    summed = jnp.zeros((inputs.shape[0], extent, inputs.shape[2], across), jnp.float32)
    for row_tap in range(3):
        for col_tap in range(3):
            summed = summed + kernel[:, row_tap, col_tap][:, None, None, None] * padded[
                :, row_tap : row_tap + extent, :, col_tap : col_tap + across
            ].astype(jnp.float32)
    return summed


def conv_depth(inputs, kernel):
    depth_len = inputs.shape[2]
    padded = jnp.pad(inputs, ((0, 0), (0, 0), (1, 1), (0, 0)))
    summed = jnp.zeros(inputs.shape, jnp.float32)
    for depth_tap in range(3):
        summed = (
            summed
            + kernel[:, depth_tap][:, None, None, None]
            * padded[:, :, depth_tap : depth_tap + depth_len, :]
        )
    return summed


def mix_channels(weights, inputs):
    channels = inputs.shape[0]
    flat = inputs.reshape(channels, -1)
    return jnp.dot(weights, flat, preferred_element_type=jnp.float32).reshape(inputs.shape)


def forward_block(inputs, kernel_xy, kernel_z, weights):
    planar = conv_plane(inputs, kernel_xy)
    axial = conv_depth(planar, kernel_z).astype(jnp.bfloat16)
    preact = mix_channels(weights, axial)
    return (planar, axial, preact)


def silu_slope(preact):
    sigma = jax.nn.sigmoid(preact)
    return sigma * (1.0 + preact * (1.0 - sigma))


def backward_block(grad_out, planar, axial, preact, around, kernel_z, weights, trim):
    grad_pre = (grad_out.astype(jnp.float32) * silu_slope(preact)).astype(jnp.bfloat16)
    channels = grad_pre.shape[0]
    grad_axial = jnp.dot(
        weights.T, grad_pre.reshape(channels, -1), preferred_element_type=jnp.float32
    ).reshape(grad_pre.shape)
    grad_planar = conv_depth(grad_axial, kernel_z[:, ::-1]).astype(jnp.bfloat16)
    extent = grad_pre.shape[1]
    own_extent = extent - 2 * trim
    own_pre = grad_pre.reshape(channels, -1)
    own_axial = axial.reshape(channels, -1)
    grad_weights = lax.dot_general(
        own_pre, own_axial, (((1,), (1,)), ((), ())), preferred_element_type=jnp.float32
    )
    depth_len = planar.shape[2]
    planar_pad = jnp.pad(planar, ((0, 0), (0, 0), (1, 1), (0, 0)))
    grad_kz = jnp.stack(
        [
            jnp.sum(
                grad_axial * planar_pad[:, :, depth_tap : depth_tap + depth_len, :], axis=(1, 2, 3)
            )
            for depth_tap in range(3)
        ],
        axis=1,
    )
    own_grad_planar = grad_planar.astype(jnp.float32)
    across = around.shape[3]
    around_pad = jnp.pad(around, ((0, 0), (0, 0), (0, 0), (1, 1)))
    rows_list = []
    for row_tap in range(3):
        cols_list = []
        for col_tap in range(3):
            cols_list.append(
                jnp.sum(
                    own_grad_planar
                    * around_pad[
                        :, row_tap : row_tap + own_extent, :, col_tap : col_tap + across
                    ].astype(jnp.float32),
                    axis=(1, 2, 3),
                )
            )
        rows_list.append(jnp.stack(cols_list, axis=1))
    grad_kxy = jnp.stack(rows_list, axis=1)
    return (grad_planar, (grad_weights, grad_kxy, grad_kz))


def edge_grads(grad_planar):
    return padded_2(grad_planar, (("sp", 1),), 1)


def settle_all(lower, upper):
    summed = lax.psum((lower[0], lower[1], lower[2], upper[0], upper[1], upper[2]), ("sp", "dp"))
    return ((summed[0], summed[1], summed[2]), (summed[3], summed[4], summed[5]))


def on_device(volume, cotangent, kernels_xy, kernels_z, mixing):
    inputs = volume[0]
    grad_top = cotangent[0]
    kernel_xy = kernels_xy.astype(jnp.float32)
    kernel_z = kernels_z.astype(jnp.float32)
    slab_len = inputs.shape[1]
    ranks = lax.axis_size("sp")
    place = lax.axis_index("sp")
    wide = padded_2(inputs, (("sp", 1),), 2)
    planar1, axial1, preact1 = forward_block(wide, kernel_xy[0], kernel_z[0], mixing[0])
    hidden = jax.nn.silu(preact1).astype(jnp.bfloat16)
    spots = place * slab_len - 1 + jnp.arange(slab_len + 2, dtype=jnp.int32)
    hidden = jnp.where(
        ((spots >= 0) & (spots < slab_len * ranks))[None, :, None, None],
        hidden,
        jnp.zeros_like(hidden),
    )
    planar2, axial2, preact2 = forward_block(hidden, kernel_xy[1], kernel_z[1], mixing[1])
    grad_planar2, upper = backward_block(
        grad_top, planar2, axial2, preact2, hidden, kernel_z[1], mixing[1], 0
    )
    grad_hidden = conv_plane(edge_grads(grad_planar2), kernel_xy[1][:, ::-1, ::-1]).astype(
        jnp.bfloat16
    )
    grad_planar1, lower = backward_block(
        grad_hidden,
        planar1[:, 1:-1],
        axial1[:, 1:-1],
        preact1[:, 1:-1],
        wide[:, 1:-1],
        kernel_z[0],
        mixing[0],
        0,
    )
    grad_inputs = conv_plane(edge_grads(grad_planar1), kernel_xy[0][:, ::-1, ::-1]).astype(
        jnp.bfloat16
    )
    lower, upper = settle_all(lower, upper)
    factor = 1.0 / math.sqrt(
        lax.axis_size("dp") * slab_len * ranks * inputs.shape[2] * inputs.shape[3]
    )
    mixing_grad = jnp.stack([lower[0], upper[0]]) * factor
    xy_grad = jnp.stack([lower[1], upper[1]]) * factor
    z_grad = jnp.stack([lower[2], upper[2]]) * factor
    return (grad_inputs[None], mixing_grad, xy_grad, z_grad)


def solution(mesh):
    return jax.shard_map(
        on_device,
        mesh=mesh,
        in_specs=(P("dp", None, "sp", None, None), P("dp", None, "sp", None, None), P(), P(), P()),
        out_specs=(P("dp", None, "sp", None, None), P(), P(), P()),
        check_vma=False,
    )
```

profile of v0, /device:TPU:0, one launch (start us, length us, event | category | flops | bytes accessed | tf_op | source)
XLA Modules:
  0.0 220.1 jit_solution(7302605697710774105)
XLA Ops:
  7.2 1.5 copy.76
  8.8 4.9 %collective-permute-start = (bf16[96,2,8,128]{3,0,2,1:T(8,128)(2,1)S(1)}, bf16[96,2,8,128]{3,0,2,1:T(8,128)(2,1)S(1)}, u32[]{:S(2)}, u32[]{:S(2)}) collective-permute-start(bf16[96,2,8,128]{3,0,2,1:T(8,128)(2,1)S(1)} %get-tuple-element.61), channel_id=1, source_target_pairs={{0,4},{4,8},{8,12},{12,16},{16,20},{20,24},{24,28},{1,5},{5,9},{9,... | collective-permute-start | bytes 1179656 | tf_op jit(solution)/shard_map/ppermute | solution.py:16
  13.7 1.3 collective-permute-start.1
  15.2 1.5 reshape.101
  16.6 13.8 %collective-permute-done = bf16[96,2,8,128]{3,0,2,1:T(8,128)(2,1)S(1)} collective-permute-done((bf16[96,2,8,128]{3,0,2,1:T(8,128)(2,1)S(1)}, bf16[96,2,8,128]{3,0,2,1:T(8,128)(2,1)S(1)}, u32[]{:S(2)}, u32[]{:S(2)}) %collective-permute-start) | collective-permute-done | bytes 393248 | tf_op jit(solution)/shard_map/ppermute | solution.py:16
  30.7 3.1 %multiply_add_fusion = f32[96,6,8,128]{3,0,2,1:T(8,128)S(1)} fusion(bf16[96,2,8,128]{3,0,2,1:T(8,128)(2,1)S(1)} %collective-permute-done.1, bf16[96,4,8,128]{3,0,2,1:T(8,128)(2,1)S(1)} %bitcast.190, bf16[96,2,8,128]{3,0,2,1:T(8,128)(2,1)S(1)} %collective-permute-done, bf16[96,8,8,128]{3,0,2,1:T(8,128)(2,1)S(1)} %pad_maximum_fusion, ...), kind=kLoop, calls=%fused_computation.66 | loop fusion | flops 18874368 | bytes 6689280 | tf_op jit(solution)/shard_map/add | solution.py:29
  33.8 1.4 copy-done
  38.0 3.0 %fusion.24 = f32[96,4,8,128]{3,2,1,0:T(8,128)S(1)} fusion(f32[96]{0:T(128)S(1)} %get-tuple-element.64, f32[96]{0:T(128)S(1)} %get-tuple-element.65, f32[96]{0:T(128)S(1)} %get-tuple-element.66, f32[96]{0:T(128)S(1)} %get-tuple-element.67, f32[96]{0:T(128)S(1)} %get-tuple-element.68, f32[96]{0:T(128)S(1)} %get-tuple-element.69, f32[96]{0:T(128)S(1)} %get-tuple-element.70, ...), kind=kLoop, calls=%fused_computation.88 | loop fusion | flops 10223616 | bytes 5116416 | tf_op jit(solution)/shard_map/add | solution.py:29
  44.1 6.6 %multiply_reduce_fusion.2 = (f32[96]{0:T(128)S(1)}, f32[96]{0:T(128)S(1)}, f32[96]{0:T(128)S(1)}, f32[96]{0:T(128)S(1)}, f32[96]{0:T(128)S(1)}, /*index=5*/f32[9...) fusion(f32[96,4,8,128]{3,2,1,0:T(8,128)S(1)} %bitcast.196, ...), kind=kLoop, calls=%fused_computation.147 | loop fusion | flops 15727488 | bytes 7477248 | tf_op jit(solution)/shard_map/reduce_sum | solution.py:84
  50.8 4.4 %collective-permute-start.2 = (bf16[96,1,8,128]{3,2,1,0:T(8,128)(2,1)S(1)}, bf16[96,1,8,128]{3,2,1,0:T(8,128)(2,1)S(1)}, u32[]{:S(2)}, u32[]{:S(2)}) collective-permute-start(bf16[96,1,8,128]{3,2,1,0:T(8,128)(2,1)S(1)} %get-tuple-element.59), channel_id=1, source_target_pairs={{0,4},{4,8},{8,12},{12,16},{16,20},{20,24},{24,28},{1,5},{5,9},{9,... | collective-permute-start | bytes 589832 | tf_op jit(solution)/shard_map/ppermute | solution.py:16
  55.2 1.5 collective-permute-start.3
  58.8 1.2 convolution_bitcast_fusion.3
  59.9 4.3 %collective-permute-done.3 = bf16[96,1,8,128]{3,2,1,0:T(8,128)(2,1)S(1)} collective-permute-done((bf16[96,1,8,128]{3,2,1,0:T(8,128)(2,1)S(1)}, bf16[96,1,8,128]{3,2,1,0:T(8,128)(2,1)S(1)}, u32[]{:S(2)}, u32[]{:S(2)}) %collective-permute-start.3) | collective-permute-done | bytes 196640 | tf_op jit(solution)/shard_map/ppermute | solution.py:17
  64.3 1.5 fusion.9
  65.8 3.5 %multiply_convert_fusion.1 = bf16[96,4,8,128]{3,2,1,0:T(8,128)(2,1)S(1)} fusion(f32[96,6,8,128]{3,2,1,0:T(8,128)S(1)} %bitcast.193, bf16[96,6,8,130]{3,2,1,0:T(8,128)(2,1)S(1)} %fusion.9, f32[96]{0:T(128)S(1)} %get-tuple-element.71, bf16[96,1,8,128]{3,2,1,0:T(8,128)(2,1)S(1)} %collective-permute-done.3, bf16[96,4,8,128]{3,2,1,0:T(8,128)(2,1)S(1)} %get-tuple-element.56, ...), kind=kLoop, calls=%fused_computation.149 | loop fusion | flops 15335424 | bytes 8260992 | tf_op jit(solution)/shard_map/convert_element_type | solution.py:67
  72.6 1.4 fusion.31
  74.6 2.8 %fusion.60 = (f32[96]{0:T(128)S(1)}, f32[96]{0:T(128)S(1)}, f32[96]{0:T(128)S(1)}, f32[96]{0:T(128)S(1)}, f32[96]{0:T(128)S(1)}, /*index=5*/f32[96]{0:T(128)S(1)...) fusion(bf16[96,6,8,128]{3,0,2,1:T(8,128)(2,1)S(1)} %slice-done.1, ...), kind=kLoop, calls=%fused_computation.124 | loop fusion | flops 15727776 | bytes 5902848 | tf_op jit(solution)/shard_map/reduce_sum | solution.py:99
  78.1 4.5 %collective-permute-start.4 = (bf16[96,1,8,128]{3,0,2,1:T(8,128)(2,1)S(1)}, bf16[96,1,8,128]{3,0,2,1:T(8,128)(2,1)S(1)}, u32[]{:S(2)}, u32[]{:S(2)}) collective-permute-start(bf16[96,1,8,128]{3,0,2,1:T(8,128)(2,1)S(1)} %get-tuple-element.57), channel_id=1, source_target_pairs={{0,4},{4,8},{8,12},{12,16},{16,20},{20,24},{24,28},{1,5},{5,9},{9,... | collective-permute-start | bytes 589832 | tf_op jit(solution)/shard_map/ppermute | solution.py:16
  82.7 1.3 collective-permute-start.5
  84.0 120.5 %all-reduce.13.cloned.1.call-done = (f32[1,96,96]{2,1,0:T(8,128)}, f32[1,96,96]{2,1,0:T(8,128)}, f32[1,96,3,3]{1,3,2,0:T(4,128)}, f32[1,96,3,3]{1,3,2,0:T(4,128)...) async-done(((f32[1,96,96]{2,1,0:T(8,128)}, f32[1,96,96]{2,1,0:T(8,128)}, f32[1,96,3,3]{1,3,2,0:T(4,128)}, f32[1,96,3,3]{1,3,2,0:T(4,128)}, f32[1,96,3]{1,2,0:T(4,128)}, ...) | async-done | bytes 82960 | tf_op jit(solution)/shard_map/psum | solution.py:117
  207.0 1.5 maximum_multiply_fusion
  208.5 1.6 fusion.11
  210.1 2.0 fusion.92
  212.1 1.2 copy.31
  (68 shorter events, 15.5 us)
Async XLA Ops:
  7.2 7.9 %copy-start.7 = (bf16[2,96,3,3]{1,0,3,2:T(2,128)(2,1)S(1)}, bf16[2,96,3,3]{1,0,3,2:T(2,128)(2,1)}, u32[]{:S(2)}) copy-start(bf16[2,96,3,3]{1,0,3,2:T(2,128)(2,1)} %param.7) | copy-start | bytes 10372
  7.2 7.9 %copy-start.8 = (bf16[2,96,3]{1,0,2:T(2,128)(2,1)S(1)}, bf16[2,96,3]{1,0,2:T(2,128)(2,1)}, u32[]{:S(2)}) copy-start(bf16[2,96,3]{1,0,2:T(2,128)(2,1)} %param.8) | copy-start | bytes 3460
  7.2 8.0 %copy-start.4 = (bf16[1,96,4,8,128]{4,3,2,1,0:T(8,128)(2,1)S(1)}, bf16[1,96,4,8,128]{4,3,2,1,0:T(8,128)(2,1)}, u32[]{:S(2)}) copy-start(bf16[1,96,4,8,128]{4,3,2,1,0:T(8,128)(2,1)} %param.6) | copy-start | bytes 2359300
  7.2 197.3 %all-reduce.13.cloned.1.call-start = ((), (), s32[]{:S(2)}) async-start(), calls=%async_computation | async-start | bytes 229376 | tf_op jit(solution)/shard_map/psum | solution.py:117
  8.8 21.7 %collective-permute-start = (bf16[96,2,8,128]{3,0,2,1:T(8,128)(2,1)S(1)}, bf16[96,2,8,128]{3,0,2,1:T(8,128)(2,1)S(1)}, u32[]{:S(2)}, u32[]{:S(2)}) collective-permute-start(bf16[96,2,8,128]{3,0,2,1:T(8,128)(2,1)S(1)} %get-tuple-element.61), channel_id=1, source_target_pairs={{0,4},{4,8},{8,12},{12,16},{16,20},{20,24},{24,28},{1,5},{5,9},{9,... | collective-permute-start | bytes 1179656 | tf_op jit(solution)/shard_map/ppermute | solution.py:16
  13.7 16.8 %collective-permute-start.1 = (bf16[96,2,8,128]{3,0,2,1:T(8,128)(2,1)S(1)}, bf16[96,2,8,128]{3,0,2,1:T(8,128)(2,1)S(1)}, u32[]{:S(2)}, u32[]{:S(2)}) collective-permute-start(bf16[96,2,8,128]{3,0,2,1:T(8,128)(2,1)S(1)} %get-tuple-element.62), channel_id=1, source_target_pairs={{4,0},{8,4},{12,8},{16,12},{20,16},{24,20},{28,24},{5,1},{9,5},{13... | collective-permute-start | bytes 1179656 | tf_op jit(solution)/shard_map/ppermute | solution.py:17
  30.7 3.1 %copy-start.2 = (bf16[96,8,8,128]{3,0,2,1:T(8,128)(2,1)}, bf16[96,8,8,128]{3,0,2,1:T(8,128)(2,1)S(1)}, u32[]{:S(2)}) copy-start(bf16[96,8,8,128]{3,0,2,1:T(8,128)(2,1)S(1)} %pad_maximum_fusion) | copy-start | bytes 4718596
  33.7 1.4 copy-start
  35.7 0.8 copy-start.6
  41.6 1.4 copy-start.5
  50.8 9.2 %collective-permute-start.2 = (bf16[96,1,8,128]{3,2,1,0:T(8,128)(2,1)S(1)}, bf16[96,1,8,128]{3,2,1,0:T(8,128)(2,1)S(1)}, u32[]{:S(2)}, u32[]{:S(2)}) collective-permute-start(bf16[96,1,8,128]{3,2,1,0:T(8,128)(2,1)S(1)} %get-tuple-element.59), channel_id=1, source_target_pairs={{0,4},{4,8},{8,12},{12,16},{16,20},{20,24},{24,28},{1,5},{5,9},{9,... | collective-permute-start | bytes 589832 | tf_op jit(solution)/shard_map/ppermute | solution.py:16
  55.2 9.1 %collective-permute-start.3 = (bf16[96,1,8,128]{3,2,1,0:T(8,128)(2,1)S(1)}, bf16[96,1,8,128]{3,2,1,0:T(8,128)(2,1)S(1)}, u32[]{:S(2)}, u32[]{:S(2)}) collective-permute-start(bf16[96,1,8,128]{3,2,1,0:T(8,128)(2,1)S(1)} %get-tuple-element.60), channel_id=1, source_target_pairs={{4,0},{8,4},{12,8},{16,12},{20,16},{24,20},{28,24},{5,1},{9,5},{13... | collective-permute-start | bytes 589832 | tf_op jit(solution)/shard_map/ppermute | solution.py:17
  70.4 1.7 copy-start.1
  70.8 1.8 slice-start
  72.6 2.0 slice-start.1
  72.6 2.0 copy-start.3
  78.1 130.4 %collective-permute-start.4 = (bf16[96,1,8,128]{3,0,2,1:T(8,128)(2,1)S(1)}, bf16[96,1,8,128]{3,0,2,1:T(8,128)(2,1)S(1)}, u32[]{:S(2)}, u32[]{:S(2)}) collective-permute-start(bf16[96,1,8,128]{3,0,2,1:T(8,128)(2,1)S(1)} %get-tuple-element.57), channel_id=1, source_target_pairs={{0,4},{4,8},{8,12},{12,16},{16,20},{20,24},{24,28},{1,5},{5,9},{9,... | collective-permute-start | bytes 589832 | tf_op jit(solution)/shard_map/ppermute | solution.py:16
  82.7 125.8 %collective-permute-start.5 = (bf16[96,1,8,128]{3,0,2,1:T(8,128)(2,1)S(1)}, bf16[96,1,8,128]{3,0,2,1:T(8,128)(2,1)S(1)}, u32[]{:S(2)}, u32[]{:S(2)}) collective-permute-start(bf16[96,1,8,128]{3,0,2,1:T(8,128)(2,1)S(1)} %get-tuple-element.58), channel_id=1, source_target_pairs={{4,0},{8,4},{12,8},{16,12},{20,16},{24,20},{28,24},{5,1},{9,5},{13... | collective-permute-start | bytes 589832 | tf_op jit(solution)/shard_map/ppermute | solution.py:17
Sparse Core Ops, SparseCore 0:
  78.2 126.1 all-reduce.12
where the time goes:
time: 221 us; the launch traced here: 220 us
  waiting for transfers between devices  139 us (63%)
  other arithmetic  33.4 us (15%)
  starting transfers between devices  17.9 us (8%)
  between operations  14.4 us (7%)
  local copies, waits for them, and re-layouts  11.5 us (5%)
  matrix products  4.28 us (2%)
    psum x1, waiting for transfers between devices, settle_all(): lax.psum((lower[0], lower[1], lower[2], upper[0], upper[1], upper[2]), ('...  120 us
    ppermute x3, waiting for transfers between devices, padded_2(): before = lax.ppermute(last, axis, up)  13.8 us
    ppermute x3, starting transfers between devices, padded_2(): before = lax.ppermute(last, axis, up)  13.8 us
    unnamed x28, local copies, waits for them, and re-layouts  8.82 us
    reduce_sum x2, other arithmetic, backward_block(): jnp.sum(grad_axial * planar_pad[:, :, depth_tap:depth_tap + depth_len, :]...  7.96 us
    add x2, other arithmetic, conv_plane(): summed + kernel[:, row_tap, col_tap][:, None, None, None] * padded[:, row...  6.08 us
  transfers between devices with their start and end apart: 7, of which 3 were waited for; matrix products, arithmetic and copies ran while one was open for 4% of the time, Pallas kernels for 0%

commit v1 on v0

--- a/solution.py
+++ b/solution.py
@@ -113,8 +113,24 @@
     return padded_2(grad_planar, (("sp", 1),), 1)
 
 
+def all_sum(total):
+    for axis in ("dp", "sp"):
+        count, step = (lax.axis_size(axis), 1)
+        while step < count:
+            total = total + lax.ppermute(total, axis, [(i, i ^ step) for i in range(count)])
+            step *= 2
+    return total
+
+
 def settle_all(lower, upper):
-    summed = lax.psum((lower[0], lower[1], lower[2], upper[0], upper[1], upper[2]), ("sp", "dp"))
+    parts = (lower[0], lower[1], lower[2], upper[0], upper[1], upper[2])
+    flat = jnp.concatenate([part.reshape(-1) for part in parts])
+    flat = jnp.pad(flat, (0, -flat.size % 1024)).reshape(-1, 128)
+    flat = all_sum(flat).reshape(-1)
+    summed, at = ([], 0)
+    for part in parts:
+        summed.append(flat[at : at + part.size].reshape(part.shape))
+        at += part.size
     return ((summed[0], summed[1], summed[2]), (summed[3], summed[4], summed[5]))
 
 

time: 221 us -> 125 us (0.57)
  waiting for transfers between devices: 139 us -> 22.6 us
  local copies, waits for them, and re-layouts: 11.5 us -> 26.4 us
  between operations: 14.4 us -> 1.63 us
  starting transfers between devices: 17.9 us -> 30.1 us
  other arithmetic: 33.4 us -> 39.3 us
    psum x1 -> x0, waiting for transfers between devices: 120 us -> none  [settle_all(): lax.psum((lower[0], lower[1], lower[2], upper[0], upper[1], upper[2]), ('...]
    ppermute x0 -> x5, starting transfers between devices: none -> 11.5 us  [all_sum(): lax.ppermute(total, axis, [(i, i ^ step) for i in range(count)])]
    ppermute x0 -> x5, waiting for transfers between devices: none -> 8.8 us  [all_sum(): lax.ppermute(total, axis, [(i, i ^ step) for i in range(count)])]
    reshape x0 -> x7, local copies, waits for them, and re-layouts: none -> 4.87 us  [the longest x6 4.86 us: settle_all(): flat = jnp.concatenate([part.reshape(-1) for part in parts])]
    another operation x0 -> x14, local copies, waits for them, and re-layouts: none -> 3.2 us  [the longest x2 0.98 us: backward_block(): grad_kxy = jnp.stack(rows_list, axis=1)]
    unnamed x28 -> x120, local copies, waits for them, and re-layouts: 8.82 us -> 11.9 us
    ppermute x3, waiting for transfers between devices: 4.33 us -> 1.63 us  [padded_2(): after = lax.ppermute(first, axis, down)]
    another operation x4 -> x2, other arithmetic: 2.4 us -> 0.02 us  [backward_block(): jnp.stack([jnp.sum(grad_axial * planar_pad[:, :, depth_tap:depth_tap + de...]
  transfers between devices with their start and end apart: 7 -> 11, of which waited for: 3 -> 5; matrix products, arithmetic and copies ran while one was open for 4% -> 10% of each run, Pallas kernels for 0% -> 0%
where the time goes in v1:
time: 125 us; the launch traced here: 124 us
  other arithmetic  39.3 us (31%)
  starting transfers between devices  30.1 us (24%)
  local copies, waits for them, and re-layouts  26.4 us (21%)
  waiting for transfers between devices  22.6 us (18%)
  matrix products  4.25 us (3%)
  between operations  1.63 us (1%)
    ppermute x3, starting transfers between devices, padded_2(): before = lax.ppermute(last, axis, up)  14.5 us
    ppermute x3, waiting for transfers between devices, padded_2(): before = lax.ppermute(last, axis, up)  12.2 us
    unnamed x120, local copies, waits for them, and re-layouts  11.9 us
    ppermute x5, starting transfers between devices, all_sum(): lax.ppermute(total, axis, [(i, i ^ step) for i in range(count)])  11.5 us
    reduce_sum x2, other arithmetic, backward_block(): jnp.sum(grad_axial * planar_pad[:, :, depth_tap:depth_tap + depth_len, :]...  10.1 us
    ppermute x5, waiting for transfers between devices, all_sum(): lax.ppermute(total, axis, [(i, i ^ step) for i in range(count)])  8.8 us
    add x2, other arithmetic, conv_plane(): summed + kernel[:, row_tap, col_tap][:, None, None, None] * padded[:, row...  6.98 us
    convert_element_type x2, other arithmetic, backward_block(): (grad_out.astype(jnp.float32) * silu_slope(preact)).astype(jnp.bfloat16)  5.05 us
  transfers between devices with their start and end apart: 11, of which 5 were waited for; matrix products, arithmetic and copies ran while one was open for 10% of the time, Pallas kernels for 0%

profile of v1, /device:TPU:0, one launch (start us, length us, event | category | flops | bytes accessed | tf_op | source)
XLA Modules:
  0.0 124.3 jit_solution(3493584855756208972)
XLA Ops:
  0.7 1.5 %copy.97 = bf16[1,96,4,8,128]{4,1,3,2,0:T(8,128)(2,1)S(1)} copy(bf16[1,96,4,8,128]{4,3,2,1,0:T(8,128)(2,1)} %param.5) | data formatting | bytes 1572864 | tf_op args[0]
  2.2 4.9 %collective-permute-start = (bf16[96,2,8,128]{3,0,2,1:T(8,128)(2,1)S(1)}, bf16[96,2,8,128]{3,0,2,1:T(8,128)(2,1)S(1)}, u32[]{:S(2)}, u32[]{:S(2)}) collective-permute-start(bf16[96,2,8,128]{3,0,2,1:T(8,128)(2,1)S(1)} %get-tuple-element.59), channel_id=1, source_target_pairs={{0,4},{4,8},{8,12},{12,16},{16,20},{20,24},{24,28},{1,5},{5,9},{9,... | collective-permute-start | bytes 1179656 | tf_op jit(solution)/shard_map/ppermute | solution.py:16
  10.2 1.5 %reshape.137 = f32[96,4096]{1,0:T(8,128)} reshape(bf16[1,96,4,8,128]{4,3,2,1,0:T(8,128)(2,1)S(1)} %copy-done.9) | data formatting | bytes 2359296 | tf_op jit(solution)/shard_map/convert_element_type | solution.py:67
  11.7 12.2 %collective-permute-done = bf16[96,2,8,128]{3,0,2,1:T(8,128)(2,1)S(1)} collective-permute-done((bf16[96,2,8,128]{3,0,2,1:T(8,128)(2,1)S(1)}, bf16[96,2,8,128]{3,0,2,1:T(8,128)(2,1)S(1)}, u32[]{:S(2)}, u32[]{:S(2)}) %collective-permute-start) | collective-permute-done | bytes 393248 | tf_op jit(solution)/shard_map/ppermute | solution.py:16
  25.3 4.0 %multiply_add_fusion = f32[96,6,8,128]{3,0,2,1:T(8,128)S(1)} fusion(bf16[96,2,8,128]{3,0,2,1:T(8,128)(2,1)} %copy-done.7, bf16[96,4,8,128]{3,0,2,1:T(8,128)(2,1)S(1)} %bitcast.185, bf16[96,2,8,128]{3,0,2,1:T(8,128)(2,1)S(1)} %collective-permute-done, bf16[96,8,8,128]{3,0,2,1:T(8,128)(2,1)S(1)} %pad_maximum_fusion, f32[96]{0:T(128)S(1)} %copy-done.32, ...), kind=kLoop, calls=%fused_computation.66 | loop fusion | flops 18874368 | bytes 6689280 | tf_op jit(solution)/shard_map/add | solution.py:29
  34.0 3.0 %fusion.24 = f32[96,4,8,128]{3,2,1,0:T(8,128)S(1)} fusion(f32[96]{0:T(128)S(1)} %get-tuple-element.68, f32[96]{0:T(128)S(1)} %get-tuple-element.69, f32[96]{0:T(128)S(1)} %get-tuple-element.70, f32[96]{0:T(128)S(1)} %get-tuple-element.71, f32[96]{0:T(128)S(1)} %get-tuple-element.72, f32[96]{0:T(128)S(1)} %get-tuple-element.73, f32[96]{0:T(128)S(1)} %get-tuple-element.74, ...), kind=kLoop, calls=%fused_computation.88 | loop fusion | flops 10223616 | bytes 5116416 | tf_op jit(solution)/shard_map/add | solution.py:29
  40.8 7.8 %multiply_reduce_fusion.2 = (f32[96]{0:T(128)S(1)}, f32[96]{0:T(128)S(1)}, f32[96]{0:T(128)S(1)}, f32[96]{0:T(128)}, f32[96]{0:T(128)S(1)}, /*index=5*/f32[96]{0...) fusion(f32[96,4,8,128]{3,2,1,0:T(8,128)S(1)} %bitcast.191, ...), kind=kLoop, calls=%fused_computation.147 | loop fusion | flops 15727488 | bytes 7477248 | tf_op jit(solution)/shard_map/reduce_sum | solution.py:84
  54.1 1.8 %fusion.106 = (bf16[96,1,8,128]{3,2,1,0:T(8,128)(2,1)}, bf16[96,1,8,128]{3,2,1,0:T(8,128)(2,1)}) fusion(bf16[96,4,8,128]{3,2,1,0:T(8,128)(2,1)} %get-tuple-element.53), kind=kLoop, calls=%fused_computation.235 | loop fusion | bytes 786432 | tf_op jit(solution)/shard_map/slice | solution.py:14
  56.0 5.1 %collective-permute-start.2 = (bf16[96,1,8,128]{3,2,1,0:T(8,128)(2,1)}, bf16[96,1,8,128]{3,2,1,0:T(8,128)(2,1)}, u32[]{:S(2)}, u32[]{:S(2)}) collective-permute-start(bf16[96,1,8,128]{3,2,1,0:T(8,128)(2,1)} %get-tuple-element.57), channel_id=1, source_target_pairs={{0,4},{4,8},{8,12},{12,16},{16,20},{20,24},{24,28},{1,5},{5,9},{9,... | collective-permute-start | bytes 589832 | tf_op jit(solution)/shard_map/ppermute | solution.py:16
  62.5 1.8 %copy.67 = f32[12,8,32,128]{3,2,1,0:T(8,128)S(1)} copy(f32[12,8,32,128]{3,1,2,0:T(8,128)} %bitcast.189) | data formatting | bytes 3145728
  66.6 1.5 %reshape.132 = f32[9216]{0:T(1024)} reshape(f32[96,96]{1,0:T(8,128)} %convolution_bitcast_fusion.3) | data formatting | bytes 73728 | tf_op jit(solution)/shard_map/reshape | solution.py:127
  68.2 1.6 %collective-permute-done.3 = bf16[96,1,8,128]{3,2,1,0:T(8,128)(2,1)} collective-permute-done((bf16[96,1,8,128]{3,2,1,0:T(8,128)(2,1)}, bf16[96,1,8,128]{3,2,1,0:T(8,128)(2,1)}, u32[]{:S(2)}, u32[]{:S(2)}) %collective-permute-start.3) | collective-permute-done | bytes 196640 | tf_op jit(solution)/shard_map/ppermute | solution.py:17
  69.8 2.6 %fusion.9 = bf16[96,6,8,130]{3,2,1,0:T(8,128)(2,1)S(1)} fusion(bf16[96,1,8,128]{3,2,1,0:T(8,128)(2,1)} %collective-permute-done.3, bf16[96,4,8,128]{3,2,1,0:T(8,128)(2,1)} %get-tuple-element.53, bf16[96,1,8,128]{3,2,1,0:T(8,128)(2,1)} %collective-permute-done.2), kind=kLoop, calls=%fused_computation.57 | loop fusion | flops 7188480 | bytes 2377728 | tf_op jit(solution)/shard_map/concatenate | solution.py:18
  72.5 4.5 %multiply_convert_fusion.1 = bf16[96,4,8,128]{3,2,1,0:T(8,128)(2,1)S(1)} fusion(f32[96,6,8,128]{3,2,1,0:T(8,128)S(1)} %bitcast.188, bf16[96,6,8,130]{3,2,1,0:T(8,128)(2,1)S(1)} %fusion.9, f32[96]{0:T(128)S(1)} %copy-done.54, bf16[96,1,8,128]{3,2,1,0:T(8,128)(2,1)} %collective-permute-done.3, bf16[96,4,8,128]{3,2,1,0:T(8,128)(2,1)S(1)} %copy-done.3, ...), kind=kLoop, calls=%fused_computation.149 | loop fusion | flops 15335424 | bytes 8260992 | tf_op jit(solution)/shard_map/convert_element_type | solution.py:67
  80.2 2.3 %fusion.31 = (f32[96]{0:T(128)S(1)}, f32[96]{0:T(128)S(1)}, f32[96]{0:T(128)S(1)}, f32[96,4,8,128]{3,0,2,1:T(8,128)}) fusion(f32[96,4,8,128]{3,0,2,1:T(8,128)S(1)} %slice-done, f32[96,4,8,128]{3,2,1,0:T(8,128)S(1)} %bitcast.192, f32[96,6,8,128]{3,0,2,1:T(8,128)S(1)} %copy-done.1), kind=kLoop, calls=%fused_computation.95 | loop fusion | flops 2359008 | bytes 6292608 | tf_op jit(solution)/shard_map/reduce_sum | solution.py:84
  82.9 4.6 %fusion.60 = (f32[96]{0:T(128)S(1)}, f32[96]{0:T(128)S(1)}, f32[96]{0:T(128)S(1)}, f32[96]{0:T(128)S(1)}, f32[96]{0:T(128)S(1)}, /*index=5*/f32[96]{0:T(128)S(1)...) fusion(bf16[96,6,8,128]{3,0,2,1:T(8,128)(2,1)S(1)} %slice-done.1, ...), kind=kLoop, calls=%fused_computation.124 | loop fusion | flops 15727776 | bytes 5902848 | tf_op jit(solution)/shard_map/reduce_sum | solution.py:99
  91.1 1.5 %collective-permute-start.7 = (f32[168,128]{1,0:T(8,128)S(1)}, f32[168,128]{1,0:T(8,128)S(1)}, u32[]{:S(2)}, u32[]{:S(2)}) collective-permute-start(f32[168,128]{1,0:T(8,128)S(1)} %fusion.102), channel_id=1, source_target_pairs={{0,2},{1,3},{2,0},{3,1},{4,6},{5,7},{6,4},{7,5},{8,10},{9,11},{10,... | collective-permute-start | bytes 258056 | tf_op jit(solution)/shard_map/ppermute | solution.py:120
  92.6 4.6 %collective-permute-start.4 = (bf16[96,1,8,128]{3,0,2,1:T(8,128)(2,1)S(1)}, bf16[96,1,8,128]{3,0,2,1:T(8,128)(2,1)S(1)}, u32[]{:S(2)}, u32[]{:S(2)}) collective-permute-start(bf16[96,1,8,128]{3,0,2,1:T(8,128)(2,1)S(1)} %get-tuple-element.55), channel_id=1, source_target_pairs={{0,4},{4,8},{8,12},{12,16},{16,20},{20,24},{24,28},{1,5},{5,9},{9,... | collective-permute-start | bytes 589832 | tf_op jit(solution)/shard_map/ppermute | solution.py:16
  98.5 3.3 %collective-permute-start.8 = (f32[168,128]{1,0:T(8,128)S(1)}, f32[168,128]{1,0:T(8,128)S(1)}, u32[]{:S(2)}, u32[]{:S(2)}) collective-permute-start(f32[168,128]{1,0:T(8,128)S(1)} %fusion.113), channel_id=1, source_target_pairs={{0,4},{4,0},{8,12},{12,8},{16,20},{20,16},{24,28},{28,24},{1,5},{5... | collective-permute-start | bytes 258056 | tf_op jit(solution)/shard_map/ppermute | solution.py:120
  101.8 6.4 %collective-permute-done.8 = f32[168,128]{1,0:T(8,128)S(1)} collective-permute-done((f32[168,128]{1,0:T(8,128)S(1)}, f32[168,128]{1,0:T(8,128)S(1)}, u32[]{:S(2)}, u32[]{:S(2)}) %collective-permute-start.8) | collective-permute-done | bytes 86048 | tf_op jit(solution)/shard_map/ppermute | solution.py:120
  108.3 3.8 %collective-permute-start.9 = (f32[168,128]{1,0:T(8,128)S(1)}, f32[168,128]{1,0:T(8,128)S(1)}, u32[]{:S(2)}, u32[]{:S(2)}) collective-permute-start(f32[168,128]{1,0:T(8,128)S(1)} %add.241), channel_id=1, source_target_pairs={{0,8},{4,12},{8,0},{12,4},{16,24},{20,28},{24,16},{28,20},{1,9},{5... | collective-permute-start | bytes 258056 | tf_op jit(solution)/shard_map/ppermute | solution.py:120
  112.1 1.6 %fusion.11 = bf16[96,6,8,130]{3,0,2,1:T(8,128)(2,1)S(1)} fusion(bf16[96,1,8,128]{3,0,2,1:T(8,128)(2,1)S(1)} %collective-permute-done.5, bf16[96,4,8,128]{3,0,2,1:T(8,128)(2,1)S(1)} %get-tuple-element.43, bf16[96,1,8,128]{3,0,2,1:T(8,128)(2,1)S(1)} %collective-permute-done.4), kind=kLoop, calls=%fused_computation.59 | loop fusion | flops 7188480 | bytes 2377728 | tf_op jit(solution)/shard_map/concatenate | solution.py:18
  114.8 2.9 %collective-permute-start.10 = (f32[168,128]{1,0:T(8,128)S(1)}, f32[168,128]{1,0:T(8,128)S(1)}, u32[]{:S(2)}, u32[]{:S(2)}) collective-permute-start(f32[168,128]{1,0:T(8,128)S(1)} %add.242), channel_id=1, source_target_pairs={{0,16},{4,20},{8,24},{12,28},{16,0},{20,4},{24,8},{28,12},{1,17},{... | collective-permute-start | bytes 258056 | tf_op jit(solution)/shard_map/ppermute | solution.py:120
  117.7 2.0 %fusion.92 = bf16[1,96,4,8,128]{4,1,3,2,0:T(8,128)(2,1)S(1)} fusion(bf16[96,6,8,130]{3,0,2,1:T(8,128)(2,1)S(1)} %fusion.11, f32[96]{0:T(128)S(1)} %get-tuple-element.76, bf16[96,1,8,128]{3,0,2,1:T(8,128)(2,1)S(1)} %collective-permute-done.5, bf16[96,4,8,128]{3,0,2,1:T(8,128)(2,1)S(1)} %get-tuple-element.43, f32[96]{0:T(128)S(1)} %copy-done.31, ...), kind=kLoop, calls=%fused_computation.180 | loop fusion | flops 11403264 | bytes 6688128 | tf_op jit(solution)/shard_map/broadcast_in_dim | solution.py:181
  (197 shorter events, 36.1 us)
Async XLA Ops:
  0.7 9.5 %copy-start.9 = (bf16[1,96,4,8,128]{4,3,2,1,0:T(8,128)(2,1)S(1)}, bf16[1,96,4,8,128]{4,3,2,1,0:T(8,128)(2,1)}, u32[]{:S(2)}) copy-start(bf16[1,96,4,8,128]{4,3,2,1,0:T(8,128)(2,1)} %param.6) | copy-start | bytes 2359300
  2.2 21.7 %collective-permute-start = (bf16[96,2,8,128]{3,0,2,1:T(8,128)(2,1)S(1)}, bf16[96,2,8,128]{3,0,2,1:T(8,128)(2,1)S(1)}, u32[]{:S(2)}, u32[]{:S(2)}) collective-permute-start(bf16[96,2,8,128]{3,0,2,1:T(8,128)(2,1)S(1)} %get-tuple-element.59), channel_id=1, source_target_pairs={{0,4},{4,8},{8,12},{12,16},{16,20},{20,24},{24,28},{1,5},{5,9},{9,... | collective-permute-start | bytes 1179656 | tf_op jit(solution)/shard_map/ppermute | solution.py:16
  7.1 16.8 %collective-permute-start.1 = (bf16[96,2,8,128]{3,0,2,1:T(8,128)(2,1)S(1)}, bf16[96,2,8,128]{3,0,2,1:T(8,128)(2,1)S(1)}, u32[]{:S(2)}, u32[]{:S(2)}) collective-permute-start(bf16[96,2,8,128]{3,0,2,1:T(8,128)(2,1)S(1)} %get-tuple-element.60), channel_id=1, source_target_pairs={{4,0},{8,4},{12,8},{16,12},{20,16},{24,20},{28,24},{5,1},{9,5},{13... | collective-permute-start | bytes 1179656 | tf_op jit(solution)/shard_map/ppermute | solution.py:17
  9.1 15.6 %copy-start.18 = (f32[96]{0:T(128)}, f32[96]{0:T(128)S(1)}, u32[]{:S(2)}) copy-start(f32[96]{0:T(128)S(1)} %get-tuple-element.77) | copy-start | bytes 1156
  9.1 15.6 %copy-start.20 = (f32[96]{0:T(128)}, f32[96]{0:T(128)S(1)}, u32[]{:S(2)}) copy-start(f32[96]{0:T(128)S(1)} %get-tuple-element.78) | copy-start | bytes 1156
  9.1 15.6 %copy-start.22 = (f32[96]{0:T(128)}, f32[96]{0:T(128)S(1)}, u32[]{:S(2)}) copy-start(f32[96]{0:T(128)S(1)} %get-tuple-element.79) | copy-start | bytes 1156
  11.6 22.3 %copy-start.37 = (f32[96]{0:T(128)}, f32[96]{0:T(128)S(1)}, u32[]{:S(2)}) copy-start(f32[96]{0:T(128)S(1)} %get-tuple-element.67) | copy-start | bytes 1156
  11.7 22.3 %copy-start.39 = (f32[96]{0:T(128)}, f32[96]{0:T(128)S(1)}, u32[]{:S(2)}) copy-start(f32[96]{0:T(128)S(1)} %get-tuple-element.68) | copy-start | bytes 1156
  11.7 22.3 %copy-start.41 = (f32[96]{0:T(128)}, f32[96]{0:T(128)S(1)}, u32[]{:S(2)}) copy-start(f32[96]{0:T(128)S(1)} %get-tuple-element.69) | copy-start | bytes 1156
  11.7 22.3 %copy-start.43 = (f32[96]{0:T(128)}, f32[96]{0:T(128)S(1)}, u32[]{:S(2)}) copy-start(f32[96]{0:T(128)S(1)} %get-tuple-element.70) | copy-start | bytes 1156
  11.7 22.3 %copy-start.45 = (f32[96]{0:T(128)}, f32[96]{0:T(128)S(1)}, u32[]{:S(2)}) copy-start(f32[96]{0:T(128)S(1)} %get-tuple-element.71) | copy-start | bytes 1156
  11.7 22.3 %copy-start.47 = (f32[96]{0:T(128)}, f32[96]{0:T(128)S(1)}, u32[]{:S(2)}) copy-start(f32[96]{0:T(128)S(1)} %get-tuple-element.72) | copy-start | bytes 1156
  11.7 22.3 %copy-start.49 = (f32[96]{0:T(128)}, f32[96]{0:T(128)S(1)}, u32[]{:S(2)}) copy-start(f32[96]{0:T(128)S(1)} %get-tuple-element.73) | copy-start | bytes 1156
  11.7 22.3 %copy-start.51 = (f32[96]{0:T(128)}, f32[96]{0:T(128)S(1)}, u32[]{:S(2)}) copy-start(f32[96]{0:T(128)S(1)} %get-tuple-element.74) | copy-start | bytes 1156
  11.7 22.3 %copy-start.53 = (f32[96]{0:T(128)}, f32[96]{0:T(128)S(1)}, u32[]{:S(2)}) copy-start(f32[96]{0:T(128)S(1)} %get-tuple-element.75) | copy-start | bytes 1156
  56.0 12.2 %collective-permute-start.2 = (bf16[96,1,8,128]{3,2,1,0:T(8,128)(2,1)}, bf16[96,1,8,128]{3,2,1,0:T(8,128)(2,1)}, u32[]{:S(2)}, u32[]{:S(2)}) collective-permute-start(bf16[96,1,8,128]{3,2,1,0:T(8,128)(2,1)} %get-tuple-element.57), channel_id=1, source_target_pairs={{0,4},{4,8},{8,12},{12,16},{16,20},{20,24},{24,28},{1,5},{5,9},{9,... | collective-permute-start | bytes 589832 | tf_op jit(solution)/shard_map/ppermute | solution.py:16
  61.0 8.7 %collective-permute-start.3 = (bf16[96,1,8,128]{3,2,1,0:T(8,128)(2,1)}, bf16[96,1,8,128]{3,2,1,0:T(8,128)(2,1)}, u32[]{:S(2)}, u32[]{:S(2)}) collective-permute-start(bf16[96,1,8,128]{3,2,1,0:T(8,128)(2,1)} %get-tuple-element.58), channel_id=1, source_target_pairs={{4,0},{8,4},{12,8},{16,12},{20,16},{24,20},{28,24},{5,1},{9,5},{13... | collective-permute-start | bytes 589832 | tf_op jit(solution)/shard_map/ppermute | solution.py:17
  89.7 1.3 %collective-permute-start.6 = (f32[168,128]{1,0:T(8,128)S(1)}, f32[168,128]{1,0:T(8,128)S(1)}, u32[]{:S(2)}, u32[]{:S(2)}) collective-permute-start(f32[168,128]{1,0:T(8,128)S(1)} %pad_bitcast_fusion), channel_id=1, source_target_pairs={{0,1},{1,0},{2,3},{3,2},{4,5},{5,4},{6,7},{7,6},{8,9},{9,8},{10,11... | collective-permute-start | bytes 258056 | tf_op jit(solution)/shard_map/ppermute | solution.py:120
  91.1 7.4 %collective-permute-start.7 = (f32[168,128]{1,0:T(8,128)S(1)}, f32[168,128]{1,0:T(8,128)S(1)}, u32[]{:S(2)}, u32[]{:S(2)}) collective-permute-start(f32[168,128]{1,0:T(8,128)S(1)} %fusion.102), channel_id=1, source_target_pairs={{0,2},{1,3},{2,0},{3,1},{4,6},{5,7},{6,4},{7,5},{8,10},{9,11},{10,... | collective-permute-start | bytes 258056 | tf_op jit(solution)/shard_map/ppermute | solution.py:120
  92.6 19.4 %collective-permute-start.4 = (bf16[96,1,8,128]{3,0,2,1:T(8,128)(2,1)S(1)}, bf16[96,1,8,128]{3,0,2,1:T(8,128)(2,1)S(1)}, u32[]{:S(2)}, u32[]{:S(2)}) collective-permute-start(bf16[96,1,8,128]{3,0,2,1:T(8,128)(2,1)S(1)} %get-tuple-element.55), channel_id=1, source_target_pairs={{0,4},{4,8},{8,12},{12,16},{16,20},{20,24},{24,28},{1,5},{5,9},{9,... | collective-permute-start | bytes 589832 | tf_op jit(solution)/shard_map/ppermute | solution.py:16
  97.2 14.9 %collective-permute-start.5 = (bf16[96,1,8,128]{3,0,2,1:T(8,128)(2,1)S(1)}, bf16[96,1,8,128]{3,0,2,1:T(8,128)(2,1)S(1)}, u32[]{:S(2)}, u32[]{:S(2)}) collective-permute-start(bf16[96,1,8,128]{3,0,2,1:T(8,128)(2,1)S(1)} %get-tuple-element.56), channel_id=1, source_target_pairs={{4,0},{8,4},{12,8},{16,12},{20,16},{24,20},{28,24},{5,1},{9,5},{13... | collective-permute-start | bytes 589832 | tf_op jit(solution)/shard_map/ppermute | solution.py:17
  98.5 9.6 %collective-permute-start.8 = (f32[168,128]{1,0:T(8,128)S(1)}, f32[168,128]{1,0:T(8,128)S(1)}, u32[]{:S(2)}, u32[]{:S(2)}) collective-permute-start(f32[168,128]{1,0:T(8,128)S(1)} %fusion.113), channel_id=1, source_target_pairs={{0,4},{4,0},{8,12},{12,8},{16,20},{20,16},{24,28},{28,24},{1,5},{5... | collective-permute-start | bytes 258056 | tf_op jit(solution)/shard_map/ppermute | solution.py:120
  108.3 6.5 %collective-permute-start.9 = (f32[168,128]{1,0:T(8,128)S(1)}, f32[168,128]{1,0:T(8,128)S(1)}, u32[]{:S(2)}, u32[]{:S(2)}) collective-permute-start(f32[168,128]{1,0:T(8,128)S(1)} %add.241), channel_id=1, source_target_pairs={{0,8},{4,12},{8,0},{12,4},{16,24},{20,28},{24,16},{28,20},{1,9},{5... | collective-permute-start | bytes 258056 | tf_op jit(solution)/shard_map/ppermute | solution.py:120
  114.8 6.1 %collective-permute-start.10 = (f32[168,128]{1,0:T(8,128)S(1)}, f32[168,128]{1,0:T(8,128)S(1)}, u32[]{:S(2)}, u32[]{:S(2)}) collective-permute-start(f32[168,128]{1,0:T(8,128)S(1)} %add.242), channel_id=1, source_target_pairs={{0,16},{4,20},{8,24},{12,28},{16,0},{20,4},{24,8},{28,12},{1,17},{... | collective-permute-start | bytes 258056 | tf_op jit(solution)/shard_map/ppermute | solution.py:120
  (45 other events, 175.2 us)

commit v2 on v0

v2 whole, which is shorter than its diff:
```python
import functools
import math

import jax
import jax.numpy as jnp
from jax import lax
from jax.experimental import pallas as pl
from jax.experimental.pallas import tpu as pltpu
from jax.sharding import PartitionSpec as P

GROUP = 16
BF16 = jnp.bfloat16
F32 = jnp.float32


class Planes:
    def __init__(self, sizes, *parts):
        self.channels, self.nz, self.ny = sizes
        self.at = {}
        for ref, indices in parts:
            for spot, index in enumerate(indices):
                self.at[index] = (ref, spot)

    def __contains__(self, index):
        return index in self.at

    def tile(self, index, z, rows):
        ref, spot = self.at[index]
        return ref.at[rows, pl.ds((spot * self.nz + z) * self.ny, self.ny)]

    def span(self, index, start, size):
        ref, spot = self.at[index]
        return ref.at[:, pl.ds(spot * self.nz * self.ny + start, size)]

    def get(self, index, z, rows):
        return self.tile(index, z, rows)[...].astype(F32)

    def put(self, index, z, rows, value):
        self.tile(index, z, rows)[...] = value.astype(BF16)


def over_groups(channels, body):
    def step(group, carry):
        body(pl.ds(pl.multiple_of(group * GROUP, GROUP), GROUP))
        return carry

    lax.fori_loop(0, channels // GROUP, step, 0)


def spread(taps_ref, block, rows, ny, first, count):
    packed = taps_ref[block, rows, :]
    return [jnp.broadcast_to(packed[:, t : t + 1], (GROUP, ny)) for t in range(first, first + count)]


def plane_taps(taps_ref, block, rows, ny, flip):
    taps = spread(taps_ref, block, rows, ny, 0, 9)
    if flip:
        taps = taps[::-1]
    lane = lax.broadcasted_iota(jnp.int32, (GROUP, ny), 1)
    keep = (lane != ny - 1, None, lane != 0)
    return [
        [jnp.where(keep[j], taps[3 * i + j], 0.0) if keep[j] is not None else taps[3 * i + j] for j in range(3)]
        for i in range(3)
    ]


def plane_conv(taps, source, index, z, rows, ny):
    sums = [None, None, None]
    for i in range(3):
        if index + i - 1 in source:
            value = source.get(index + i - 1, z, rows)
            for j in range(3):
                term = taps[i][j] * value
                sums[j] = term if sums[j] is None else sums[j] + term
    return sums[1] + pltpu.roll(sums[0], 1, 1) + pltpu.roll(sums[2], ny - 1, 1)


def depth_conv(taps, values, z):
    total = taps[1] * values[z]
    if z > 0:
        total = total + taps[0] * values[z - 1]
    if z < len(values) - 1:
        total = total + taps[2] * values[z + 1]
    return total


def forward_taps(taps_ref, block, indices, source, planar, axial):
    nz, ny = source.nz, source.ny

    def body(rows):
        taps = plane_taps(taps_ref, block, rows, ny, False)
        depth = spread(taps_ref, block, rows, ny, 9, 3)
        for index in indices:
            values = [plane_conv(taps, source, index, z, rows, ny) for z in range(nz)]
            for z in range(nz):
                planar.put(index, z, rows, values[z])
                axial.put(index, z, rows, depth_conv(depth, values, z))

    over_groups(source.channels, body)


def mixed(mix_ref, block, indices, source, use):
    size = source.nz * source.ny
    step = math.gcd(size, 256)
    weights = mix_ref[block]
    for index in indices:
        for start in range(0, size, step):
            product = jnp.dot(weights, source.span(index, start, step)[...], preferred_element_type=F32)
            use(index, start, step, product)


def gate(preact):
    sigma = 0.5 * jnp.tanh(0.5 * preact) + 0.5
    value = preact * sigma
    return value, sigma + value * (1.0 - sigma)


def hidden_of(mix_ref, indices, axial, hidden, slope, masks):
    def use(index, start, step, preact):
        value, rate = gate(preact)
        if index in masks:
            value, rate = value * masks[index], rate * masks[index]
        hidden.span(index, start, step)[...] = value.astype(BF16)
        slope.span(index, start, step)[...] = rate.astype(BF16)

    mixed(mix_ref, 0, indices, axial, use)


def top_gradient(mix_ref, indices, axial, cotangent, grad_pre):
    def use(index, start, step, preact):
        _, rate = gate(preact)
        grad = cotangent.span(index, start, step)[...].astype(F32) * rate
        grad_pre.span(index, start, step)[...] = grad.astype(BF16)

    mixed(mix_ref, 1, indices, axial, use)


def axial_gradient(mix_t_ref, block, indices, grad_pre, grad_axial):
    def use(index, start, step, product):
        grad_axial.span(index, start, step)[...] = product.astype(BF16)

    mixed(mix_t_ref, block, indices, grad_pre, use)


def planar_gradient(taps_ref, block, indices, grad_axial, grad_planar):
    nz, ny = grad_axial.nz, grad_axial.ny

    def body(rows):
        depth = spread(taps_ref, block, rows, ny, 9, 3)[::-1]
        for index in indices:
            values = [grad_axial.get(index, z, rows) for z in range(nz)]
            for z in range(nz):
                grad_planar.put(index, z, rows, depth_conv(depth, values, z))

    over_groups(grad_axial.channels, body)


def input_gradient(taps_ref, block, indices, grad_planar, target, slope):
    nz, ny = grad_planar.nz, grad_planar.ny

    def body(rows):
        taps = plane_taps(taps_ref, block, rows, ny, True)
        for index in indices:
            for z in range(nz):
                value = plane_conv(taps, grad_planar, index, z, rows, ny)
                if slope is not None:
                    value = value * slope.get(index, z, rows)
                target.put(index, z, rows, value)

    over_groups(grad_planar.channels, body)


def tap_sums(block, indices, grad_planar, source, grad_axial, planar, sums_ref):
    nz, ny = source.nz, source.ny

    def body(rows):
        lane = lax.broadcasted_iota(jnp.int32, (GROUP, ny), 1)
        sums = [None] * 12

        def add(tap, term):
            sums[tap] = term if sums[tap] is None else sums[tap] + term

        for index in indices:
            for z in range(nz):
                grad = grad_planar.get(index, z, rows)
                shifted = (pltpu.roll(grad, ny - 1, 1), grad, pltpu.roll(grad, 1, 1))
                for i in range(3):
                    if index + i - 1 in source:
                        value = source.get(index + i - 1, z, rows)
                        for j in range(3):
                            add(3 * i + j, shifted[j] * value)
                grad = grad_axial.get(index, z, rows)
                for t in range(3):
                    if 0 <= z + t - 1 < nz:
                        add(9 + t, grad * planar.get(index, z + t - 1, rows))
        for i in range(3):
            sums[3 * i] = jnp.where(lane != ny - 1, sums[3 * i], 0.0)
            sums[3 * i + 2] = jnp.where(lane != 0, sums[3 * i + 2], 0.0)
        for t in range(12):
            sums_ref[block, t, rows, :] = sums[t]

    over_groups(source.channels, body)


def mixing_sum(indices, grad_pre, axial):
    size = grad_pre.nz * grad_pre.ny
    total = None
    for index in indices:
        term = lax.dot_general(
            grad_pre.span(index, 0, size)[...],
            axial.span(index, 0, size)[...],
            (((1,), (1,)), ((), ())),
            preferred_element_type=F32,
        )
        total = term if total is None else total + term
    return total


def inner_kernel(sizes, slab, vol, taps, mix, pl1, ax1, sl1, hid):
    inner = range(1, slab - 1)
    planar, axial, slope, hidden = (Planes(sizes, (ref, inner)) for ref in (pl1, ax1, sl1, hid))
    forward_taps(taps, 0, inner, Planes(sizes, (vol, range(slab))), planar, axial)
    hidden_of(mix, inner, axial, hidden, slope, {})


def middle_kernel(
    sizes, slab, vol, lo1, hi1, cot, taps, mix, mix_t, hid_i,
    pl1, ax1, sl1, hid, pl2, ax2, gpre2, gax2, gpl2,
):
    inner, edges = range(1, slab - 1), (0, slab - 1)
    volume = Planes(sizes, (vol, range(slab)), (lo1, (-1,)), (hi1, (slab,)))
    axial = Planes(sizes, (ax1, edges))
    forward_taps(taps, 0, edges, volume, Planes(sizes, (pl1, edges)), axial)
    hidden_of(mix, edges, axial, Planes(sizes, (hid, edges)), Planes(sizes, (sl1, edges)), {})
    hidden = Planes(sizes, (hid_i, inner), (hid, edges))
    cotangent = Planes(sizes, (cot, range(slab)))
    axial, grad_pre = Planes(sizes, (ax2, inner)), Planes(sizes, (gpre2, inner))
    grad_axial = Planes(sizes, (gax2, inner))
    forward_taps(taps, 1, inner, hidden, Planes(sizes, (pl2, inner)), axial)
    top_gradient(mix, inner, axial, cotangent, grad_pre)
    axial_gradient(mix_t, 1, inner, grad_pre, grad_axial)
    planar_gradient(taps, 1, inner, grad_axial, Planes(sizes, (gpl2, inner)))


def edge_kernel(
    sizes, slab, flags, vol, lo1, hi1, lo2, hi2, cot, taps, mix, mix_t, hid_i, hid_e, sl1_e, gpl2_i,
    pl1, ax1, hid, pl2, ax2, gpre2, gax2, gpl2, gpre1, gax1, gpl1, send_lo, send_hi, sl1,
):
    inner, edges, rims = range(1, slab - 1), (0, slab - 1), (-1, slab)
    outer = (-1, 0, slab - 1, slab)
    masks = {-1: flags[0], slab: flags[1]}
    volume = Planes(
        sizes, (vol, range(slab)), (lo1, (-1,)), (hi1, (slab,)), (lo2, (-2,)), (hi2, (slab + 1,))
    )
    axial = Planes(sizes, (ax1, rims))
    forward_taps(taps, 0, rims, volume, Planes(sizes, (pl1, rims)), axial)
    hidden_of(mix, rims, axial, Planes(sizes, (hid, rims)), Planes(sizes, (sl1, rims)), masks)
    hidden = Planes(sizes, (hid_i, inner), (hid_e, edges), (hid, rims))
    cotangent = Planes(sizes, (cot, range(slab)))
    axial, grad_pre = Planes(sizes, (ax2, edges)), Planes(sizes, (gpre2, edges))
    grad_axial = Planes(sizes, (gax2, edges))
    forward_taps(taps, 1, edges, hidden, Planes(sizes, (pl2, edges)), axial)
    top_gradient(mix, edges, axial, cotangent, grad_pre)
    axial_gradient(mix_t, 1, edges, grad_pre, grad_axial)
    planar_gradient(taps, 1, edges, grad_axial, Planes(sizes, (gpl2, edges)))
    grad_planar = Planes(sizes, (gpl2, edges), (gpl2_i, inner))
    slope = Planes(sizes, (sl1_e, edges), (sl1, rims))
    grad_pre, grad_axial = Planes(sizes, (gpre1, outer)), Planes(sizes, (gax1, outer))
    input_gradient(taps, 1, outer, grad_planar, grad_pre, slope)
    axial_gradient(mix_t, 0, outer, grad_pre, grad_axial)
    grad_planar = Planes(sizes, (gpl1, outer))
    planar_gradient(taps, 0, outer, grad_axial, grad_planar)
    low = Planes(sizes, *((gpl1, (-1, 0)),))
    input_gradient(taps, 0, (-2, -1), low, Planes(sizes, (send_lo, (-2, -1))), None)
    high = Planes(sizes)
    for index in (slab - 1, slab):
        high.at[index] = grad_planar.at[index]
    input_gradient(taps, 0, (slab, slab + 1), high, Planes(sizes, (send_hi, (slab, slab + 1))), None)


def weight_kernel(
    sizes, slab, factor, vol, lo1, hi1, lo2, hi2, taps, mix_t,
    pl1_i, ax1_i, sl1_i, hid_i, pl1_e, ax1_e, hid_e, pl2_i, ax2_i, gpre2_i, gax2_i, gpl2_i,
    pl1_r, ax1_r, hid_r, pl2_e, ax2_e, gpre2_e, gax2_e, gpl2_e, gpre1_o, gax1_o, gpl1_o,
    gpl1, payload, gpre1, gax1, sums,
):
    inner, edges, rims = range(1, slab - 1), (0, slab - 1), (-1, slab)
    outer, own, wide = (-1, 0, slab - 1, slab), range(slab), range(-1, slab + 1)
    channels, _, ny = sizes
    grad_planar2 = Planes(sizes, (gpl2_i, inner), (gpl2_e, edges))
    grad_pre1 = Planes(sizes, (gpre1, inner), (gpre1_o, outer))
    grad_axial1 = Planes(sizes, (gax1, inner), (gax1_o, outer))
    grad_planar1 = Planes(sizes, (gpl1, inner), (gpl1_o, outer))
    input_gradient(taps, 1, inner, grad_planar2, grad_pre1, Planes(sizes, (sl1_i, inner)))
    axial_gradient(mix_t, 0, inner, grad_pre1, grad_axial1)
    planar_gradient(taps, 0, inner, grad_axial1, grad_planar1)
    volume = Planes(
        sizes, (vol, own), (lo1, (-1,)), (hi1, (slab,)), (lo2, (-2,)), (hi2, (slab + 1,))
    )
    hidden = Planes(sizes, (hid_i, inner), (hid_e, edges), (hid_r, rims))
    planar1 = Planes(sizes, (pl1_i, inner), (pl1_e, edges), (pl1_r, rims))
    axial1 = Planes(sizes, (ax1_i, inner), (ax1_e, edges), (ax1_r, rims))
    planar2 = Planes(sizes, (pl2_i, inner), (pl2_e, edges))
    axial2 = Planes(sizes, (ax2_i, inner), (ax2_e, edges))
    grad_pre2 = Planes(sizes, (gpre2_i, inner), (gpre2_e, edges))
    grad_axial2 = Planes(sizes, (gax2_i, inner), (gax2_e, edges))
    tap_sums(0, wide, grad_planar1, volume, grad_axial1, planar1, sums)
    tap_sums(1, own, grad_planar2, hidden, grad_axial2, planar2, sums)
    mixing = (mixing_sum(wide, grad_pre1, axial1), mixing_sum(own, grad_pre2, axial2))
    lane = lax.broadcasted_iota(jnp.int32, (channels, payload.shape[2]), 1)
    for block in range(2):
        packed = jnp.zeros(payload.shape[1:], F32)
        for t in range(12):
            total = jnp.sum(sums[block, t], axis=1, keepdims=True)
            packed = packed + jnp.where(lane == channels + t, total, 0.0)
        payload[block] = packed * factor
        payload[block, :, :channels] = mixing[block] * factor


def volume_kernel(sizes, slab, taps, gpl1_i, gpl1_o, out):
    inner, outer = range(1, slab - 1), (-1, 0, slab - 1, slab)
    grad_planar = Planes(sizes, (gpl1_i, inner), (gpl1_o, outer))
    input_gradient(taps, 0, range(slab), grad_planar, Planes(sizes, (out, range(slab))), None)


def call(kernel, name, operands, outputs, scratch=(), flops=0, scalars=0):
    vmem = pl.BlockSpec(memory_space=pltpu.VMEM)
    smem = pl.BlockSpec(memory_space=pltpu.SMEM)
    return pl.pallas_call(
        kernel,
        name=name,
        out_shape=outputs,
        in_specs=[smem] * scalars + [vmem] * (len(operands) - scalars),
        out_specs=[vmem] * len(outputs),
        scratch_shapes=scratch,
        compiler_params=pltpu.CompilerParams(vmem_limit_bytes=32 << 20),
        cost_estimate=pl.CostEstimate(flops=flops, bytes_accessed=1 << 20, transcendentals=0),
    )(*operands)


def all_sum(total):
    for axis in ("dp", "sp"):
        count, step = lax.axis_size(axis), 1
        while step < count:
            mine = total.astype(BF16)
            other = lax.ppermute(mine, axis, [(i, i ^ step) for i in range(count)])
            total = mine.astype(F32) + other.astype(F32)
            step *= 2
    return total


def on_device(volume, cotangent, kernels_xy, kernels_z, mixing):
    _, channels, slab, nz, ny = volume.shape
    plane = nz * ny
    sizes = (channels, nz, ny)
    ranks, place = lax.axis_size("sp"), lax.axis_index("sp")
    up = [(i, i + 1) for i in range(ranks - 1)]
    down = [(j, i) for i, j in up]

    def flat(planes):
        return planes.reshape(channels, -1)

    lo1 = lax.ppermute(flat(volume[0, :, slab - 1]), "sp", up)
    hi1 = lax.ppermute(flat(volume[0, :, 0]), "sp", down)
    lo2 = lax.ppermute(flat(volume[0, :, slab - 2]), "sp", up)
    hi2 = lax.ppermute(flat(volume[0, :, 1]), "sp", down)
    vol, cot = flat(volume[0]), flat(cotangent[0])
    taps = jnp.concatenate(
        [kernels_xy.reshape(2, channels, 9), kernels_z, jnp.zeros((2, channels, 116), BF16)], axis=2
    ).astype(F32)
    mix, mix_t = mixing, jnp.swapaxes(mixing, 1, 2)
    flags = jnp.stack([place > 0, place < ranks - 1]).astype(F32)

    def planes(count):
        return jax.ShapeDtypeStruct((channels, count * plane), BF16)

    def scratch(count):
        return pltpu.VMEM((channels, count * plane), BF16)

    inside = slab - 2
    pl1_i, ax1_i, sl1_i, hid_i = call(
        functools.partial(inner_kernel, sizes, slab), "inner", (vol, taps, mix), [planes(inside)] * 4
    )
    pl1_e, ax1_e, sl1_e, hid_e, pl2_i, ax2_i, gpre2_i, gax2_i, gpl2_i = call(
        functools.partial(middle_kernel, sizes, slab),
        "middle",
        (vol, lo1, hi1, cot, taps, mix, mix_t, hid_i),
        [planes(2)] * 4 + [planes(inside)] * 5,
    )
    pl1_r, ax1_r, hid_r, pl2_e, ax2_e, gpre2_e, gax2_e, gpl2_e, gpre1_o, gax1_o, gpl1_o, send_lo, send_hi = call(
        functools.partial(edge_kernel, sizes, slab),
        "edge",
        (flags, vol, lo1, hi1, lo2, hi2, cot, taps, mix, mix_t, hid_i, hid_e, sl1_e, gpl2_i),
        [planes(2)] * 8 + [planes(4)] * 3 + [planes(2)] * 2,
        scratch=[scratch(2)],
        scalars=1,
    )
    from_lo = lax.ppermute(send_hi, "sp", up)
    from_hi = lax.ppermute(send_lo, "sp", down)
    count = lax.axis_size("dp") * slab * ranks * nz * ny
    gpl1_i, payload = call(
        functools.partial(weight_kernel, sizes, slab, 1.0 / math.sqrt(count)),
        "weights",
        (
            vol, lo1, hi1, lo2, hi2, taps, mix_t,
            pl1_i, ax1_i, sl1_i, hid_i, pl1_e, ax1_e, hid_e, pl2_i, ax2_i, gpre2_i, gax2_i, gpl2_i,
            pl1_r, ax1_r, hid_r, pl2_e, ax2_e, gpre2_e, gax2_e, gpl2_e, gpre1_o, gax1_o, gpl1_o,
        ),
        [planes(inside), jax.ShapeDtypeStruct((2, channels, 128), F32)],
        scratch=[scratch(inside), scratch(inside), pltpu.VMEM((2, 12, channels, ny), F32)],
    )
    total = all_sum(payload)
    (own,) = call(
        functools.partial(volume_kernel, sizes, slab), "volume", (taps, gpl1_i, gpl1_o), [planes(slab)]
    )
    parts = own.astype(F32).reshape(channels, slab, nz, ny)
    from_lo = from_lo.astype(F32).reshape(channels, 2, nz, ny)
    from_hi = from_hi.astype(F32).reshape(channels, 2, nz, ny)
    parts = parts + jnp.pad(from_lo, ((0, 0), (0, slab - 2), (0, 0), (0, 0)))
    parts = parts + jnp.pad(from_hi, ((0, 0), (slab - 2, 0), (0, 0), (0, 0)))
    return (
        parts.astype(BF16)[None],
        total[:, :, :channels],
        total[:, :, channels : channels + 9].reshape(2, channels, 3, 3),
        total[:, :, channels + 9 : channels + 12],
    )


def solution(mesh):
    return jax.shard_map(
        on_device,
        mesh=mesh,
        in_specs=(P("dp", None, "sp", None, None), P("dp", None, "sp", None, None), P(), P(), P()),
        out_specs=(P("dp", None, "sp", None, None), P(), P(), P()),
        check_vma=False,
    )
```

time: 221 us -> 78.5 us (0.36)
  waiting for transfers between devices: 139 us -> 17.1 us
  other arithmetic: 33.4 us -> 1.51 us
  Pallas kernels: 0 us -> 25.5 us
  between operations: 14.4 us -> 0.96 us
  starting transfers between devices: 17.9 us -> 25.5 us
  matrix products: 4.28 us -> 0 us
  local copies, waits for them, and re-layouts: 11.5 us -> 7.56 us
    psum x1 -> x0, waiting for transfers between devices: 120 us -> none  [settle_all(): lax.psum((lower[0], lower[1], lower[2], upper[0], upper[1], upper[2]), ('...]
    pallas_call x0 -> x5, Pallas kernels: none -> 25.5 us  [call(): pl.pallas_call(kernel, name=name, out_shape=outputs, in_specs=[smem] * sc...]
    reduce_sum x3 -> x0, other arithmetic: 10.8 us -> none  [the longest x2 7.96 us: backward_block(): jnp.sum(grad_axial * planar_pad[:, :, depth_tap:depth_tap + depth_len, :]...]
    ppermute x6 -> x11, starting transfers between devices: 17.9 us -> 25.5 us  [the longest x5 8.7 us: all_sum(): other = lax.ppermute(mine, axis, [(i, i ^ step) for i in range(count)])]
    add x2 -> x1, other arithmetic: 6.08 us -> 0.01 us  [all_sum(): total = mine.astype(F32) + other.astype(F32)]
    convert_element_type x4 -> x7, other arithmetic: 5.25 us -> 0.24 us  [the longest x1 0.09 us: on_device(): taps = jnp.concatenate([kernels_xy.reshape(2, channels, 9), kernels_z, jn...]
    unnamed x28 -> x22, local copies, waits for them, and re-layouts: 8.82 us -> 4.48 us
    dot_general x6 -> x0, matrix products: 4.28 us -> none  [the longest x2 2.2 us: backward_block(): lax.dot_general(own_pre, own_axial, (((1,), (1,)), ((), ())), preferred_e...]
  transfers between devices with their start and end apart: 7 -> 11, of which waited for: 3 -> 5; matrix products, arithmetic and copies ran while one was open for 4% -> 8% of each run, Pallas kernels for 0% -> 10%
where the time goes in v2:
time: 78.5 us; the launch traced here: 78.2 us
  starting transfers between devices  25.5 us (32%)
  Pallas kernels  25.5 us (32%)
  waiting for transfers between devices  17.1 us (22%)
  local copies, waits for them, and re-layouts  7.56 us (10%)
  other arithmetic  1.51 us (2%)
  between operations  0.96 us (1%)
    pallas_call x5, Pallas kernels, call(): pl.pallas_call(kernel, name=name, out_shape=outputs, in_specs=[smem] * sc...  25.5 us
    ppermute x5, waiting for transfers between devices, all_sum(): other = lax.ppermute(mine, axis, [(i, i ^ step) for i in range(count)])  13.8 us
    ppermute x5, starting transfers between devices, all_sum(): other = lax.ppermute(mine, axis, [(i, i ^ step) for i in range(count)])  8.7 us
    ppermute x1, starting transfers between devices, on_device(): lo2 = lax.ppermute(flat(volume[0, :, slab - 2]), 'sp', up)  4.88 us
    ppermute x1, starting transfers between devices, on_device(): from_lo = lax.ppermute(send_hi, 'sp', up)  4.68 us
    unnamed x22, local copies, waits for them, and re-layouts  4.48 us
    ppermute x1, starting transfers between devices, on_device(): lo1 = lax.ppermute(flat(volume[0, :, slab - 1]), 'sp', up)  3.42 us
    ppermute x1, waiting for transfers between devices, on_device(): hi1 = lax.ppermute(flat(volume[0, :, 0]), 'sp', down)  3.32 us
  transfers between devices with their start and end apart: 11, of which 5 were waited for; matrix products, arithmetic and copies ran while one was open for 8% of the time, Pallas kernels for 10%

profile of v2, /device:TPU:0, one launch (start us, length us, event | category | flops | bytes accessed | tf_op | source)
XLA Modules:
  0.0 78.2 jit_solution(984961326862002974)
XLA Ops:
  0.7 1.4 %fusion.1 = (bf16[1,96,1,8,128]{4,3,2,1,0:T(8,128)(2,1)S(1)}, bf16[1,96,1,8,128]{4,3,2,1,0:T(8,128)(2,1)S(1)}, bf16[1,96,1,8,128]{4,3,2,1,0:T(8,128)(2,1)S(1)}, bf16[1,96,1,8,128]{4,3,2,1,0:T(8,128)(2,1)S(1)}) fusion(bf16[1,96,4,8,128]{4,3,2,1,0:T(8,128)(2,1)} %param.5), kind=kLoop, calls=%fused_computation.14 | loop fusion | bytes 1572864 | tf_op jit(solution)/shard_map/slice | solution.py:366
  2.1 4.9 %collective-permute-start.2 = (bf16[96,1024]{1,0:T(8,128)(2,1)S(1)}, bf16[96,1024]{1,0:T(8,128)(2,1)S(1)}, u32[]{:S(2)}, u32[]{:S(2)}) collective-permute-start(bf16[96,1024]{1,0:T(8,128)(2,1)S(1)} %bitcast.54), channel_id=1, source_target_pairs={{0,4},{4,8},{8,12},{12,16},{16,20},{20,24},{24,28},{1,5},{5,9},{9,... | collective-permute-start | bytes 589832 | tf_op jit(solution)/shard_map/ppermute | solution.py:365
  7.0 0.7 copy.33
  7.7 3.4 %collective-permute-start = (bf16[96,1024]{1,0:T(8,128)(2,1)}, bf16[96,1024]{1,0:T(8,128)(2,1)S(1)}, u32[]{:S(2)}, u32[]{:S(2)}) collective-permute-start(bf16[96,1024]{1,0:T(8,128)(2,1)} %bitcast.40), channel_id=1, source_target_pairs={{0,4},{4,8},{8,12},{12,16},{16,20},{20,24},{24,28},{1,5},{5,9},{9,... | collective-permute-start | bytes 589832 | tf_op jit(solution)/shard_map/ppermute | solution.py:363
  11.8 1.3 %collective-permute-start.1 = (bf16[96,1024]{1,0:T(8,128)(2,1)}, bf16[96,1024]{1,0:T(8,128)(2,1)S(1)}, u32[]{:S(2)}, u32[]{:S(2)}) collective-permute-start(bf16[96,1024]{1,0:T(8,128)(2,1)} %bitcast.39), channel_id=1, source_target_pairs={{4,0},{8,4},{12,8},{16,12},{20,16},{24,20},{28,24},{5,1},{9,5},{13... | collective-permute-start | bytes 589832 | tf_op jit(solution)/shard_map/ppermute | solution.py:364
  13.8 1.3 %collective-permute-start.3 = (bf16[96,1024]{1,0:T(8,128)(2,1)}, bf16[96,1024]{1,0:T(8,128)(2,1)S(1)}, u32[]{:S(2)}, u32[]{:S(2)}) collective-permute-start(bf16[96,1024]{1,0:T(8,128)(2,1)} %bitcast.37), channel_id=1, source_target_pairs={{4,0},{8,4},{12,8},{16,12},{20,16},{24,20},{28,24},{5,1},{9,5},{13... | collective-permute-start | bytes 589832 | tf_op jit(solution)/shard_map/ppermute | solution.py:366
  16.4 1.8 %inner.1 = (bf16[96,2048]{1,0:T(8,128)(2,1)S(1)}, bf16[96,2048]{1,0:T(8,128)(2,1)S(1)}, bf16[96,2048]{1,0:T(8,128)(2,1)S(1)}, bf16[96,2048]{1,0:T(8,128)(2,1)S(1)}) custom-call(bf16[96,4096]{1,0:T(8,128)(2,1)S(1)} %reshape_squeeze.18.vol, f32[2,96,128]{2,1,0:T(8,128)S(1)} %maximum_convert_fusion.taps, bf16[2,96,96]{2,1,0:T(8,128)(2,1)S(1)} %copy-done), custom_call_target="tpu_custom_call" | custom-call | bytes 1048576 | tf_op jit(solution)/shard_map/inner/pallas_call | solution.py:329
  18.3 3.3 %collective-permute-done.1.hi1 = bf16[96,1024]{1,0:T(8,128)(2,1)S(1)} collective-permute-done((bf16[96,1024]{1,0:T(8,128)(2,1)}, bf16[96,1024]{1,0:T(8,128)(2,1)S(1)}, u32[]{:S(2)}, u32[]{:S(2)}) %collective-permute-start.1) | collective-permute-done | bytes 196640 | tf_op jit(solution)/shard_map/ppermute | solution.py:364
  21.6 4.4 %middle.1 = (bf16[96,2048]{1,0:T(8,128)(2,1)S(1)}, bf16[96,2048]{1,0:T(8,128)(2,1)S(1)}, bf16[96,2048]{1,0:T(8,128)(2,1)S(1)}, bf16[96,2048]{1,0:T(8,128)(2,1)S(...) custom-call(bf16[96,4096]{1,0:T(8,128)(2,1)S(1)} %reshape_squeeze.18, ...), custom_call_target="tpu_custom_call" | custom-call | bytes 1048576 | tf_op jit(solution)/shard_map/middle/pallas_call | solution.py:329
  26.0 10.5 %edge.1 = (bf16[96,2048]{1,0:T(8,128)(2,1)S(1)}, bf16[96,2048]{1,0:T(8,128)(2,1)S(1)}, bf16[96,2048]{1,0:T(8,128)(2,1)S(1)}, bf16[96,2048]{1,0:T(8,128)(2,1)S(1)...) custom-call(f32[2]{0:T(128)S(1)} %add_convert_fusion.5.flags, ...), custom_call_target="tpu_custom_call" | custom-call | bytes 1048576 | tf_op jit(solution)/shard_map/edge/pallas_call | solution.py:329
  36.5 7.1 %weights.1 = (bf16[96,2048]{1,0:T(8,128)(2,1)S(1)}, f32[2,96,128]{2,1,0:T(8,128)S(1)}) custom-call(bf16[96,4096]{1,0:T(8,128)(2,1)S(1)} %reshape_squeeze.18.vol, bf16[96,1024]{1,0:T(8,128)(2,1)S(1)} %collective-permute-done.lo1, bf16[96,1024]{1,0:T(8,128)(2,1)S(1)} %collective-permute-done.1.hi1, bf16[96,1024]{1,0:T(8,128)(2,1)S(1)} %collective-permute-done.2.lo2, ...), custom_call_target="tpu_custom_call" | custom-call | bytes 1048576 | tf_op jit(solution)/shard_map/weights/pallas_call | solution.py:329
  43.6 1.2 %collective-permute-done.6 = bf16[2,96,128]{2,1,0:T(8,128)(2,1)S(1)} collective-permute-done((bf16[2,96,128]{2,1,0:T(8,128)(2,1)S(1)}, bf16[2,96,128]{2,1,0:T(8,128)(2,1)S(1)}, u32[]{:S(2)}, u32[]{:S(2)}) %collective-permute-start.6) | collective-permute-done | bytes 49184 | tf_op jit(solution)/shard_map/ppermute | solution.py:346
  44.9 1.6 %collective-permute-start.7 = (bf16[2,96,128]{2,1,0:T(8,128)(2,1)S(1)}, bf16[2,96,128]{2,1,0:T(8,128)(2,1)S(1)}, u32[]{:S(2)}, u32[]{:S(2)}) collective-permute-start(bf16[2,96,128]{2,1,0:T(8,128)(2,1)S(1)} %add_convert_fusion.4), channel_id=1, source_target_pairs={{0,2},{1,3},{2,0},{3,1},{4,6},{5,7},{6,4},{7,5},{8,10},{9,11},{10,... | collective-permute-start | bytes 147464 | tf_op jit(solution)/shard_map/ppermute | solution.py:346
  46.4 2.6 %collective-permute-done.7 = bf16[2,96,128]{2,1,0:T(8,128)(2,1)S(1)} collective-permute-done((bf16[2,96,128]{2,1,0:T(8,128)(2,1)S(1)}, bf16[2,96,128]{2,1,0:T(8,128)(2,1)S(1)}, u32[]{:S(2)}, u32[]{:S(2)}) %collective-permute-start.7) | collective-permute-done | bytes 49184 | tf_op jit(solution)/shard_map/ppermute | solution.py:346
  49.1 2.2 %collective-permute-start.8 = (bf16[2,96,128]{2,1,0:T(8,128)(2,1)S(1)}, bf16[2,96,128]{2,1,0:T(8,128)(2,1)S(1)}, u32[]{:S(2)}, u32[]{:S(2)}) collective-permute-start(bf16[2,96,128]{2,1,0:T(8,128)(2,1)S(1)} %add_convert_fusion.3), channel_id=1, source_target_pairs={{0,4},{4,0},{8,12},{12,8},{16,20},{20,16},{24,28},{28,24},{1,5},{5... | collective-permute-start | bytes 147464 | tf_op jit(solution)/shard_map/ppermute | solution.py:346
  51.3 2.1 %collective-permute-done.8 = bf16[2,96,128]{2,1,0:T(8,128)(2,1)S(1)} collective-permute-done((bf16[2,96,128]{2,1,0:T(8,128)(2,1)S(1)}, bf16[2,96,128]{2,1,0:T(8,128)(2,1)S(1)}, u32[]{:S(2)}, u32[]{:S(2)}) %collective-permute-start.8) | collective-permute-done | bytes 49184 | tf_op jit(solution)/shard_map/ppermute | solution.py:346
  53.4 1.7 %collective-permute-start.9 = (bf16[2,96,128]{2,1,0:T(8,128)(2,1)S(1)}, bf16[2,96,128]{2,1,0:T(8,128)(2,1)S(1)}, u32[]{:S(2)}, u32[]{:S(2)}) collective-permute-start(bf16[2,96,128]{2,1,0:T(8,128)(2,1)S(1)} %add_convert_fusion.2), channel_id=1, source_target_pairs={{0,8},{4,12},{8,0},{12,4},{16,24},{20,28},{24,16},{28,20},{1,9},{5... | collective-permute-start | bytes 147464 | tf_op jit(solution)/shard_map/ppermute | solution.py:346
  55.0 1.8 %volume.1 = bf16[96,4096]{1,0:T(8,128)(2,1)S(1)} custom-call(f32[2,96,128]{2,1,0:T(8,128)S(1)} %maximum_convert_fusion.taps, bf16[96,2048]{1,0:T(8,128)(2,1)S(1)} %get-tuple-element.56.gpl1_i, bf16[96,4096]{1,0:T(8,128)(2,1)S(1)} %get-tuple-element.55.gpl1_o), custom_call_target="tpu_custom_call" | custom-call | bytes 1048576 | tf_op jit(solution)/shard_map/volume/pallas_call | solution.py:329
  56.8 4.7 %collective-permute-start.4 = (bf16[96,2048]{1,0:T(8,128)(2,1)S(1)}, bf16[96,2048]{1,0:T(8,128)(2,1)}, u32[]{:S(2)}, u32[]{:S(2)}) collective-permute-start(bf16[96,2048]{1,0:T(8,128)(2,1)S(1)} %get-tuple-element.57), channel_id=1, source_target_pairs={{0,4},{4,8},{8,12},{12,16},{16,20},{20,24},{24,28},{1,5},{5,9},{9,... | collective-permute-start | bytes 1179656 | tf_op jit(solution)/shard_map/ppermute | solution.py:398
  61.5 1.3 %collective-permute-start.5 = (bf16[96,2048]{1,0:T(8,128)(2,1)S(1)}, bf16[96,2048]{1,0:T(8,128)(2,1)S(1)}, u32[]{:S(2)}, u32[]{:S(2)}) collective-permute-start(bf16[96,2048]{1,0:T(8,128)(2,1)S(1)} %get-tuple-element.58), channel_id=1, source_target_pairs={{4,0},{8,4},{12,8},{16,12},{20,16},{24,20},{28,24},{5,1},{9,5},{13... | collective-permute-start | bytes 1179656 | tf_op jit(solution)/shard_map/ppermute | solution.py:399
  62.8 3.2 %collective-permute-start.10 = (bf16[2,96,128]{2,1,0:T(8,128)(2,1)S(1)}, bf16[2,96,128]{2,1,0:T(8,128)(2,1)S(1)}, u32[]{:S(2)}, u32[]{:S(2)}) collective-permute-start(bf16[2,96,128]{2,1,0:T(8,128)(2,1)S(1)} %add_convert_fusion.1), channel_id=1, source_target_pairs={{0,16},{4,20},{8,24},{12,28},{16,0},{20,4},{24,8},{28,12},{1,17},{... | collective-permute-start | bytes 147464 | tf_op jit(solution)/shard_map/ppermute | solution.py:346
  66.5 7.9 %collective-permute-done.10 = bf16[2,96,128]{2,1,0:T(8,128)(2,1)S(1)} collective-permute-done((bf16[2,96,128]{2,1,0:T(8,128)(2,1)S(1)}, bf16[2,96,128]{2,1,0:T(8,128)(2,1)S(1)}, u32[]{:S(2)}, u32[]{:S(2)}) %collective-permute-start.10) | collective-permute-done | bytes 49184 | tf_op jit(solution)/shard_map/ppermute | solution.py:346
  75.9 1.1 %copy.24 = bf16[12,8,16,128]{3,2,1,0:T(8,128)(2,1)S(1)} copy(bf16[12,8,16,128]{3,1,2,0:T(8,128)(2,1)} %bitcast.23) | data formatting | bytes 786432
  77.1 1.1 %fusion = bf16[1,96,4,8,128]{4,3,2,1,0:T(8,128)(2,1)} fusion(f32[96,4,8,128]{3,2,1,0:T(8,128)S(1)} %bitcast.45, bf16[96,2,8,128]{3,2,1,0:T(8,128)(2,1)S(1)} %bitcast.47, bf16[96,2,8,128]{3,2,1,0:T(8,128)(2,1)S(1)} %bitcast.46), kind=kLoop, calls=%fused_computation.2 | loop fusion | flops 1966080 | bytes 3145728 | tf_op jit(solution)/shard_map/broadcast_in_dim | solution.py:422
  (44 shorter events, 4.9 us)
Async XLA Ops:
  0.6 14.9 %copy-start.1 = (bf16[1,96,4,8,128]{4,3,2,1,0:T(8,128)(2,1)S(1)}, bf16[1,96,4,8,128]{4,3,2,1,0:T(8,128)(2,1)}, u32[]{:S(2)}) copy-start(bf16[1,96,4,8,128]{4,3,2,1,0:T(8,128)(2,1)} %param.5) | copy-start | bytes 2359300
  0.6 14.4 %copy-start.4 = (bf16[2,96,3,3]{1,0,3,2:T(2,128)(2,1)S(1)}, bf16[2,96,3,3]{1,0,3,2:T(2,128)(2,1)}, u32[]{:S(2)}) copy-start(bf16[2,96,3,3]{1,0,3,2:T(2,128)(2,1)} %param.7) | copy-start | bytes 10372
  0.7 14.6 %copy-start.5 = (bf16[2,96,3]{1,0,2:T(2,128)(2,1)S(1)}, bf16[2,96,3]{1,0,2:T(2,128)(2,1)}, u32[]{:S(2)}) copy-start(bf16[2,96,3]{1,0,2:T(2,128)(2,1)} %param.8) | copy-start | bytes 3460
  2.1 13.8 %copy-start = (bf16[2,96,96]{2,1,0:T(8,128)(2,1)S(1)}, bf16[2,96,96]{2,1,0:T(8,128)(2,1)}, u32[]{:S(2)}) copy-start(bf16[2,96,96]{2,1,0:T(8,128)(2,1)} %mix.5) | copy-start | bytes 110596
  2.1 23.9 %collective-permute-start.2 = (bf16[96,1024]{1,0:T(8,128)(2,1)S(1)}, bf16[96,1024]{1,0:T(8,128)(2,1)S(1)}, u32[]{:S(2)}, u32[]{:S(2)}) collective-permute-start(bf16[96,1024]{1,0:T(8,128)(2,1)S(1)} %bitcast.54), channel_id=1, source_target_pairs={{0,4},{4,8},{8,12},{12,16},{16,20},{20,24},{24,28},{1,5},{5,9},{9,... | collective-permute-start | bytes 589832 | tf_op jit(solution)/shard_map/ppermute | solution.py:365
  7.0 9.1 %copy-start.3 = (bf16[1,96,4,8,128]{4,3,2,1,0:T(8,128)(2,1)S(1)}, bf16[1,96,4,8,128]{4,3,2,1,0:T(8,128)(2,1)}, u32[]{:S(2)}) copy-start(bf16[1,96,4,8,128]{4,3,2,1,0:T(8,128)(2,1)} %param.6) | copy-start | bytes 2359300
  7.7 10.6 %collective-permute-start = (bf16[96,1024]{1,0:T(8,128)(2,1)}, bf16[96,1024]{1,0:T(8,128)(2,1)S(1)}, u32[]{:S(2)}, u32[]{:S(2)}) collective-permute-start(bf16[96,1024]{1,0:T(8,128)(2,1)} %bitcast.40), channel_id=1, source_target_pairs={{0,4},{4,8},{8,12},{12,16},{16,20},{20,24},{24,28},{1,5},{5,9},{9,... | collective-permute-start | bytes 589832 | tf_op jit(solution)/shard_map/ppermute | solution.py:363
  11.8 9.8 %collective-permute-start.1 = (bf16[96,1024]{1,0:T(8,128)(2,1)}, bf16[96,1024]{1,0:T(8,128)(2,1)S(1)}, u32[]{:S(2)}, u32[]{:S(2)}) collective-permute-start(bf16[96,1024]{1,0:T(8,128)(2,1)} %bitcast.39), channel_id=1, source_target_pairs={{4,0},{8,4},{12,8},{16,12},{20,16},{24,20},{28,24},{5,1},{9,5},{13... | collective-permute-start | bytes 589832 | tf_op jit(solution)/shard_map/ppermute | solution.py:364
  13.8 12.2 %collective-permute-start.3 = (bf16[96,1024]{1,0:T(8,128)(2,1)}, bf16[96,1024]{1,0:T(8,128)(2,1)S(1)}, u32[]{:S(2)}, u32[]{:S(2)}) collective-permute-start(bf16[96,1024]{1,0:T(8,128)(2,1)} %bitcast.37), channel_id=1, source_target_pairs={{4,0},{8,4},{12,8},{16,12},{20,16},{24,20},{28,24},{5,1},{9,5},{13... | collective-permute-start | bytes 589832 | tf_op jit(solution)/shard_map/ppermute | solution.py:366
  43.6 1.3 %collective-permute-start.6 = (bf16[2,96,128]{2,1,0:T(8,128)(2,1)S(1)}, bf16[2,96,128]{2,1,0:T(8,128)(2,1)S(1)}, u32[]{:S(2)}, u32[]{:S(2)}) collective-permute-start(bf16[2,96,128]{2,1,0:T(8,128)(2,1)S(1)} %convert_element_type.64), channel_id=1, source_target_pairs={{0,1},{1,0},{2,3},{3,2},{4,5},{5,4},{6,7},{7,6},{8,9},{9,8},{10,11... | collective-permute-start | bytes 147464 | tf_op jit(solution)/shard_map/ppermute | solution.py:346
  44.9 4.2 %collective-permute-start.7 = (bf16[2,96,128]{2,1,0:T(8,128)(2,1)S(1)}, bf16[2,96,128]{2,1,0:T(8,128)(2,1)S(1)}, u32[]{:S(2)}, u32[]{:S(2)}) collective-permute-start(bf16[2,96,128]{2,1,0:T(8,128)(2,1)S(1)} %add_convert_fusion.4), channel_id=1, source_target_pairs={{0,2},{1,3},{2,0},{3,1},{4,6},{5,7},{6,4},{7,5},{8,10},{9,11},{10,... | collective-permute-start | bytes 147464 | tf_op jit(solution)/shard_map/ppermute | solution.py:346
  49.1 4.3 %collective-permute-start.8 = (bf16[2,96,128]{2,1,0:T(8,128)(2,1)S(1)}, bf16[2,96,128]{2,1,0:T(8,128)(2,1)S(1)}, u32[]{:S(2)}, u32[]{:S(2)}) collective-permute-start(bf16[2,96,128]{2,1,0:T(8,128)(2,1)S(1)} %add_convert_fusion.3), channel_id=1, source_target_pairs={{0,4},{4,0},{8,12},{12,8},{16,20},{20,16},{24,28},{28,24},{1,5},{5... | collective-permute-start | bytes 147464 | tf_op jit(solution)/shard_map/ppermute | solution.py:346
  53.4 9.4 %collective-permute-start.9 = (bf16[2,96,128]{2,1,0:T(8,128)(2,1)S(1)}, bf16[2,96,128]{2,1,0:T(8,128)(2,1)S(1)}, u32[]{:S(2)}, u32[]{:S(2)}) collective-permute-start(bf16[2,96,128]{2,1,0:T(8,128)(2,1)S(1)} %add_convert_fusion.2), channel_id=1, source_target_pairs={{0,8},{4,12},{8,0},{12,4},{16,24},{20,28},{24,16},{28,20},{1,9},{5... | collective-permute-start | bytes 147464 | tf_op jit(solution)/shard_map/ppermute | solution.py:346
  56.8 19.1 %collective-permute-start.4 = (bf16[96,2048]{1,0:T(8,128)(2,1)S(1)}, bf16[96,2048]{1,0:T(8,128)(2,1)}, u32[]{:S(2)}, u32[]{:S(2)}) collective-permute-start(bf16[96,2048]{1,0:T(8,128)(2,1)S(1)} %get-tuple-element.57), channel_id=1, source_target_pairs={{0,4},{4,8},{8,12},{12,16},{16,20},{20,24},{24,28},{1,5},{5,9},{9,... | collective-permute-start | bytes 1179656 | tf_op jit(solution)/shard_map/ppermute | solution.py:398
  61.5 15.5 %collective-permute-start.5 = (bf16[96,2048]{1,0:T(8,128)(2,1)S(1)}, bf16[96,2048]{1,0:T(8,128)(2,1)S(1)}, u32[]{:S(2)}, u32[]{:S(2)}) collective-permute-start(bf16[96,2048]{1,0:T(8,128)(2,1)S(1)} %get-tuple-element.58), channel_id=1, source_target_pairs={{4,0},{8,4},{12,8},{16,12},{20,16},{24,20},{28,24},{5,1},{9,5},{13... | collective-permute-start | bytes 1179656 | tf_op jit(solution)/shard_map/ppermute | solution.py:399
  62.8 11.5 %collective-permute-start.10 = (bf16[2,96,128]{2,1,0:T(8,128)(2,1)S(1)}, bf16[2,96,128]{2,1,0:T(8,128)(2,1)S(1)}, u32[]{:S(2)}, u32[]{:S(2)}) collective-permute-start(bf16[2,96,128]{2,1,0:T(8,128)(2,1)S(1)} %add_convert_fusion.1), channel_id=1, source_target_pairs={{0,16},{4,20},{8,24},{12,28},{16,0},{20,4},{24,8},{28,12},{1,17},{... | collective-permute-start | bytes 147464 | tf_op jit(solution)/shard_map/ppermute | solution.py:346
  74.4 3.8 %copy-start.2 = (f32[2,96,128]{2,1,0:T(8,128)}, f32[2,96,128]{2,1,0:T(8,128)S(1)}, u32[]{:S(2)}) copy-start(f32[2,96,128]{2,1,0:T(8,128)S(1)} %convert_add_fusion) | copy-start | bytes 294916

commit v3 on v2

--- a/solution.py
+++ b/solution.py
@@ -44,24 +44,28 @@
         body(pl.ds(pl.multiple_of(group * GROUP, GROUP), GROUP))
         return carry
 
-    lax.fori_loop(0, channels // GROUP, step, 0)
-
-
-def spread(taps_ref, block, rows, ny, first, count):
-    packed = taps_ref[block, rows, :]
-    return [jnp.broadcast_to(packed[:, t : t + 1], (GROUP, ny)) for t in range(first, first + count)]
-
-
-def plane_taps(taps_ref, block, rows, ny, flip):
-    taps = spread(taps_ref, block, rows, ny, 0, 9)
-    if flip:
-        taps = taps[::-1]
-    lane = lax.broadcasted_iota(jnp.int32, (GROUP, ny), 1)
-    keep = (lane != ny - 1, None, lane != 0)
-    return [
-        [jnp.where(keep[j], taps[3 * i + j], 0.0) if keep[j] is not None else taps[3 * i + j] for j in range(3)]
-        for i in range(3)
-    ]
+    lax.fori_loop(0, channels // GROUP, step, 0, unroll=3)
+
+
+def spread(taps_ref, block, rows, first, count):
+    return [taps_ref[block, t, rows, :].astype(F32) for t in range(first, first + count)]
+
+
+def plane_taps(taps_ref, block, rows, flip):
+    taps = spread(taps_ref, block, rows, 9 if flip else 0, 9)
+    return [taps[3 * i : 3 * i + 3] for i in range(3)]
+
+
+def wide_taps(kernels_xy, kernels_z, ny):
+    channels = kernels_xy.shape[1]
+    lane = lax.broadcasted_iota(jnp.int32, (1, 1, 3, 1, ny), 4)
+    column = lax.broadcasted_iota(jnp.int32, (1, 1, 3, 1, ny), 2)
+    keep = ((column != 0) | (lane != ny - 1)) & ((column != 2) | (lane != 0))
+    planes = jnp.moveaxis(kernels_xy, 1, 3)
+    planes = jnp.concatenate([planes, planes[:, ::-1, ::-1]], axis=1)[..., None]
+    planes = jnp.where(keep, planes, jnp.zeros((), planes.dtype)).reshape(2, 18, channels, ny)
+    depth = jnp.broadcast_to(jnp.moveaxis(kernels_z, 1, 2)[..., None], (2, 3, channels, ny))
+    return jnp.concatenate([planes, depth], axis=1)
 
 
 def plane_conv(taps, source, index, z, rows, ny):
@@ -88,8 +92,8 @@
     nz, ny = source.nz, source.ny
 
     def body(rows):
-        taps = plane_taps(taps_ref, block, rows, ny, False)
-        depth = spread(taps_ref, block, rows, ny, 9, 3)
+        taps = plane_taps(taps_ref, block, rows, False)
+        depth = spread(taps_ref, block, rows, 18, 3)
         for index in indices:
             values = [plane_conv(taps, source, index, z, rows, ny) for z in range(nz)]
             for z in range(nz):
@@ -143,10 +147,10 @@
 
 
 def planar_gradient(taps_ref, block, indices, grad_axial, grad_planar):
-    nz, ny = grad_axial.nz, grad_axial.ny
+    nz = grad_axial.nz
 
     def body(rows):
-        depth = spread(taps_ref, block, rows, ny, 9, 3)[::-1]
+        depth = spread(taps_ref, block, rows, 18, 3)[::-1]
         for index in indices:
             values = [grad_axial.get(index, z, rows) for z in range(nz)]
             for z in range(nz):
@@ -159,7 +163,7 @@
     nz, ny = grad_planar.nz, grad_planar.ny
 
     def body(rows):
-        taps = plane_taps(taps_ref, block, rows, ny, True)
+        taps = plane_taps(taps_ref, block, rows, True)
         for index in indices:
             for z in range(nz):
                 value = plane_conv(taps, grad_planar, index, z, rows, ny)
@@ -270,12 +274,10 @@
     axial_gradient(mix_t, 0, outer, grad_pre, grad_axial)
     grad_planar = Planes(sizes, (gpl1, outer))
     planar_gradient(taps, 0, outer, grad_axial, grad_planar)
-    low = Planes(sizes, *((gpl1, (-1, 0)),))
-    input_gradient(taps, 0, (-2, -1), low, Planes(sizes, (send_lo, (-2, -1))), None)
-    high = Planes(sizes)
-    for index in (slab - 1, slab):
-        high.at[index] = grad_planar.at[index]
-    input_gradient(taps, 0, (slab, slab + 1), high, Planes(sizes, (send_hi, (slab, slab + 1))), None)
+    sent = (-2, -1, slab, slab + 1)
+    input_gradient(
+        taps, 0, sent, grad_planar, Planes(sizes, (send_lo, sent[:2]), (send_hi, sent[2:])), None
+    )
 
 
 def weight_kernel(
@@ -365,9 +367,7 @@
     lo2 = lax.ppermute(flat(volume[0, :, slab - 2]), "sp", up)
     hi2 = lax.ppermute(flat(volume[0, :, 1]), "sp", down)
     vol, cot = flat(volume[0]), flat(cotangent[0])
-    taps = jnp.concatenate(
-        [kernels_xy.reshape(2, channels, 9), kernels_z, jnp.zeros((2, channels, 116), BF16)], axis=2
-    ).astype(F32)
+    taps = wide_taps(kernels_xy, kernels_z, ny)
     mix, mix_t = mixing, jnp.swapaxes(mixing, 1, 2)
     flags = jnp.stack([place > 0, place < ranks - 1]).astype(F32)
 

time: 78.5 us -> 72 us (0.917)
  Pallas kernels: 25.5 us -> 16.9 us
  starting transfers between devices: 25.5 us -> 27 us
    pallas_call x5, Pallas kernels: 25.5 us -> 16.9 us  [call(): pl.pallas_call(kernel, name=name, out_shape=outputs, in_specs=[smem] * sc...]
    ppermute x5, starting transfers between devices: 8.7 us -> 11.1 us  [all_sum(): other = lax.ppermute(mine, axis, [(i, i ^ step) for i in range(count)])]
    ppermute x1, starting transfers between devices: 4.68 us -> 3.67 us  [on_device(): from_lo = lax.ppermute(send_hi, 'sp', up)]
    unnamed x22 -> x21, local copies, waits for them, and re-layouts: 4.48 us -> 4.36 us
  transfers between devices with their start and end apart: 11 -> 11, of which waited for: 5 -> 5; matrix products, arithmetic and copies ran while one was open for 8% -> 10% of each run, Pallas kernels for 10% -> 7%
where the time goes in v3:
time: 72 us; the launch traced here: 71.7 us
  starting transfers between devices  27 us (38%)
  waiting for transfers between devices  17.3 us (24%)
  Pallas kernels  16.9 us (23%)
  local copies, waits for them, and re-layouts  7.41 us (10%)
  other arithmetic  2.14 us (3%)
  between operations  1.02 us (1%)
    pallas_call x5, Pallas kernels, call(): pl.pallas_call(kernel, name=name, out_shape=outputs, in_specs=[smem] * sc...  16.9 us
    ppermute x5, waiting for transfers between devices, all_sum(): other = lax.ppermute(mine, axis, [(i, i ^ step) for i in range(count)])  13.8 us
    ppermute x5, starting transfers between devices, all_sum(): other = lax.ppermute(mine, axis, [(i, i ^ step) for i in range(count)])  11.1 us
    ppermute x1, starting transfers between devices, on_device(): lo2 = lax.ppermute(flat(volume[0, :, slab - 2]), 'sp', up)  5.01 us
    unnamed x21, local copies, waits for them, and re-layouts  4.36 us
    ppermute x1, starting transfers between devices, on_device(): from_lo = lax.ppermute(send_hi, 'sp', up)  3.67 us
    ppermute x1, waiting for transfers between devices, on_device(): hi1 = lax.ppermute(flat(volume[0, :, 0]), 'sp', down)  3.45 us
    ppermute x1, starting transfers between devices, on_device(): lo1 = lax.ppermute(flat(volume[0, :, slab - 1]), 'sp', up)  3.42 us
  transfers between devices with their start and end apart: 11, of which 5 were waited for; matrix products, arithmetic and copies ran while one was open for 10% of the time, Pallas kernels for 7%

profile of v3, /device:TPU:0, one launch (start us, length us, event | category | flops | bytes accessed | tf_op | source)
XLA Modules:
  0.0 71.7 jit_solution(2020941392831962684)
XLA Ops:
  0.6 1.4 %fusion.1 = (bf16[1,96,1,8,128]{4,3,2,1,0:T(8,128)(2,1)S(1)}, bf16[1,96,1,8,128]{4,3,2,1,0:T(8,128)(2,1)S(1)}, bf16[1,96,1,8,128]{4,3,2,1,0:T(8,128)(2,1)S(1)}, bf16[1,96,1,8,128]{4,3,2,1,0:T(8,128)(2,1)S(1)}) fusion(bf16[1,96,4,8,128]{4,3,2,1,0:T(8,128)(2,1)} %param.5), kind=kLoop, calls=%fused_computation.21 | loop fusion | bytes 1572864 | tf_op jit(solution)/shard_map/slice | solution.py:368
  2.1 5.0 %collective-permute-start.2 = (bf16[96,1024]{1,0:T(8,128)(2,1)S(1)}, bf16[96,1024]{1,0:T(8,128)(2,1)S(1)}, u32[]{:S(2)}, u32[]{:S(2)}) collective-permute-start(bf16[96,1024]{1,0:T(8,128)(2,1)S(1)} %bitcast.56), channel_id=1, source_target_pairs={{0,4},{4,8},{8,12},{12,16},{16,20},{20,24},{24,28},{1,5},{5,9},{9,... | collective-permute-start | bytes 589832 | tf_op jit(solution)/shard_map/ppermute | solution.py:367
  7.1 0.7 copy.33
  7.8 3.4 %collective-permute-start = (bf16[96,1024]{1,0:T(8,128)(2,1)}, bf16[96,1024]{1,0:T(8,128)(2,1)S(1)}, u32[]{:S(2)}, u32[]{:S(2)}) collective-permute-start(bf16[96,1024]{1,0:T(8,128)(2,1)} %bitcast.42), channel_id=1, source_target_pairs={{0,4},{4,8},{8,12},{12,16},{16,20},{20,24},{24,28},{1,5},{5,9},{9,... | collective-permute-start | bytes 589832 | tf_op jit(solution)/shard_map/ppermute | solution.py:365
  11.9 1.3 %collective-permute-start.1 = (bf16[96,1024]{1,0:T(8,128)(2,1)}, bf16[96,1024]{1,0:T(8,128)(2,1)S(1)}, u32[]{:S(2)}, u32[]{:S(2)}) collective-permute-start(bf16[96,1024]{1,0:T(8,128)(2,1)} %bitcast.41), channel_id=1, source_target_pairs={{4,0},{8,4},{12,8},{16,12},{20,16},{24,20},{28,24},{5,1},{9,5},{13... | collective-permute-start | bytes 589832 | tf_op jit(solution)/shard_map/ppermute | solution.py:366
  13.9 1.3 %collective-permute-start.3 = (bf16[96,1024]{1,0:T(8,128)(2,1)}, bf16[96,1024]{1,0:T(8,128)(2,1)S(1)}, u32[]{:S(2)}, u32[]{:S(2)}) collective-permute-start(bf16[96,1024]{1,0:T(8,128)(2,1)} %bitcast.39), channel_id=1, source_target_pairs={{4,0},{8,4},{12,8},{16,12},{20,16},{24,20},{28,24},{5,1},{9,5},{13... | collective-permute-start | bytes 589832 | tf_op jit(solution)/shard_map/ppermute | solution.py:368
  17.0 1.1 %inner.1 = (bf16[96,2048]{1,0:T(8,128)(2,1)S(1)}, bf16[96,2048]{1,0:T(8,128)(2,1)S(1)}, bf16[96,2048]{1,0:T(8,128)(2,1)S(1)}, bf16[96,2048]{1,0:T(8,128)(2,1)S(1)}) custom-call(bf16[96,4096]{1,0:T(8,128)(2,1)S(1)} %reshape_squeeze.18.vol, bf16[2,21,96,128]{3,2,1,0:T(8,128)(2,1)S(1)} %pad_maximum_fusion.taps, bf16[2,96,96]{2,1,0:T(8,128)(2,1)S(1)} %copy-done), custom_call_target="tpu_custom_call" | custom-call | bytes 1048576 | tf_op jit(solution)/shard_map/inner/pallas_call | solution.py:331
  18.3 3.5 %collective-permute-done.1.hi1 = bf16[96,1024]{1,0:T(8,128)(2,1)S(1)} collective-permute-done((bf16[96,1024]{1,0:T(8,128)(2,1)}, bf16[96,1024]{1,0:T(8,128)(2,1)S(1)}, u32[]{:S(2)}, u32[]{:S(2)}) %collective-permute-start.1) | collective-permute-done | bytes 196640 | tf_op jit(solution)/shard_map/ppermute | solution.py:366
  21.7 2.7 %middle.1 = (bf16[96,2048]{1,0:T(8,128)(2,1)S(1)}, bf16[96,2048]{1,0:T(8,128)(2,1)S(1)}, bf16[96,2048]{1,0:T(8,128)(2,1)S(1)}, bf16[96,2048]{1,0:T(8,128)(2,1)S(...) custom-call(bf16[96,4096]{1,0:T(8,128)(2,1)S(1)} %reshape_squeeze.18, ...), custom_call_target="tpu_custom_call" | custom-call | bytes 1048576 | tf_op jit(solution)/shard_map/middle/pallas_call | solution.py:331
  24.4 6.0 %edge.1 = (bf16[96,2048]{1,0:T(8,128)(2,1)S(1)}, bf16[96,2048]{1,0:T(8,128)(2,1)S(1)}, bf16[96,2048]{1,0:T(8,128)(2,1)S(1)}, bf16[96,2048]{1,0:T(8,128)(2,1)S(1)...) custom-call(f32[2]{0:T(128)S(1)} %add_convert_fusion.5.flags, ...), custom_call_target="tpu_custom_call" | custom-call | bytes 1048576 | tf_op jit(solution)/shard_map/edge/pallas_call | solution.py:331
  30.5 5.9 %weights.1 = (bf16[96,2048]{1,0:T(8,128)(2,1)S(1)}, f32[2,96,128]{2,1,0:T(8,128)S(1)}) custom-call(bf16[96,4096]{1,0:T(8,128)(2,1)S(1)} %reshape_squeeze.18.vol, bf16[96,1024]{1,0:T(8,128)(2,1)S(1)} %collective-permute-done.lo1, bf16[96,1024]{1,0:T(8,128)(2,1)S(1)} %collective-permute-done.1.hi1, bf16[96,1024]{1,0:T(8,128)(2,1)S(1)} %collective-permute-done.2.lo2, ...), custom_call_target="tpu_custom_call" | custom-call | bytes 1048576 | tf_op jit(solution)/shard_map/weights/pallas_call | solution.py:331
  36.5 1.2 %collective-permute-done.6 = bf16[2,96,128]{2,1,0:T(8,128)(2,1)S(1)} collective-permute-done((bf16[2,96,128]{2,1,0:T(8,128)(2,1)S(1)}, bf16[2,96,128]{2,1,0:T(8,128)(2,1)S(1)}, u32[]{:S(2)}, u32[]{:S(2)}) %collective-permute-start.6) | collective-permute-done | bytes 49184 | tf_op jit(solution)/shard_map/ppermute | solution.py:348
  37.7 1.6 %collective-permute-start.7 = (bf16[2,96,128]{2,1,0:T(8,128)(2,1)S(1)}, bf16[2,96,128]{2,1,0:T(8,128)(2,1)S(1)}, u32[]{:S(2)}, u32[]{:S(2)}) collective-permute-start(bf16[2,96,128]{2,1,0:T(8,128)(2,1)S(1)} %add_convert_fusion.4), channel_id=1, source_target_pairs={{0,2},{1,3},{2,0},{3,1},{4,6},{5,7},{6,4},{7,5},{8,10},{9,11},{10,... | collective-permute-start | bytes 147464 | tf_op jit(solution)/shard_map/ppermute | solution.py:348
  39.3 2.6 %collective-permute-done.7 = bf16[2,96,128]{2,1,0:T(8,128)(2,1)S(1)} collective-permute-done((bf16[2,96,128]{2,1,0:T(8,128)(2,1)S(1)}, bf16[2,96,128]{2,1,0:T(8,128)(2,1)S(1)}, u32[]{:S(2)}, u32[]{:S(2)}) %collective-permute-start.7) | collective-permute-done | bytes 49184 | tf_op jit(solution)/shard_map/ppermute | solution.py:348
  41.9 2.3 %collective-permute-start.8 = (bf16[2,96,128]{2,1,0:T(8,128)(2,1)S(1)}, bf16[2,96,128]{2,1,0:T(8,128)(2,1)S(1)}, u32[]{:S(2)}, u32[]{:S(2)}) collective-permute-start(bf16[2,96,128]{2,1,0:T(8,128)(2,1)S(1)} %add_convert_fusion.3), channel_id=1, source_target_pairs={{0,4},{4,0},{8,12},{12,8},{16,20},{20,16},{24,28},{28,24},{1,5},{5... | collective-permute-start | bytes 147464 | tf_op jit(solution)/shard_map/ppermute | solution.py:348
  44.2 2.1 %collective-permute-done.8 = bf16[2,96,128]{2,1,0:T(8,128)(2,1)S(1)} collective-permute-done((bf16[2,96,128]{2,1,0:T(8,128)(2,1)S(1)}, bf16[2,96,128]{2,1,0:T(8,128)(2,1)S(1)}, u32[]{:S(2)}, u32[]{:S(2)}) %collective-permute-start.8) | collective-permute-done | bytes 49184 | tf_op jit(solution)/shard_map/ppermute | solution.py:348
  46.3 2.7 %collective-permute-start.9 = (bf16[2,96,128]{2,1,0:T(8,128)(2,1)S(1)}, bf16[2,96,128]{2,1,0:T(8,128)(2,1)S(1)}, u32[]{:S(2)}, u32[]{:S(2)}) collective-permute-start(bf16[2,96,128]{2,1,0:T(8,128)(2,1)S(1)} %add_convert_fusion.2), channel_id=1, source_target_pairs={{0,8},{4,12},{8,0},{12,4},{16,24},{20,28},{24,16},{28,20},{1,9},{5... | collective-permute-start | bytes 147464 | tf_op jit(solution)/shard_map/ppermute | solution.py:348
  49.0 1.1 %volume.1 = bf16[96,4096]{1,0:T(8,128)(2,1)S(1)} custom-call(bf16[2,21,96,128]{3,2,1,0:T(8,128)(2,1)S(1)} %pad_maximum_fusion.taps, bf16[96,2048]{1,0:T(8,128)(2,1)S(1)} %get-tuple-element.56.gpl1_i, bf16[96,4096]{1,0:T(8,128)(2,1)S(1)} %get-tuple-element.55.gpl1_o), custom_call_target="tpu_custom_call" | custom-call | bytes 1048576 | tf_op jit(solution)/shard_map/volume/pallas_call | solution.py:331
  50.1 3.7 %collective-permute-start.4 = (bf16[96,2048]{1,0:T(8,128)(2,1)S(1)}, bf16[96,2048]{1,0:T(8,128)(2,1)}, u32[]{:S(2)}, u32[]{:S(2)}) collective-permute-start(bf16[96,2048]{1,0:T(8,128)(2,1)S(1)} %get-tuple-element.57), channel_id=1, source_target_pairs={{0,4},{4,8},{8,12},{12,16},{16,20},{20,24},{24,28},{1,5},{5,9},{9,... | collective-permute-start | bytes 1179656 | tf_op jit(solution)/shard_map/ppermute | solution.py:398
  53.8 1.3 %collective-permute-start.5 = (bf16[96,2048]{1,0:T(8,128)(2,1)S(1)}, bf16[96,2048]{1,0:T(8,128)(2,1)S(1)}, u32[]{:S(2)}, u32[]{:S(2)}) collective-permute-start(bf16[96,2048]{1,0:T(8,128)(2,1)S(1)} %get-tuple-element.58), channel_id=1, source_target_pairs={{4,0},{8,4},{12,8},{16,12},{20,16},{24,20},{28,24},{5,1},{9,5},{13... | collective-permute-start | bytes 1179656 | tf_op jit(solution)/shard_map/ppermute | solution.py:399
  55.1 4.5 %collective-permute-start.10 = (bf16[2,96,128]{2,1,0:T(8,128)(2,1)S(1)}, bf16[2,96,128]{2,1,0:T(8,128)(2,1)S(1)}, u32[]{:S(2)}, u32[]{:S(2)}) collective-permute-start(bf16[2,96,128]{2,1,0:T(8,128)(2,1)S(1)} %add_convert_fusion.1), channel_id=1, source_target_pairs={{0,16},{4,20},{8,24},{12,28},{16,0},{20,4},{24,8},{28,12},{1,17},{... | collective-permute-start | bytes 147464 | tf_op jit(solution)/shard_map/ppermute | solution.py:348
  60.0 7.9 %collective-permute-done.10 = bf16[2,96,128]{2,1,0:T(8,128)(2,1)S(1)} collective-permute-done((bf16[2,96,128]{2,1,0:T(8,128)(2,1)S(1)}, bf16[2,96,128]{2,1,0:T(8,128)(2,1)S(1)}, u32[]{:S(2)}, u32[]{:S(2)}) %collective-permute-start.10) | collective-permute-done | bytes 49184 | tf_op jit(solution)/shard_map/ppermute | solution.py:348
  69.4 1.1 %copy.24 = bf16[12,8,16,128]{3,2,1,0:T(8,128)(2,1)S(1)} copy(bf16[12,8,16,128]{3,1,2,0:T(8,128)(2,1)} %bitcast.25) | data formatting | bytes 786432
  70.6 1.1 %fusion = bf16[1,96,4,8,128]{4,3,2,1,0:T(8,128)(2,1)} fusion(f32[96,4,8,128]{3,2,1,0:T(8,128)S(1)} %bitcast.47, bf16[96,2,8,128]{3,2,1,0:T(8,128)(2,1)S(1)} %bitcast.49, bf16[96,2,8,128]{3,2,1,0:T(8,128)(2,1)S(1)} %bitcast.48), kind=kLoop, calls=%fused_computation.4 | loop fusion | flops 1966080 | bytes 3145728 | tf_op jit(solution)/shard_map/broadcast_in_dim | solution.py:422
  (51 shorter events, 5.4 us)
Async XLA Ops:
  0.6 14.6 %copy-start.1 = (bf16[1,96,4,8,128]{4,3,2,1,0:T(8,128)(2,1)S(1)}, bf16[1,96,4,8,128]{4,3,2,1,0:T(8,128)(2,1)}, u32[]{:S(2)}) copy-start(bf16[1,96,4,8,128]{4,3,2,1,0:T(8,128)(2,1)} %param.5) | copy-start | bytes 2359300
  2.0 13.6 %copy-start.5 = (bf16[2,96,3]{1,0,2:T(2,128)(2,1)S(1)}, bf16[2,96,3]{1,0,2:T(2,128)(2,1)}, u32[]{:S(2)}) copy-start(bf16[2,96,3]{1,0,2:T(2,128)(2,1)} %param.8) | copy-start | bytes 3460
  2.0 13.7 %copy-start.4 = (bf16[2,96,3,3]{1,0,3,2:T(2,128)(2,1)S(1)}, bf16[2,96,3,3]{1,0,3,2:T(2,128)(2,1)}, u32[]{:S(2)}) copy-start(bf16[2,96,3,3]{1,0,3,2:T(2,128)(2,1)} %param.7) | copy-start | bytes 10372
  2.0 13.8 %copy-start = (bf16[2,96,96]{2,1,0:T(8,128)(2,1)S(1)}, bf16[2,96,96]{2,1,0:T(8,128)(2,1)}, u32[]{:S(2)}) copy-start(bf16[2,96,96]{2,1,0:T(8,128)(2,1)} %mix.5) | copy-start | bytes 110596
  2.1 13.8 %copy-start.3 = (bf16[1,96,4,8,128]{4,3,2,1,0:T(8,128)(2,1)S(1)}, bf16[1,96,4,8,128]{4,3,2,1,0:T(8,128)(2,1)}, u32[]{:S(2)}) copy-start(bf16[1,96,4,8,128]{4,3,2,1,0:T(8,128)(2,1)} %param.6) | copy-start | bytes 2359300
  2.1 22.3 %collective-permute-start.2 = (bf16[96,1024]{1,0:T(8,128)(2,1)S(1)}, bf16[96,1024]{1,0:T(8,128)(2,1)S(1)}, u32[]{:S(2)}, u32[]{:S(2)}) collective-permute-start(bf16[96,1024]{1,0:T(8,128)(2,1)S(1)} %bitcast.56), channel_id=1, source_target_pairs={{0,4},{4,8},{8,12},{12,16},{16,20},{20,24},{24,28},{1,5},{5,9},{9,... | collective-permute-start | bytes 589832 | tf_op jit(solution)/shard_map/ppermute | solution.py:367
  7.8 10.4 %collective-permute-start = (bf16[96,1024]{1,0:T(8,128)(2,1)}, bf16[96,1024]{1,0:T(8,128)(2,1)S(1)}, u32[]{:S(2)}, u32[]{:S(2)}) collective-permute-start(bf16[96,1024]{1,0:T(8,128)(2,1)} %bitcast.42), channel_id=1, source_target_pairs={{0,4},{4,8},{8,12},{12,16},{16,20},{20,24},{24,28},{1,5},{5,9},{9,... | collective-permute-start | bytes 589832 | tf_op jit(solution)/shard_map/ppermute | solution.py:365
  11.9 9.8 %collective-permute-start.1 = (bf16[96,1024]{1,0:T(8,128)(2,1)}, bf16[96,1024]{1,0:T(8,128)(2,1)S(1)}, u32[]{:S(2)}, u32[]{:S(2)}) collective-permute-start(bf16[96,1024]{1,0:T(8,128)(2,1)} %bitcast.41), channel_id=1, source_target_pairs={{4,0},{8,4},{12,8},{16,12},{20,16},{24,20},{28,24},{5,1},{9,5},{13... | collective-permute-start | bytes 589832 | tf_op jit(solution)/shard_map/ppermute | solution.py:366
  13.9 10.5 %collective-permute-start.3 = (bf16[96,1024]{1,0:T(8,128)(2,1)}, bf16[96,1024]{1,0:T(8,128)(2,1)S(1)}, u32[]{:S(2)}, u32[]{:S(2)}) collective-permute-start(bf16[96,1024]{1,0:T(8,128)(2,1)} %bitcast.39), channel_id=1, source_target_pairs={{4,0},{8,4},{12,8},{16,12},{20,16},{24,20},{28,24},{5,1},{9,5},{13... | collective-permute-start | bytes 589832 | tf_op jit(solution)/shard_map/ppermute | solution.py:368
  36.4 1.3 %collective-permute-start.6 = (bf16[2,96,128]{2,1,0:T(8,128)(2,1)S(1)}, bf16[2,96,128]{2,1,0:T(8,128)(2,1)S(1)}, u32[]{:S(2)}, u32[]{:S(2)}) collective-permute-start(bf16[2,96,128]{2,1,0:T(8,128)(2,1)S(1)} %convert_element_type.60), channel_id=1, source_target_pairs={{0,1},{1,0},{2,3},{3,2},{4,5},{5,4},{6,7},{7,6},{8,9},{9,8},{10,11... | collective-permute-start | bytes 147464 | tf_op jit(solution)/shard_map/ppermute | solution.py:348
  37.7 4.2 %collective-permute-start.7 = (bf16[2,96,128]{2,1,0:T(8,128)(2,1)S(1)}, bf16[2,96,128]{2,1,0:T(8,128)(2,1)S(1)}, u32[]{:S(2)}, u32[]{:S(2)}) collective-permute-start(bf16[2,96,128]{2,1,0:T(8,128)(2,1)S(1)} %add_convert_fusion.4), channel_id=1, source_target_pairs={{0,2},{1,3},{2,0},{3,1},{4,6},{5,7},{6,4},{7,5},{8,10},{9,11},{10,... | collective-permute-start | bytes 147464 | tf_op jit(solution)/shard_map/ppermute | solution.py:348
  41.9 4.4 %collective-permute-start.8 = (bf16[2,96,128]{2,1,0:T(8,128)(2,1)S(1)}, bf16[2,96,128]{2,1,0:T(8,128)(2,1)S(1)}, u32[]{:S(2)}, u32[]{:S(2)}) collective-permute-start(bf16[2,96,128]{2,1,0:T(8,128)(2,1)S(1)} %add_convert_fusion.3), channel_id=1, source_target_pairs={{0,4},{4,0},{8,12},{12,8},{16,20},{20,16},{24,28},{28,24},{1,5},{5... | collective-permute-start | bytes 147464 | tf_op jit(solution)/shard_map/ppermute | solution.py:348
  46.3 8.8 %collective-permute-start.9 = (bf16[2,96,128]{2,1,0:T(8,128)(2,1)S(1)}, bf16[2,96,128]{2,1,0:T(8,128)(2,1)S(1)}, u32[]{:S(2)}, u32[]{:S(2)}) collective-permute-start(bf16[2,96,128]{2,1,0:T(8,128)(2,1)S(1)} %add_convert_fusion.2), channel_id=1, source_target_pairs={{0,8},{4,12},{8,0},{12,4},{16,24},{20,28},{24,16},{28,20},{1,9},{5... | collective-permute-start | bytes 147464 | tf_op jit(solution)/shard_map/ppermute | solution.py:348
  50.1 19.3 %collective-permute-start.4 = (bf16[96,2048]{1,0:T(8,128)(2,1)S(1)}, bf16[96,2048]{1,0:T(8,128)(2,1)}, u32[]{:S(2)}, u32[]{:S(2)}) collective-permute-start(bf16[96,2048]{1,0:T(8,128)(2,1)S(1)} %get-tuple-element.57), channel_id=1, source_target_pairs={{0,4},{4,8},{8,12},{12,16},{16,20},{20,24},{24,28},{1,5},{5,9},{9,... | collective-permute-start | bytes 1179656 | tf_op jit(solution)/shard_map/ppermute | solution.py:398
  53.8 16.7 %collective-permute-start.5 = (bf16[96,2048]{1,0:T(8,128)(2,1)S(1)}, bf16[96,2048]{1,0:T(8,128)(2,1)S(1)}, u32[]{:S(2)}, u32[]{:S(2)}) collective-permute-start(bf16[96,2048]{1,0:T(8,128)(2,1)S(1)} %get-tuple-element.58), channel_id=1, source_target_pairs={{4,0},{8,4},{12,8},{16,12},{20,16},{24,20},{28,24},{5,1},{9,5},{13... | collective-permute-start | bytes 1179656 | tf_op jit(solution)/shard_map/ppermute | solution.py:399
  55.1 12.8 %collective-permute-start.10 = (bf16[2,96,128]{2,1,0:T(8,128)(2,1)S(1)}, bf16[2,96,128]{2,1,0:T(8,128)(2,1)S(1)}, u32[]{:S(2)}, u32[]{:S(2)}) collective-permute-start(bf16[2,96,128]{2,1,0:T(8,128)(2,1)S(1)} %add_convert_fusion.1), channel_id=1, source_target_pairs={{0,16},{4,20},{8,24},{12,28},{16,0},{20,4},{24,8},{28,12},{1,17},{... | collective-permute-start | bytes 147464 | tf_op jit(solution)/shard_map/ppermute | solution.py:348
  67.9 3.8 %copy-start.2 = (f32[2,96,128]{2,1,0:T(8,128)}, f32[2,96,128]{2,1,0:T(8,128)S(1)}, u32[]{:S(2)}) copy-start(f32[2,96,128]{2,1,0:T(8,128)S(1)} %convert_add_fusion) | copy-start | bytes 294916

commit v4 on v3

--- a/solution.py
+++ b/solution.py
@@ -398,18 +398,30 @@
     from_lo = lax.ppermute(send_hi, "sp", up)
     from_hi = lax.ppermute(send_lo, "sp", down)
     count = lax.axis_size("dp") * slab * ranks * nz * ny
-    gpl1_i, payload = call(
-        functools.partial(weight_kernel, sizes, slab, 1.0 / math.sqrt(count)),
-        "weights",
+
+    def weight_sums(operands):
+        gpl1_i, payload = call(
+            functools.partial(weight_kernel, sizes, slab, 1.0 / math.sqrt(count)),
+            "weights",
+            operands,
+            [planes(inside), jax.ShapeDtypeStruct((2, channels, 128), F32)],
+            scratch=[scratch(inside), scratch(inside), pltpu.VMEM((2, 12, channels, ny), F32)],
+        )
+        return gpl1_i, all_sum(payload)
+
+    def nothing(operands):
+        return jnp.zeros((channels, inside * plane), BF16), jnp.zeros((2, channels, 128), F32)
+
+    gpl1_i, total = lax.cond(
+        place < ranks,
+        weight_sums,
+        nothing,
         (
             vol, lo1, hi1, lo2, hi2, taps, mix_t,
             pl1_i, ax1_i, sl1_i, hid_i, pl1_e, ax1_e, hid_e, pl2_i, ax2_i, gpre2_i, gax2_i, gpl2_i,
             pl1_r, ax1_r, hid_r, pl2_e, ax2_e, gpre2_e, gax2_e, gpl2_e, gpre1_o, gax1_o, gpl1_o,
         ),
-        [planes(inside), jax.ShapeDtypeStruct((2, channels, 128), F32)],
-        scratch=[scratch(inside), scratch(inside), pltpu.VMEM((2, 12, channels, ny), F32)],
-    )
-    total = all_sum(payload)
+    )
     (own,) = call(
         functools.partial(volume_kernel, sizes, slab), "volume", (taps, gpl1_i, gpl1_o), [planes(slab)]
     )

time: 72 us -> 84.7 us (1.18)
  Pallas kernels: 16.9 us -> 28.4 us
  local copies, waits for them, and re-layouts: 7.41 us -> 11.8 us
  waiting for transfers between devices: 17.3 us -> 13.3 us
    pallas_call x5, Pallas kernels: 16.9 us -> 28.4 us  [call(): pl.pallas_call(kernel, name=name, out_shape=outputs, in_specs=[smem] * sc...]
    ppermute x5, waiting for transfers between devices: 13.8 us -> 10.4 us  [all_sum(): other = lax.ppermute(mine, axis, [(i, i ^ step) for i in range(count)])]
    slice x2, local copies, waits for them, and re-layouts: 0.77 us -> 2.6 us  [on_device(): total[:, :, channels:channels + 9].reshape(2, channels, 3, 3)]
    cond x0 -> x2, local copies, waits for them, and re-layouts: none -> 1.62 us
    slice x1, local copies, waits for them, and re-layouts: 0.08 us -> 0.97 us  [on_device(): total[:, :, channels + 9:channels + 12]]
    unnamed x21 -> x28, local copies, waits for them, and re-layouts: 4.36 us -> 4.38 us
  transfers between devices with their start and end apart: 11 -> 11, of which waited for: 5 -> 6; matrix products, arithmetic and copies ran while one was open for 10% -> 13% of each run, Pallas kernels for 7% -> 23%
where the time goes in v4:
time: 84.7 us; the launch traced here: 84.1 us
  Pallas kernels  28.4 us (34%)
  starting transfers between devices  26.9 us (32%)
  waiting for transfers between devices  13.3 us (16%)
  local copies, waits for them, and re-layouts  11.8 us (14%)
  other arithmetic  2.78 us (3%)
  between operations  0.92 us (1%)
    pallas_call x5, Pallas kernels, call(): pl.pallas_call(kernel, name=name, out_shape=outputs, in_specs=[smem] * sc...  28.4 us
    ppermute x5, waiting for transfers between devices, all_sum(): other = lax.ppermute(mine, axis, [(i, i ^ step) for i in range(count)])  10.4 us
    ppermute x5, starting transfers between devices, all_sum(): other = lax.ppermute(mine, axis, [(i, i ^ step) for i in range(count)])  10.3 us
    ppermute x1, starting transfers between devices, on_device(): lo2 = lax.ppermute(flat(volume[0, :, slab - 2]), 'sp', up)  5.69 us
    unnamed x28, local copies, waits for them, and re-layouts  4.38 us
    ppermute x1, starting transfers between devices, on_device(): from_lo = lax.ppermute(send_hi, 'sp', up)  3.49 us
    ppermute x1, starting transfers between devices, on_device(): lo1 = lax.ppermute(flat(volume[0, :, slab - 1]), 'sp', up)  3.41 us
    ppermute x1, waiting for transfers between devices, on_device(): hi1 = lax.ppermute(flat(volume[0, :, 0]), 'sp', down)  2.82 us
  transfers between devices with their start and end apart: 11, of which 6 were waited for; matrix products, arithmetic and copies ran while one was open for 13% of the time, Pallas kernels for 23%

profile of v4, /device:TPU:0, one launch (start us, length us, event | category | flops | bytes accessed | tf_op | source)
XLA Modules:
  0.0 84.1 jit_solution(188488405777690009)
XLA Ops:
  0.6 1.4 %fusion.1 = (bf16[1,96,1,8,128]{4,3,2,1,0:T(8,128)(2,1)S(1)}, bf16[1,96,1,8,128]{4,3,2,1,0:T(8,128)(2,1)S(1)}, bf16[1,96,1,8,128]{4,3,2,1,0:T(8,128)(2,1)S(1)}, bf16[1,96,1,8,128]{4,3,2,1,0:T(8,128)(2,1)S(1)}) fusion(bf16[1,96,4,8,128]{4,3,2,1,0:T(8,128)(2,1)} %param.7), kind=kLoop, calls=%fused_computation.21 | loop fusion | bytes 1572864 | tf_op jit(solution)/shard_map/slice | solution.py:368
  2.8 5.7 %collective-permute-start.7 = (bf16[96,1024]{1,0:T(8,128)(2,1)}, bf16[96,1024]{1,0:T(8,128)(2,1)}, u32[]{:S(2)}, u32[]{:S(2)}) collective-permute-start(bf16[96,1024]{1,0:T(8,128)(2,1)} %bitcast.40), channel_id=1, source_target_pairs={{0,4},{4,8},{8,12},{12,16},{16,20},{20,24},{24,28},{1,5},{5,9},{9,... | collective-permute-start | bytes 589832 | tf_op jit(solution)/shard_map/ppermute | solution.py:367
  9.1 3.4 %collective-permute-start.5 = (bf16[96,1024]{1,0:T(8,128)(2,1)}, bf16[96,1024]{1,0:T(8,128)(2,1)}, u32[]{:S(2)}, u32[]{:S(2)}) collective-permute-start(bf16[96,1024]{1,0:T(8,128)(2,1)} %bitcast.42), channel_id=1, source_target_pairs={{0,4},{4,8},{8,12},{12,16},{16,20},{20,24},{24,28},{1,5},{5,9},{9,... | collective-permute-start | bytes 589832 | tf_op jit(solution)/shard_map/ppermute | solution.py:365
  13.3 1.3 %collective-permute-start.6 = (bf16[96,1024]{1,0:T(8,128)(2,1)}, bf16[96,1024]{1,0:T(8,128)(2,1)}, u32[]{:S(2)}, u32[]{:S(2)}) collective-permute-start(bf16[96,1024]{1,0:T(8,128)(2,1)} %bitcast.41), channel_id=1, source_target_pairs={{4,0},{8,4},{12,8},{16,12},{20,16},{24,20},{28,24},{5,1},{9,5},{13... | collective-permute-start | bytes 589832 | tf_op jit(solution)/shard_map/ppermute | solution.py:366
  15.2 1.3 %collective-permute-start.8 = (bf16[96,1024]{1,0:T(8,128)(2,1)}, bf16[96,1024]{1,0:T(8,128)(2,1)}, u32[]{:S(2)}, u32[]{:S(2)}) collective-permute-start(bf16[96,1024]{1,0:T(8,128)(2,1)} %bitcast.39), channel_id=1, source_target_pairs={{4,0},{8,4},{12,8},{16,12},{20,16},{24,20},{28,24},{5,1},{9,5},{13... | collective-permute-start | bytes 589832 | tf_op jit(solution)/shard_map/ppermute | solution.py:368
  18.4 1.9 %inner.1 = (bf16[96,2048]{1,0:T(8,128)(2,1)}, bf16[96,2048]{1,0:T(8,128)(2,1)}, bf16[96,2048]{1,0:T(8,128)(2,1)}, bf16[96,2048]{1,0:T(8,128)(2,1)S(1)}) custom-call(bf16[96,4096]{1,0:T(8,128)(2,1)S(1)} %reshape_squeeze.18.vol, bf16[2,21,96,128]{3,2,1,0:T(8,128)(2,1)S(1)} %pad_maximum_fusion.taps, bf16[2,96,96]{2,1,0:T(8,128)(2,1)S(1)} %copy-done), custom_call_target="tpu_custom_call" | custom-call | bytes 1048576 | tf_op jit(solution)/shard_map/inner/pallas_call | solution.py:331
  20.3 2.8 %collective-permute-done.6.hi1 = bf16[96,1024]{1,0:T(8,128)(2,1)} collective-permute-done((bf16[96,1024]{1,0:T(8,128)(2,1)}, bf16[96,1024]{1,0:T(8,128)(2,1)}, u32[]{:S(2)}, u32[]{:S(2)}) %collective-permute-start.6) | collective-permute-done | bytes 196640 | tf_op jit(solution)/shard_map/ppermute | solution.py:366
  23.1 5.1 %middle.1 = (bf16[96,2048]{1,0:T(8,128)(2,1)}, bf16[96,2048]{1,0:T(8,128)(2,1)}, bf16[96,2048]{1,0:T(8,128)(2,1)S(1)}, bf16[96,2048]{1,0:T(8,128)(2,1)S(1)}, bf1...) custom-call(bf16[96,4096]{1,0:T(8,128)(2,1)S(1)} %reshape_squeeze.18, ...), custom_call_target="tpu_custom_call" | custom-call | bytes 1048576 | tf_op jit(solution)/shard_map/middle/pallas_call | solution.py:331
  28.2 9.1 %edge.1 = (bf16[96,2048]{1,0:T(8,128)(2,1)}, bf16[96,2048]{1,0:T(8,128)(2,1)}, bf16[96,2048]{1,0:T(8,128)(2,1)}, bf16[96,2048]{1,0:T(8,128)(2,1)}, bf16[96,2048]...) custom-call(f32[2]{0:T(128)S(1)} %add_convert_fusion.5.flags, ...), custom_call_target="tpu_custom_call" | custom-call | bytes 1048576 | tf_op jit(solution)/shard_map/edge/pallas_call | solution.py:331
  37.4 3.5 %collective-permute-start.9 = (bf16[96,2048]{1,0:T(8,128)(2,1)S(1)}, bf16[96,2048]{1,0:T(8,128)(2,1)}, u32[]{:S(2)}, u32[]{:S(2)}) collective-permute-start(bf16[96,2048]{1,0:T(8,128)(2,1)S(1)} %get-tuple-element.155), channel_id=1, source_target_pairs={{0,4},{4,8},{8,12},{12,16},{16,20},{20,24},{24,28},{1,5},{5,9},{9,... | collective-permute-start | bytes 1179656 | tf_op jit(solution)/shard_map/ppermute | solution.py:398
  40.9 1.5 %collective-permute-start.10 = (bf16[96,2048]{1,0:T(8,128)(2,1)S(1)}, bf16[96,2048]{1,0:T(8,128)(2,1)S(1)}, u32[]{:S(2)}, u32[]{:S(2)}) collective-permute-start(bf16[96,2048]{1,0:T(8,128)(2,1)S(1)} %get-tuple-element.156), channel_id=1, source_target_pairs={{4,0},{8,4},{12,8},{16,12},{20,16},{24,20},{28,24},{5,1},{9,5},{13... | collective-permute-start | bytes 1179656 | tf_op jit(solution)/shard_map/ppermute | solution.py:399
  42.3 36.8 %conditional.1 = (bf16[96,2048]{1,0:T(8,128)(2,1)S(1)}, f32[2,96,128]{2,1,0:T(8,128)}, f32[2,96,96]{2,1,0:T(8,128)}, f32[2,96,9]{2,1,0:T(8,128)}, f32[2,96,3,3]{1,0,3,2:T(2,128)S(1)}, /*index=5*/f32[2,96,3]{1,0,2:T(2,128)S(1)}) conditional(s32[]{:T(128)} %convert_element_type.61, () %tuple.18, (bf16[96,4096]{1,0:T(8,128)(2,1)S(1)}, ...), branch_computations={%region_0.1_spmd, %region_1.2_spmd} | conditional | flops 516096 | bytes 3199224 | solution.py:415
  42.3 10.1 %weights.1 = (bf16[96,2048]{1,0:T(8,128)(2,1)S(1)}, f32[2,96,128]{2,1,0:T(8,128)S(1)}) custom-call(bf16[96,4096]{1,0:T(8,128)(2,1)S(1)} %get-tuple-element.64.vol, bf16[96,1024]{1,0:T(8,128)(2,1)} %get-tuple-element.65.lo1, bf16[96,1024]{1,0:T(8,128)(2,1)} %get-tuple-element.66.hi1, bf16[96,1024]{1,0:T(8,128)(2,1)} %get-tuple-element.67.lo2, ...), custom_call_target="tpu_custom_call" | custom-call | bytes 1048576 | tf_op jit(solution)/shard_map/cond/branch_1_fun/weights/pallas_call | solution.py:331
  53.8 1.6 %collective-permute-start.1 = (bf16[2,96,128]{2,1,0:T(8,128)(2,1)S(1)}, bf16[2,96,128]{2,1,0:T(8,128)(2,1)S(1)}, u32[]{:S(2)}, u32[]{:S(2)}) collective-permute-start(bf16[2,96,128]{2,1,0:T(8,128)(2,1)S(1)} %add_convert_fusion.3), channel_id=1, source_target_pairs={{0,2},{1,3},{2,0},{3,1},{4,6},{5,7},{6,4},{7,5},{8,10},{9,11},{10,... | collective-permute-start | bytes 147464 | tf_op jit(solution)/shard_map/cond/branch_1_fun/ppermute | solution.py:348
  55.3 2.6 %collective-permute-done.1 = bf16[2,96,128]{2,1,0:T(8,128)(2,1)S(1)} collective-permute-done((bf16[2,96,128]{2,1,0:T(8,128)(2,1)S(1)}, bf16[2,96,128]{2,1,0:T(8,128)(2,1)S(1)}, u32[]{:S(2)}, u32[]{:S(2)}) %collective-permute-start.1) | collective-permute-done | bytes 49184 | tf_op jit(solution)/shard_map/cond/branch_1_fun/ppermute | solution.py:348
  57.9 2.7 %collective-permute-start.2 = (bf16[2,96,128]{2,1,0:T(8,128)(2,1)S(1)}, bf16[2,96,128]{2,1,0:T(8,128)(2,1)S(1)}, u32[]{:S(2)}, u32[]{:S(2)}) collective-permute-start(bf16[2,96,128]{2,1,0:T(8,128)(2,1)S(1)} %add_convert_fusion.2), channel_id=1, source_target_pairs={{0,4},{4,0},{8,12},{12,8},{16,20},{20,16},{24,28},{28,24},{1,5},{5... | collective-permute-start | bytes 147464 | tf_op jit(solution)/shard_map/cond/branch_1_fun/ppermute | solution.py:348
  60.6 2.1 %collective-permute-done.2 = bf16[2,96,128]{2,1,0:T(8,128)(2,1)S(1)} collective-permute-done((bf16[2,96,128]{2,1,0:T(8,128)(2,1)S(1)}, bf16[2,96,128]{2,1,0:T(8,128)(2,1)S(1)}, u32[]{:S(2)}, u32[]{:S(2)}) %collective-permute-start.2) | collective-permute-done | bytes 49184 | tf_op jit(solution)/shard_map/cond/branch_1_fun/ppermute | solution.py:348
  62.7 3.4 %collective-permute-start.3 = (bf16[2,96,128]{2,1,0:T(8,128)(2,1)S(1)}, bf16[2,96,128]{2,1,0:T(8,128)(2,1)S(1)}, u32[]{:S(2)}, u32[]{:S(2)}) collective-permute-start(bf16[2,96,128]{2,1,0:T(8,128)(2,1)S(1)} %add_convert_fusion.1), channel_id=1, source_target_pairs={{0,8},{4,12},{8,0},{12,4},{16,24},{20,28},{24,16},{28,20},{1,9},{5... | collective-permute-start | bytes 147464 | tf_op jit(solution)/shard_map/cond/branch_1_fun/ppermute | solution.py:348
  66.1 2.1 %collective-permute-done.3 = bf16[2,96,128]{2,1,0:T(8,128)(2,1)S(1)} collective-permute-done((bf16[2,96,128]{2,1,0:T(8,128)(2,1)S(1)}, bf16[2,96,128]{2,1,0:T(8,128)(2,1)S(1)}, u32[]{:S(2)}, u32[]{:S(2)}) %collective-permute-start.3) | collective-permute-done | bytes 49184 | tf_op jit(solution)/shard_map/cond/branch_1_fun/ppermute | solution.py:348
  68.2 2.6 %collective-permute-start.4 = (bf16[2,96,128]{2,1,0:T(8,128)(2,1)S(1)}, bf16[2,96,128]{2,1,0:T(8,128)(2,1)S(1)}, u32[]{:S(2)}, u32[]{:S(2)}) collective-permute-start(bf16[2,96,128]{2,1,0:T(8,128)(2,1)S(1)} %add_convert_fusion), channel_id=1, source_target_pairs={{0,16},{4,20},{8,24},{12,28},{16,0},{20,4},{24,8},{28,12},{1,17},{... | collective-permute-start | bytes 147464 | tf_op jit(solution)/shard_map/cond/branch_1_fun/ppermute | solution.py:348
  70.8 2.5 %collective-permute-done.4 = bf16[2,96,128]{2,1,0:T(8,128)(2,1)S(1)} collective-permute-done((bf16[2,96,128]{2,1,0:T(8,128)(2,1)S(1)}, bf16[2,96,128]{2,1,0:T(8,128)(2,1)S(1)}, u32[]{:S(2)}, u32[]{:S(2)}) %collective-permute-start.4) | collective-permute-done | bytes 49184 | tf_op jit(solution)/shard_map/cond/branch_1_fun/ppermute | solution.py:348
  73.9 1.6 %slice.38 = f32[2,96,9]{2,1,0:T(8,128)} slice(f32[2,96,128]{2,1,0:T(8,128)} %convert_add_fusion), slice={[0:2], [0:96], [96:105]} | slice | bytes 13824 | tf_op jit(solution)/shard_map/slice | solution.py:436
  77.5 1.5 %copy.44 = f32[2,96,96]{2,1,0:T(8,128)} copy(f32[2,96,96]{2,1,0:T(8,128)} %bitcast.43) | data formatting | bytes 147456 | tf_op jit(solution)/shard_map/cond
  79.1 2.3 %volume.1 = bf16[96,4096]{1,0:T(8,128)(2,1)S(1)} custom-call(bf16[2,21,96,128]{3,2,1,0:T(8,128)(2,1)S(1)} %pad_maximum_fusion.taps, bf16[96,2048]{1,0:T(8,128)(2,1)S(1)} %get-tuple-element.154.gpl1_i, bf16[96,4096]{1,0:T(8,128)(2,1)} %get-tuple-element.153.gpl1_o), custom_call_target="tpu_custom_call" | custom-call | bytes 1048576 | tf_op jit(solution)/shard_map/volume/pallas_call | solution.py:331
  (61 shorter events, 11.3 us)
Async XLA Ops:
  0.6 15.9 %copy-start.2 = (bf16[1,96,4,8,128]{4,3,2,1,0:T(8,128)(2,1)S(1)}, bf16[1,96,4,8,128]{4,3,2,1,0:T(8,128)(2,1)}, u32[]{:S(2)}) copy-start(bf16[1,96,4,8,128]{4,3,2,1,0:T(8,128)(2,1)} %param.7) | copy-start | bytes 2359300
  2.0 14.9 %copy-start.9 = (bf16[2,96,3]{1,0,2:T(2,128)(2,1)S(1)}, bf16[2,96,3]{1,0,2:T(2,128)(2,1)}, u32[]{:S(2)}) copy-start(bf16[2,96,3]{1,0,2:T(2,128)(2,1)} %param.10) | copy-start | bytes 3460
  2.0 15.0 %copy-start.6 = (bf16[2,96,3,3]{1,0,3,2:T(2,128)(2,1)S(1)}, bf16[2,96,3,3]{1,0,3,2:T(2,128)(2,1)}, u32[]{:S(2)}) copy-start(bf16[2,96,3,3]{1,0,3,2:T(2,128)(2,1)} %param.9) | copy-start | bytes 10372
  2.0 15.1 %copy-start = (bf16[2,96,96]{2,1,0:T(8,128)(2,1)S(1)}, bf16[2,96,96]{2,1,0:T(8,128)(2,1)}, u32[]{:S(2)}) copy-start(bf16[2,96,96]{2,1,0:T(8,128)(2,1)} %mix.5) | copy-start | bytes 110596
  2.7 14.5 %copy-start.5 = (bf16[1,96,4,8,128]{4,3,2,1,0:T(8,128)(2,1)S(1)}, bf16[1,96,4,8,128]{4,3,2,1,0:T(8,128)(2,1)}, u32[]{:S(2)}) copy-start(bf16[1,96,4,8,128]{4,3,2,1,0:T(8,128)(2,1)} %param.8) | copy-start | bytes 2359300
  2.8 25.5 %collective-permute-start.7 = (bf16[96,1024]{1,0:T(8,128)(2,1)}, bf16[96,1024]{1,0:T(8,128)(2,1)}, u32[]{:S(2)}, u32[]{:S(2)}) collective-permute-start(bf16[96,1024]{1,0:T(8,128)(2,1)} %bitcast.40), channel_id=1, source_target_pairs={{0,4},{4,8},{8,12},{12,16},{16,20},{20,24},{24,28},{1,5},{5,9},{9,... | collective-permute-start | bytes 589832 | tf_op jit(solution)/shard_map/ppermute | solution.py:367
  9.1 11.2 %collective-permute-start.5 = (bf16[96,1024]{1,0:T(8,128)(2,1)}, bf16[96,1024]{1,0:T(8,128)(2,1)}, u32[]{:S(2)}, u32[]{:S(2)}) collective-permute-start(bf16[96,1024]{1,0:T(8,128)(2,1)} %bitcast.42), channel_id=1, source_target_pairs={{0,4},{4,8},{8,12},{12,16},{16,20},{20,24},{24,28},{1,5},{5,9},{9,... | collective-permute-start | bytes 589832 | tf_op jit(solution)/shard_map/ppermute | solution.py:365
  13.3 9.9 %collective-permute-start.6 = (bf16[96,1024]{1,0:T(8,128)(2,1)}, bf16[96,1024]{1,0:T(8,128)(2,1)}, u32[]{:S(2)}, u32[]{:S(2)}) collective-permute-start(bf16[96,1024]{1,0:T(8,128)(2,1)} %bitcast.41), channel_id=1, source_target_pairs={{4,0},{8,4},{12,8},{16,12},{20,16},{24,20},{28,24},{5,1},{9,5},{13... | collective-permute-start | bytes 589832 | tf_op jit(solution)/shard_map/ppermute | solution.py:366
  15.2 13.0 %collective-permute-start.8 = (bf16[96,1024]{1,0:T(8,128)(2,1)}, bf16[96,1024]{1,0:T(8,128)(2,1)}, u32[]{:S(2)}, u32[]{:S(2)}) collective-permute-start(bf16[96,1024]{1,0:T(8,128)(2,1)} %bitcast.39), channel_id=1, source_target_pairs={{4,0},{8,4},{12,8},{16,12},{20,16},{24,20},{28,24},{5,1},{9,5},{13... | collective-permute-start | bytes 589832 | tf_op jit(solution)/shard_map/ppermute | solution.py:368
  20.2 8.0 %copy-start.1 = (bf16[96,2048]{1,0:T(8,128)(2,1)}, bf16[96,2048]{1,0:T(8,128)(2,1)S(1)}, u32[]{:S(2)}) copy-start(bf16[96,2048]{1,0:T(8,128)(2,1)S(1)} %get-tuple-element.133.hid_i) | copy-start | bytes 1179652
  28.2 9.2 %copy-start.3 = (bf16[96,2048]{1,0:T(8,128)(2,1)}, bf16[96,2048]{1,0:T(8,128)(2,1)S(1)}, u32[]{:S(2)}) copy-start(bf16[96,2048]{1,0:T(8,128)(2,1)S(1)} %get-tuple-element.136.hid_e) | copy-start | bytes 1179652
  28.2 9.2 %copy-start.4 = (bf16[96,2048]{1,0:T(8,128)(2,1)}, bf16[96,2048]{1,0:T(8,128)(2,1)S(1)}, u32[]{:S(2)}) copy-start(bf16[96,2048]{1,0:T(8,128)(2,1)S(1)} %get-tuple-element.141.gpl2_i) | copy-start | bytes 1179652
  37.4 44.5 %collective-permute-start.9 = (bf16[96,2048]{1,0:T(8,128)(2,1)S(1)}, bf16[96,2048]{1,0:T(8,128)(2,1)}, u32[]{:S(2)}, u32[]{:S(2)}) collective-permute-start(bf16[96,2048]{1,0:T(8,128)(2,1)S(1)} %get-tuple-element.155), channel_id=1, source_target_pairs={{0,4},{4,8},{8,12},{12,16},{16,20},{20,24},{24,28},{1,5},{5,9},{9,... | collective-permute-start | bytes 1179656 | tf_op jit(solution)/shard_map/ppermute | solution.py:398
  40.9 42.1 %collective-permute-start.10 = (bf16[96,2048]{1,0:T(8,128)(2,1)S(1)}, bf16[96,2048]{1,0:T(8,128)(2,1)S(1)}, u32[]{:S(2)}, u32[]{:S(2)}) collective-permute-start(bf16[96,2048]{1,0:T(8,128)(2,1)S(1)} %get-tuple-element.156), channel_id=1, source_target_pairs={{4,0},{8,4},{12,8},{16,12},{20,16},{24,20},{28,24},{5,1},{9,5},{13... | collective-permute-start | bytes 1179656 | tf_op jit(solution)/shard_map/ppermute | solution.py:399
  52.4 1.3 %collective-permute-start = (bf16[2,96,128]{2,1,0:T(8,128)(2,1)S(1)}, bf16[2,96,128]{2,1,0:T(8,128)(2,1)S(1)}, u32[]{:S(2)}, u32[]{:S(2)}) collective-permute-start(bf16[2,96,128]{2,1,0:T(8,128)(2,1)S(1)} %convert_element_type.32), channel_id=1, source_target_pairs={{0,1},{1,0},{2,3},{3,2},{4,5},{5,4},{6,7},{7,6},{8,9},{9,8},{10,11... | collective-permute-start | bytes 147464 | tf_op jit(solution)/shard_map/cond/branch_1_fun/ppermute | solution.py:348
  53.8 4.2 %collective-permute-start.1 = (bf16[2,96,128]{2,1,0:T(8,128)(2,1)S(1)}, bf16[2,96,128]{2,1,0:T(8,128)(2,1)S(1)}, u32[]{:S(2)}, u32[]{:S(2)}) collective-permute-start(bf16[2,96,128]{2,1,0:T(8,128)(2,1)S(1)} %add_convert_fusion.3), channel_id=1, source_target_pairs={{0,2},{1,3},{2,0},{3,1},{4,6},{5,7},{6,4},{7,5},{8,10},{9,11},{10,... | collective-permute-start | bytes 147464 | tf_op jit(solution)/shard_map/cond/branch_1_fun/ppermute | solution.py:348
  57.9 4.8 %collective-permute-start.2 = (bf16[2,96,128]{2,1,0:T(8,128)(2,1)S(1)}, bf16[2,96,128]{2,1,0:T(8,128)(2,1)S(1)}, u32[]{:S(2)}, u32[]{:S(2)}) collective-permute-start(bf16[2,96,128]{2,1,0:T(8,128)(2,1)S(1)} %add_convert_fusion.2), channel_id=1, source_target_pairs={{0,4},{4,0},{8,12},{12,8},{16,20},{20,16},{24,28},{28,24},{1,5},{5... | collective-permute-start | bytes 147464 | tf_op jit(solution)/shard_map/cond/branch_1_fun/ppermute | solution.py:348
  62.7 5.5 %collective-permute-start.3 = (bf16[2,96,128]{2,1,0:T(8,128)(2,1)S(1)}, bf16[2,96,128]{2,1,0:T(8,128)(2,1)S(1)}, u32[]{:S(2)}, u32[]{:S(2)}) collective-permute-start(bf16[2,96,128]{2,1,0:T(8,128)(2,1)S(1)} %add_convert_fusion.1), channel_id=1, source_target_pairs={{0,8},{4,12},{8,0},{12,4},{16,24},{20,28},{24,16},{28,20},{1,9},{5... | collective-permute-start | bytes 147464 | tf_op jit(solution)/shard_map/cond/branch_1_fun/ppermute | solution.py:348
  68.2 5.1 %collective-permute-start.4 = (bf16[2,96,128]{2,1,0:T(8,128)(2,1)S(1)}, bf16[2,96,128]{2,1,0:T(8,128)(2,1)S(1)}, u32[]{:S(2)}, u32[]{:S(2)}) collective-permute-start(bf16[2,96,128]{2,1,0:T(8,128)(2,1)S(1)} %add_convert_fusion), channel_id=1, source_target_pairs={{0,16},{4,20},{8,24},{12,28},{16,0},{20,4},{24,8},{28,12},{1,17},{... | collective-permute-start | bytes 147464 | tf_op jit(solution)/shard_map/cond/branch_1_fun/ppermute | solution.py:348
  79.1 2.4 %copy-start.7 = (f32[2,96,3,3]{1,0,3,2:T(2,128)}, f32[2,96,3,3]{1,0,3,2:T(2,128)S(1)}, u32[]{:S(2)}) copy-start(f32[2,96,3,3]{1,0,3,2:T(2,128)S(1)} %get-tuple-element.166) | copy-start | bytes 20740
  79.1 2.4 %copy-start.8 = (f32[2,96,3]{1,0,2:T(2,128)}, f32[2,96,3]{1,0,2:T(2,128)S(1)}, u32[]{:S(2)}) copy-start(f32[2,96,3]{1,0,2:T(2,128)S(1)} %get-tuple-element.168) | copy-start | bytes 6916

commit v5 on v3

--- a/solution.py
+++ b/solution.py
@@ -159,7 +159,7 @@
     over_groups(grad_axial.channels, body)
 
 
-def input_gradient(taps_ref, block, indices, grad_planar, target, slope):
+def input_gradient(taps_ref, block, indices, grad_planar, target, slope, start=None):
     nz, ny = grad_planar.nz, grad_planar.ny
 
     def body(rows):
@@ -169,12 +169,14 @@
                 value = plane_conv(taps, grad_planar, index, z, rows, ny)
                 if slope is not None:
                     value = value * slope.get(index, z, rows)
+                if start is not None:
+                    value = value + start.get(index, z, rows)
                 target.put(index, z, rows, value)
 
     over_groups(grad_planar.channels, body)
 
 
-def tap_sums(block, indices, grad_planar, source, grad_axial, planar, sums_ref):
+def tap_sums(indices, grad_planar, source, grad_axial, planar, sums_ref, before=None):
     nz, ny = source.nz, source.ny
 
     def body(rows):
@@ -201,7 +203,9 @@
             sums[3 * i] = jnp.where(lane != ny - 1, sums[3 * i], 0.0)
             sums[3 * i + 2] = jnp.where(lane != 0, sums[3 * i + 2], 0.0)
         for t in range(12):
-            sums_ref[block, t, rows, :] = sums[t]
+            if before is not None:
+                sums[t] = sums[t] + before[t, rows, :]
+            sums_ref[t, rows, :] = sums[t]
 
     over_groups(source.channels, body)
 
@@ -220,6 +224,16 @@
     return total
 
 
+def sort_sides(odd, first, second, low, high):
+    @pl.when(odd != 0)
+    def _():
+        low[...], high[...] = first[...], second[...]
+
+    @pl.when(odd == 0)
+    def _():
+        low[...], high[...] = second[...], first[...]
+
+
 def inner_kernel(sizes, slab, vol, taps, mix, pl1, ax1, sl1, hid):
     inner = range(1, slab - 1)
     planar, axial, slope, hidden = (Planes(sizes, (ref, inner)) for ref in (pl1, ax1, sl1, hid))
@@ -228,10 +242,11 @@
 
 
 def middle_kernel(
-    sizes, slab, vol, lo1, hi1, cot, taps, mix, mix_t, hid_i,
-    pl1, ax1, sl1, hid, pl2, ax2, gpre2, gax2, gpl2,
+    sizes, slab, odd, vol, first, second, cot, taps, mix, mix_t, hid_i,
+    lo1, hi1, pl1, ax1, sl1, hid, gpl2, sums, mixing, pl2, ax2, gpre2, gax2,
 ):
     inner, edges = range(1, slab - 1), (0, slab - 1)
+    sort_sides(odd[0], first, second, lo1, hi1)
     volume = Planes(sizes, (vol, range(slab)), (lo1, (-1,)), (hi1, (slab,)))
     axial = Planes(sizes, (ax1, edges))
     forward_taps(taps, 0, edges, volume, Planes(sizes, (pl1, edges)), axial)
@@ -240,16 +255,20 @@
     cotangent = Planes(sizes, (cot, range(slab)))
     axial, grad_pre = Planes(sizes, (ax2, inner)), Planes(sizes, (gpre2, inner))
     grad_axial = Planes(sizes, (gax2, inner))
-    forward_taps(taps, 1, inner, hidden, Planes(sizes, (pl2, inner)), axial)
+    planar, grad_planar = Planes(sizes, (pl2, inner)), Planes(sizes, (gpl2, inner))
+    forward_taps(taps, 1, inner, hidden, planar, axial)
     top_gradient(mix, inner, axial, cotangent, grad_pre)
     axial_gradient(mix_t, 1, inner, grad_pre, grad_axial)
-    planar_gradient(taps, 1, inner, grad_axial, Planes(sizes, (gpl2, inner)))
+    planar_gradient(taps, 1, inner, grad_axial, grad_planar)
+    tap_sums(inner, grad_planar, hidden, grad_axial, planar, sums)
+    mixing[...] = mixing_sum(inner, grad_pre, axial)
 
 
 def edge_kernel(
-    sizes, slab, flags, vol, lo1, hi1, lo2, hi2, cot, taps, mix, mix_t, hid_i, hid_e, sl1_e, gpl2_i,
-    pl1, ax1, hid, pl2, ax2, gpre2, gax2, gpl2, gpre1, gax1, gpl1, send_lo, send_hi, sl1,
+    sizes, slab, odd, flags, vol, lo1, hi1, first, second, cot, taps, mix, mix_t, hid_i, hid_e, sl1_e, gpl2_i,
+    lo2, hi2, pl1, ax1, hid, pl2, ax2, gpre2, gax2, gpl2, gpre1, gax1, gpl1_lo, gpl1_hi, to_first, to_second, sl1,
 ):
+    sort_sides(odd[0], first, second, lo2, hi2)
     inner, edges, rims = range(1, slab - 1), (0, slab - 1), (-1, slab)
     outer = (-1, 0, slab - 1, slab)
     masks = {-1: flags[0], slab: flags[1]}
@@ -272,18 +291,15 @@
     grad_pre, grad_axial = Planes(sizes, (gpre1, outer)), Planes(sizes, (gax1, outer))
     input_gradient(taps, 1, outer, grad_planar, grad_pre, slope)
     axial_gradient(mix_t, 0, outer, grad_pre, grad_axial)
-    grad_planar = Planes(sizes, (gpl1, outer))
+    grad_planar = Planes(sizes, (gpl1_lo, outer[:2]), (gpl1_hi, outer[2:]))
     planar_gradient(taps, 0, outer, grad_axial, grad_planar)
-    sent = (-2, -1, slab, slab + 1)
-    input_gradient(
-        taps, 0, sent, grad_planar, Planes(sizes, (send_lo, sent[:2]), (send_hi, sent[2:])), None
-    )
+    sort_sides(odd[0], gpl1_lo, gpl1_hi, to_first, to_second)
 
 
 def weight_kernel(
     sizes, slab, factor, vol, lo1, hi1, lo2, hi2, taps, mix_t,
-    pl1_i, ax1_i, sl1_i, hid_i, pl1_e, ax1_e, hid_e, pl2_i, ax2_i, gpre2_i, gax2_i, gpl2_i,
-    pl1_r, ax1_r, hid_r, pl2_e, ax2_e, gpre2_e, gax2_e, gpl2_e, gpre1_o, gax1_o, gpl1_o,
+    pl1_i, ax1_i, sl1_i, hid_i, pl1_e, ax1_e, hid_e, gpl2_i, sums_i, mixing_i,
+    pl1_r, ax1_r, hid_r, pl2_e, ax2_e, gpre2_e, gax2_e, gpl2_e, gpre1_o, gax1_o, gpl1_lo, gpl1_hi,
     gpl1, payload, gpre1, gax1, sums,
 ):
     inner, edges, rims = range(1, slab - 1), (0, slab - 1), (-1, slab)
@@ -292,7 +308,7 @@
     grad_planar2 = Planes(sizes, (gpl2_i, inner), (gpl2_e, edges))
     grad_pre1 = Planes(sizes, (gpre1, inner), (gpre1_o, outer))
     grad_axial1 = Planes(sizes, (gax1, inner), (gax1_o, outer))
-    grad_planar1 = Planes(sizes, (gpl1, inner), (gpl1_o, outer))
+    grad_planar1 = Planes(sizes, (gpl1, inner), (gpl1_lo, outer[:2]), (gpl1_hi, outer[2:]))
     input_gradient(taps, 1, inner, grad_planar2, grad_pre1, Planes(sizes, (sl1_i, inner)))
     axial_gradient(mix_t, 0, inner, grad_pre1, grad_axial1)
     planar_gradient(taps, 0, inner, grad_axial1, grad_planar1)
@@ -302,30 +318,55 @@
     hidden = Planes(sizes, (hid_i, inner), (hid_e, edges), (hid_r, rims))
     planar1 = Planes(sizes, (pl1_i, inner), (pl1_e, edges), (pl1_r, rims))
     axial1 = Planes(sizes, (ax1_i, inner), (ax1_e, edges), (ax1_r, rims))
-    planar2 = Planes(sizes, (pl2_i, inner), (pl2_e, edges))
-    axial2 = Planes(sizes, (ax2_i, inner), (ax2_e, edges))
-    grad_pre2 = Planes(sizes, (gpre2_i, inner), (gpre2_e, edges))
-    grad_axial2 = Planes(sizes, (gax2_i, inner), (gax2_e, edges))
-    tap_sums(0, wide, grad_planar1, volume, grad_axial1, planar1, sums)
-    tap_sums(1, own, grad_planar2, hidden, grad_axial2, planar2, sums)
-    mixing = (mixing_sum(wide, grad_pre1, axial1), mixing_sum(own, grad_pre2, axial2))
-    lane = lax.broadcasted_iota(jnp.int32, (channels, payload.shape[2]), 1)
+    planar2, axial2 = Planes(sizes, (pl2_e, edges)), Planes(sizes, (ax2_e, edges))
+    grad_pre2, grad_axial2 = Planes(sizes, (gpre2_e, edges)), Planes(sizes, (gax2_e, edges))
+    tap_sums(wide, grad_planar1, volume, grad_axial1, planar1, sums.at[0])
+    tap_sums(edges, grad_planar2, hidden, grad_axial2, planar2, sums.at[1], sums_i)
+    mixing = (
+        mixing_sum(wide, grad_pre1, axial1),
+        mixing_sum(edges, grad_pre2, axial2) + mixing_i[...],
+    )
+    lane = lax.broadcasted_iota(jnp.int32, (channels, payload.shape[1]), 1)
     for block in range(2):
-        packed = jnp.zeros(payload.shape[1:], F32)
+        at = block * channels
+        payload[at : at + channels, :channels] = (mixing[block] * factor).astype(BF16)
+        packed = jnp.zeros((channels, payload.shape[1]), F32)
         for t in range(12):
             total = jnp.sum(sums[block, t], axis=1, keepdims=True)
-            packed = packed + jnp.where(lane == channels + t, total, 0.0)
-        payload[block] = packed * factor
-        payload[block, :, :channels] = mixing[block] * factor
-
-
-def volume_kernel(sizes, slab, taps, gpl1_i, gpl1_o, out):
+            packed = jnp.where(lane == t, total, packed)
+        turned = (packed * factor).T
+        at = 2 * channels + GROUP * block
+        payload[at : at + GROUP, :channels] = turned[:GROUP].astype(BF16)
+
+
+def volume_kernel(sizes, slab, taps, gpl1_i, gpl1_lo, gpl1_hi, out):
     inner, outer = range(1, slab - 1), (-1, 0, slab - 1, slab)
-    grad_planar = Planes(sizes, (gpl1_i, inner), (gpl1_o, outer))
+    grad_planar = Planes(sizes, (gpl1_i, inner), (gpl1_lo, outer[:2]), (gpl1_hi, outer[2:]))
     input_gradient(taps, 0, range(slab), grad_planar, Planes(sizes, (out, range(slab))), None)
 
 
-def call(kernel, name, operands, outputs, scratch=(), flops=0, scalars=0):
+def final_kernel(sizes, slab, odd, taps, own, first, second, out, from_lo, from_hi):
+    sort_sides(odd[0], first, second, from_lo, from_hi)
+    outer = (-1, 0, slab - 1, slab)
+    arrived = Planes(sizes, (from_lo, outer[:2]), (from_hi, outer[2:]))
+    start, result = Planes(sizes, (own, range(slab))), Planes(sizes, (out, range(slab)))
+    input_gradient(taps, 0, range(slab), arrived, result, None, start)
+
+
+def result_kernel(channels, mine, other, mixing, plane_taps, depth_taps):
+    for block in range(2):
+        rows = pl.ds(block * channels, channels)
+        total = mine[rows, :].astype(F32) + other[rows, :].astype(F32)
+        mixing[block] = total[:, :channels]
+        rows = pl.ds(2 * channels + GROUP * block, GROUP)
+        total = mine[rows, :].astype(F32) + other[rows, :].astype(F32)
+        for t in range(9):
+            plane_taps[t, block : block + 1, :] = total[t : t + 1, :channels]
+        for t in range(3):
+            depth_taps[t, block : block + 1, :] = total[9 + t : 10 + t, :channels]
+
+
+def call(kernel, name, operands, outputs, scratch=(), cost=1, scalars=0):
     vmem = pl.BlockSpec(memory_space=pltpu.VMEM)
     smem = pl.BlockSpec(memory_space=pltpu.SMEM)
     return pl.pallas_call(
@@ -335,20 +376,24 @@
         in_specs=[smem] * scalars + [vmem] * (len(operands) - scalars),
         out_specs=[vmem] * len(outputs),
         scratch_shapes=scratch,
-        compiler_params=pltpu.CompilerParams(vmem_limit_bytes=32 << 20),
-        cost_estimate=pl.CostEstimate(flops=flops, bytes_accessed=1 << 20, transcendentals=0),
+        compiler_params=pltpu.CompilerParams(vmem_limit_bytes=16 << 20),
+        cost_estimate=pl.CostEstimate(flops=0, bytes_accessed=cost, transcendentals=0),
     )(*operands)
 
 
-def all_sum(total):
+def all_sum(mine, arrivals):
+    arrived, spot, other = [], 0, None
     for axis in ("dp", "sp"):
         count, step = lax.axis_size(axis), 1
         while step < count:
-            mine = total.astype(BF16)
+            if other is not None:
+                mine = (mine.astype(F32) + other.astype(F32)).astype(BF16)
+            if spot in arrivals:
+                mine, value = lax.optimization_barrier((mine, arrivals[spot]))
+                arrived.append(value)
             other = lax.ppermute(mine, axis, [(i, i ^ step) for i in range(count)])
-            total = mine.astype(F32) + other.astype(F32)
-            step *= 2
-    return total
+            step, spot = step * 2, spot + 1
+    return mine, other, arrived
 
 
 def on_device(volume, cotangent, kernels_xy, kernels_z, mixing):
@@ -356,20 +401,28 @@
     plane = nz * ny
     sizes = (channels, nz, ny)
     ranks, place = lax.axis_size("sp"), lax.axis_index("sp")
-    up = [(i, i + 1) for i in range(ranks - 1)]
-    down = [(j, i) for i, j in up]
-
-    def flat(planes):
-        return planes.reshape(channels, -1)
-
-    lo1 = lax.ppermute(flat(volume[0, :, slab - 1]), "sp", up)
-    hi1 = lax.ppermute(flat(volume[0, :, 0]), "sp", down)
-    lo2 = lax.ppermute(flat(volume[0, :, slab - 2]), "sp", up)
-    hi2 = lax.ppermute(flat(volume[0, :, 1]), "sp", down)
-    vol, cot = flat(volume[0]), flat(cotangent[0])
+    odd = place % 2
+    firsts = [(i, i ^ 1) for i in range(ranks)]
+    seconds = [(i, i + 1) for i in range(1, ranks - 1, 2)] + [(i + 1, i) for i in range(1, ranks - 1, 2)]
+
+    def rims(slab_planes, low, high):
+        low = slab_planes[:, low * plane : (low + 1) * plane]
+        high = slab_planes[:, high * plane : (high + 1) * plane]
+        return jnp.where(odd != 0, low, high), jnp.where(odd != 0, high, low)
+
+    def exchange(sent):
+        return lax.ppermute(sent[0], "sp", firsts), lax.ppermute(sent[1], "sp", seconds)
+
+    vol = lax.optimization_barrier(volume[0].reshape(channels, -1))
+    near = rims(vol, 0, slab - 1)
+    later, *near = lax.optimization_barrier((vol, *near))
+    near = exchange(near)
+    far = exchange(rims(later, 1, slab - 2))
+    cot = cotangent[0].reshape(channels, -1)
     taps = wide_taps(kernels_xy, kernels_z, ny)
     mix, mix_t = mixing, jnp.swapaxes(mixing, 1, 2)
     flags = jnp.stack([place > 0, place < ranks - 1]).astype(F32)
+    odd = odd.reshape(1)
 
     def planes(count):
         return jax.ShapeDtypeStruct((channels, count * plane), BF16)
@@ -377,52 +430,77 @@
     def scratch(count):
         return pltpu.VMEM((channels, count * plane), BF16)
 
+    def sums(*shape):
+        return jax.ShapeDtypeStruct(shape, F32)
+
     inside = slab - 2
     pl1_i, ax1_i, sl1_i, hid_i = call(
-        functools.partial(inner_kernel, sizes, slab), "inner", (vol, taps, mix), [planes(inside)] * 4
-    )
-    pl1_e, ax1_e, sl1_e, hid_e, pl2_i, ax2_i, gpre2_i, gax2_i, gpl2_i = call(
+        functools.partial(inner_kernel, sizes, slab),
+        "inner",
+        (vol, taps, mix),
+        [planes(inside)] * 4,
+        cost=4 << 20,
+    )
+    lo1, hi1, pl1_e, ax1_e, sl1_e, hid_e, gpl2_i, sums_i, mixing_i = call(
         functools.partial(middle_kernel, sizes, slab),
         "middle",
-        (vol, lo1, hi1, cot, taps, mix, mix_t, hid_i),
-        [planes(2)] * 4 + [planes(inside)] * 5,
-    )
-    pl1_r, ax1_r, hid_r, pl2_e, ax2_e, gpre2_e, gax2_e, gpl2_e, gpre1_o, gax1_o, gpl1_o, send_lo, send_hi = call(
+        (odd, vol, *near, cot, taps, mix, mix_t, hid_i),
+        [planes(1)] * 2 + [planes(2)] * 4 + [planes(inside), sums(12, channels, ny), sums(channels, channels)],
+        scratch=[scratch(inside)] * 4,
+        scalars=1,
+        cost=12 << 20,
+    )
+    (
+        lo2, hi2, pl1_r, ax1_r, hid_r, pl2_e, ax2_e, gpre2_e, gax2_e, gpl2_e,
+        gpre1_o, gax1_o, gpl1_lo, gpl1_hi, to_first, to_second,
+    ) = call(
         functools.partial(edge_kernel, sizes, slab),
         "edge",
-        (flags, vol, lo1, hi1, lo2, hi2, cot, taps, mix, mix_t, hid_i, hid_e, sl1_e, gpl2_i),
-        [planes(2)] * 8 + [planes(4)] * 3 + [planes(2)] * 2,
+        (odd, flags, vol, lo1, hi1, *far, cot, taps, mix, mix_t, hid_i, hid_e, sl1_e, gpl2_i),
+        [planes(1)] * 2 + [planes(2)] * 8 + [planes(4)] * 2 + [planes(2)] * 4,
         scratch=[scratch(2)],
-        scalars=1,
-    )
-    from_lo = lax.ppermute(send_hi, "sp", up)
-    from_hi = lax.ppermute(send_lo, "sp", down)
+        scalars=2,
+        cost=18 << 20,
+    )
+    arrived = exchange((to_first, to_second))
     count = lax.axis_size("dp") * slab * ranks * nz * ny
     gpl1_i, payload = call(
         functools.partial(weight_kernel, sizes, slab, 1.0 / math.sqrt(count)),
         "weights",
         (
             vol, lo1, hi1, lo2, hi2, taps, mix_t,
-            pl1_i, ax1_i, sl1_i, hid_i, pl1_e, ax1_e, hid_e, pl2_i, ax2_i, gpre2_i, gax2_i, gpl2_i,
-            pl1_r, ax1_r, hid_r, pl2_e, ax2_e, gpre2_e, gax2_e, gpl2_e, gpre1_o, gax1_o, gpl1_o,
+            pl1_i, ax1_i, sl1_i, hid_i, pl1_e, ax1_e, hid_e, gpl2_i, sums_i, mixing_i,
+            pl1_r, ax1_r, hid_r, pl2_e, ax2_e, gpre2_e, gax2_e, gpl2_e, gpre1_o, gax1_o, gpl1_lo, gpl1_hi,
         ),
-        [planes(inside), jax.ShapeDtypeStruct((2, channels, 128), F32)],
+        [planes(inside), jax.ShapeDtypeStruct((2 * channels + 2 * GROUP, 128), BF16)],
         scratch=[scratch(inside), scratch(inside), pltpu.VMEM((2, 12, channels, ny), F32)],
     )
-    total = all_sum(payload)
+    mine, other, arrived = all_sum(payload, {1: arrived[0], 4: arrived[1]})
     (own,) = call(
-        functools.partial(volume_kernel, sizes, slab), "volume", (taps, gpl1_i, gpl1_o), [planes(slab)]
-    )
-    parts = own.astype(F32).reshape(channels, slab, nz, ny)
-    from_lo = from_lo.astype(F32).reshape(channels, 2, nz, ny)
-    from_hi = from_hi.astype(F32).reshape(channels, 2, nz, ny)
-    parts = parts + jnp.pad(from_lo, ((0, 0), (0, slab - 2), (0, 0), (0, 0)))
-    parts = parts + jnp.pad(from_hi, ((0, 0), (slab - 2, 0), (0, 0), (0, 0)))
+        functools.partial(volume_kernel, sizes, slab),
+        "volume",
+        (taps, gpl1_i, gpl1_lo, gpl1_hi),
+        [planes(slab)],
+    )
+    (grad,) = call(
+        functools.partial(final_kernel, sizes, slab),
+        "final",
+        (odd, taps, own, *arrived),
+        [planes(slab)],
+        scratch=[scratch(2)] * 2,
+        scalars=1,
+    )
+    mixing_grad, plane_grad, depth_grad = call(
+        functools.partial(result_kernel, channels),
+        "result",
+        (mine, other),
+        [sums(2, channels, channels), sums(9, 2, channels), sums(3, 2, channels)],
+    )
     return (
-        parts.astype(BF16)[None],
-        total[:, :, :channels],
-        total[:, :, channels : channels + 9].reshape(2, channels, 3, 3),
-        total[:, :, channels + 9 : channels + 12],
+        grad.reshape(1, channels, slab, nz, ny),
+        mixing_grad,
+        jnp.transpose(plane_grad.reshape(3, 3, 2, channels), (2, 3, 0, 1)),
+        jnp.transpose(depth_grad, (1, 2, 0)),
     )
 
 

time: 72 us -> 67.7 us (0.940)
  local copies, waits for them, and re-layouts: 7.41 us -> 3.11 us
  Pallas kernels: 16.9 us -> 18 us
  starting transfers between devices: 27 us -> 26 us
    unnamed x21 -> x10, local copies, waits for them, and re-layouts: 4.36 us -> 1.16 us
    ppermute x6, starting transfers between devices: 15.9 us -> 13.1 us  [the longest x3 11 us: exchange(): lax.ppermute(sent[0], 'sp', firsts)]
    slice x4 -> x0, local copies, waits for them, and re-layouts: 2.2 us -> none  [the longest x1 1.35 us: on_device(): hi2 = lax.ppermute(flat(volume[0, :, 1]), 'sp', down)]
    ppermute x5, starting transfers between devices: 11.1 us -> 12.8 us  [all_sum(): other = lax.ppermute(mine, axis, [(i, i ^ step) for i in range(count)])]
    select_n x0 -> x2, other arithmetic: none -> 1.47 us  [rims(): return (jnp.where(odd != 0, low, high), jnp.where(odd != 0, high, low))]
    ppermute x5, waiting for transfers between devices: 13.8 us -> 12.5 us  [all_sum(): other = lax.ppermute(mine, axis, [(i, i ^ step) for i in range(count)])]
    ppermute x6, waiting for transfers between devices: 3.47 us -> 4.61 us  [the longest x3 4.6 us: exchange(): lax.ppermute(sent[0], 'sp', firsts)]
    broadcast_in_dim x1 -> x0, other arithmetic: 1.12 us -> none  [on_device(): parts.astype(BF16)[None]]
  transfers between devices with their start and end apart: 11 -> 11, of which waited for: 5 -> 6; matrix products, arithmetic and copies ran while one was open for 10% -> 5% of each run, Pallas kernels for 7% -> 18%
where the time goes in v5:
time: 67.7 us; the launch traced here: 67.4 us
  starting transfers between devices  26 us (38%)
  Pallas kernels  18 us (27%)
  waiting for transfers between devices  17.2 us (25%)
  local copies, waits for them, and re-layouts  3.11 us (5%)
  other arithmetic  2.34 us (3%)
  between operations  0.9 us (1%)
    pallas_call x7, Pallas kernels, call(): pl.pallas_call(kernel, name=name, out_shape=outputs, in_specs=[smem] * sc...  18 us
    ppermute x5, starting transfers between devices, all_sum(): other = lax.ppermute(mine, axis, [(i, i ^ step) for i in range(count)])  12.8 us
    ppermute x5, waiting for transfers between devices, all_sum(): other = lax.ppermute(mine, axis, [(i, i ^ step) for i in range(count)])  12.5 us
    ppermute x3, starting transfers between devices, exchange(): lax.ppermute(sent[0], 'sp', firsts)  11 us
    ppermute x3, waiting for transfers between devices, exchange(): lax.ppermute(sent[0], 'sp', firsts)  4.6 us
    ppermute x3, starting transfers between devices, exchange(): lax.ppermute(sent[1], 'sp', seconds)  2.13 us
    select_n x2, other arithmetic, rims(): return (jnp.where(odd != 0, low, high), jnp.where(odd != 0, high, low))  1.47 us
    another operation x1, local copies, waits for them, and re-layouts, on_device(): vol = lax.optimization_barrier(volume[0].reshape(channels, -1))  1.43 us
  transfers between devices with their start and end apart: 11, of which 6 were waited for; matrix products, arithmetic and copies ran while one was open for 5% of the time, Pallas kernels for 18%

profile of v5, /device:TPU:0, one launch (start us, length us, event | category | flops | bytes accessed | tf_op | source)
XLA Modules:
  0.0 67.4 jit_solution(8280156666349927620)
XLA Ops:
  0.6 1.4 %reshape_squeeze.6.vol = bf16[96,4096]{1,0:T(8,128)(2,1)S(1)} reshape(bf16[1,96,4,8,128]{4,3,2,1,0:T(8,128)(2,1)} %param.5) | data formatting | bytes 1572864 | tf_op jit(solution)/shard_map/reshape;squeeze | solution.py:416
  2.1 0.8 %broadcast_select_fusion.3 = (bf16[96,1024]{1,0:T(8,128)(2,1)}, bf16[96,1024]{1,0:T(8,128)(2,1)}) fusion(pred[]{:T(512)S(6)} %ne.41, bf16[96,4096]{1,0:T(8,128)(2,1)S(1)} %reshape_squeeze.6.vol), kind=kLoop, calls=%fused_computation.4 | loop fusion | flops 196608 | bytes 786433 | tf_op jit(solution)/shard_map/jit(_where)/select_n | solution.py:411
  2.9 3.0 %collective-permute-start = (bf16[96,1024]{1,0:T(8,128)(2,1)}, bf16[96,1024]{1,0:T(8,128)(2,1)S(1)}, u32[]{:S(2)}, u32[]{:S(2)}) collective-permute-start(bf16[96,1024]{1,0:T(8,128)(2,1)} %get-tuple-element.45), channel_id=1, source_target_pairs={{0,4},{4,0},{8,12},{12,8},{16,20},{20,16},{24,28},{28,24},{1,5},{5... | collective-permute-start | bytes 589832 | tf_op jit(solution)/shard_map/ppermute | solution.py:414
  6.5 0.7 %broadcast_select_fusion.1 = (bf16[96,1024]{1,0:T(8,128)(2,1)}, bf16[96,1024]{1,0:T(8,128)(2,1)S(1)}) fusion(pred[]{:T(512)S(6)} %ne.41, bf16[96,4096]{1,0:T(8,128)(2,1)S(1)} %reshape_squeeze.6.vol), kind=kLoop, calls=%fused_computation.2 | loop fusion | flops 196608 | bytes 786433 | tf_op jit(solution)/shard_map/jit(_where)/select_n | solution.py:411
  7.2 0.8 %collective-permute-start.3 = (bf16[96,1024]{1,0:T(8,128)(2,1)}, bf16[96,1024]{1,0:T(8,128)(2,1)S(1)}, u32[]{:S(2)}, u32[]{:S(2)}) collective-permute-start(bf16[96,1024]{1,0:T(8,128)(2,1)} %get-tuple-element.86), channel_id=1, source_target_pairs={{4,8},{12,16},{20,24},{8,4},{16,12},{24,20},{5,9},{13,17},{21,25},... | collective-permute-start | bytes 589832 | tf_op jit(solution)/shard_map/ppermute | solution.py:414
  8.0 5.6 %collective-permute-start.2 = (bf16[96,1024]{1,0:T(8,128)(2,1)S(1)}, bf16[96,1024]{1,0:T(8,128)(2,1)S(1)}, u32[]{:S(2)}, u32[]{:S(2)}) collective-permute-start(bf16[96,1024]{1,0:T(8,128)(2,1)S(1)} %get-tuple-element.87), channel_id=1, source_target_pairs={{0,4},{4,0},{8,12},{12,8},{16,20},{20,16},{24,28},{28,24},{1,5},{5... | collective-permute-start | bytes 589832 | tf_op jit(solution)/shard_map/ppermute | solution.py:414
  15.1 1.1 %inner.1 = (bf16[96,2048]{1,0:T(8,128)(2,1)S(1)}, bf16[96,2048]{1,0:T(8,128)(2,1)S(1)}, bf16[96,2048]{1,0:T(8,128)(2,1)S(1)}, bf16[96,2048]{1,0:T(8,128)(2,1)S(1)}) custom-call(bf16[96,4096]{1,0:T(8,128)(2,1)S(1)} %reshape_squeeze.6.vol, bf16[2,21,96,128]{3,2,1,0:T(8,128)(2,1)S(1)} %pad_maximum_fusion.taps, bf16[2,96,96]{2,1,0:T(8,128)(2,1)S(1)} %copy-done), custom_call_target="tpu_custom_call" | custom-call | bytes 4194304 | tf_op jit(solution)/shard_map/inner/pallas_call | solution.py:372
  16.3 3.6 %collective-permute-done.first = bf16[96,1024]{1,0:T(8,128)(2,1)S(1)} collective-permute-done((bf16[96,1024]{1,0:T(8,128)(2,1)}, bf16[96,1024]{1,0:T(8,128)(2,1)S(1)}, u32[]{:S(2)}, u32[]{:S(2)}) %collective-permute-start) | collective-permute-done | bytes 196640 | tf_op jit(solution)/shard_map/ppermute | solution.py:414
  19.9 3.8 %middle.1 = (bf16[96,1024]{1,0:T(8,128)(2,1)S(1)}, bf16[96,1024]{1,0:T(8,128)(2,1)S(1)}, bf16[96,2048]{1,0:T(8,128)(2,1)S(1)}, bf16[96,2048]{1,0:T(8,128)(2,1)S(...) custom-call(s32[1]{0:T(128)} %bitcast.odd, ...), custom_call_target="tpu_custom_call" | custom-call | bytes 12582912 | tf_op jit(solution)/shard_map/middle/pallas_call | solution.py:372
  23.7 5.1 %edge.1 = (bf16[96,1024]{1,0:T(8,128)(2,1)S(1)}, bf16[96,1024]{1,0:T(8,128)(2,1)S(1)}, bf16[96,2048]{1,0:T(8,128)(2,1)S(1)}, bf16[96,2048]{1,0:T(8,128)(2,1)S(1)...) custom-call(s32[1]{0:T(128)} %bitcast.odd, ...), custom_call_target="tpu_custom_call" | custom-call | bytes 18874368 | tf_op jit(solution)/shard_map/edge/pallas_call | solution.py:372
  28.9 2.5 %collective-permute-start.5 = (bf16[96,2048]{1,0:T(8,128)(2,1)S(1)}, bf16[96,2048]{1,0:T(8,128)(2,1)S(1)}, u32[]{:S(2)}, u32[]{:S(2)}) collective-permute-start(bf16[96,2048]{1,0:T(8,128)(2,1)S(1)} %get-tuple-element.77), channel_id=1, source_target_pairs={{0,4},{4,0},{8,12},{12,8},{16,20},{20,16},{24,28},{28,24},{1,5},{5... | collective-permute-start | bytes 1179656 | tf_op jit(solution)/shard_map/ppermute | solution.py:414
  31.3 5.0 %weights.1 = (bf16[96,2048]{1,0:T(8,128)(2,1)S(1)}, bf16[224,128]{1,0:T(8,128)(2,1)S(1)}) custom-call(bf16[96,4096]{1,0:T(8,128)(2,1)S(1)} %reshape_squeeze.6.vol, bf16[96,1024]{1,0:T(8,128)(2,1)S(1)} %get-tuple-element.48.lo1, bf16[96,1024]{1,0:T(8,128)(2,1)S(1)} %get-tuple-element.49.hi1, bf16[96,1024]{1,0:T(8,128)(2,1)S(1)} %get-tuple-element.54.lo2, ...), custom_call_target="tpu_custom_call" | custom-call | bytes 1 | tf_op jit(solution)/shard_map/weights/pallas_call | solution.py:372
  36.5 1.2 %collective-permute-done.4 = bf16[224,128]{1,0:T(8,128)(2,1)S(1)} collective-permute-done((bf16[224,128]{1,0:T(8,128)(2,1)S(1)}, bf16[224,128]{1,0:T(8,128)(2,1)S(1)}, u32[]{:S(2)}, u32[]{:S(2)}) %collective-permute-start.4) | collective-permute-done | bytes 57376 | tf_op jit(solution)/shard_map/ppermute | solution.py:394
  37.7 1.0 %collective-permute-done.5.first = bf16[96,2048]{1,0:T(8,128)(2,1)S(1)} collective-permute-done((bf16[96,2048]{1,0:T(8,128)(2,1)S(1)}, bf16[96,2048]{1,0:T(8,128)(2,1)S(1)}, u32[]{:S(2)}, u32[]{:S(2)}) %collective-permute-start.5) | collective-permute-done | bytes 393248 | tf_op jit(solution)/shard_map/ppermute | solution.py:414
  38.7 1.6 %collective-permute-start.6 = (bf16[224,128]{1,0:T(8,128)(2,1)S(1)}, bf16[224,128]{1,0:T(8,128)(2,1)S(1)}, u32[]{:S(2)}, u32[]{:S(2)}) collective-permute-start(bf16[224,128]{1,0:T(8,128)(2,1)S(1)} %add_convert_fusion.3), channel_id=1, source_target_pairs={{0,2},{1,3},{2,0},{3,1},{4,6},{5,7},{6,4},{7,5},{8,10},{9,11},{10,... | collective-permute-start | bytes 172040 | tf_op jit(solution)/shard_map/ppermute | solution.py:394
  40.3 2.6 %collective-permute-done.6 = bf16[224,128]{1,0:T(8,128)(2,1)S(1)} collective-permute-done((bf16[224,128]{1,0:T(8,128)(2,1)S(1)}, bf16[224,128]{1,0:T(8,128)(2,1)S(1)}, u32[]{:S(2)}, u32[]{:S(2)}) %collective-permute-start.6) | collective-permute-done | bytes 57376 | tf_op jit(solution)/shard_map/ppermute | solution.py:394
  42.9 1.8 %collective-permute-start.7 = (bf16[224,128]{1,0:T(8,128)(2,1)S(1)}, bf16[224,128]{1,0:T(8,128)(2,1)S(1)}, u32[]{:S(2)}, u32[]{:S(2)}) collective-permute-start(bf16[224,128]{1,0:T(8,128)(2,1)S(1)} %add_convert_fusion.2), channel_id=1, source_target_pairs={{0,4},{4,0},{8,12},{12,8},{16,20},{20,16},{24,28},{28,24},{1,5},{5... | collective-permute-start | bytes 172040 | tf_op jit(solution)/shard_map/ppermute | solution.py:394
  45.4 6.6 %collective-permute-done.7 = bf16[224,128]{1,0:T(8,128)(2,1)S(1)} collective-permute-done((bf16[224,128]{1,0:T(8,128)(2,1)S(1)}, bf16[224,128]{1,0:T(8,128)(2,1)S(1)}, u32[]{:S(2)}, u32[]{:S(2)}) %collective-permute-start.7) | collective-permute-done | bytes 57376 | tf_op jit(solution)/shard_map/ppermute | solution.py:394
  52.0 3.2 %collective-permute-start.8 = (bf16[224,128]{1,0:T(8,128)(2,1)S(1)}, bf16[224,128]{1,0:T(8,128)(2,1)S(1)}, u32[]{:S(2)}, u32[]{:S(2)}) collective-permute-start(bf16[224,128]{1,0:T(8,128)(2,1)S(1)} %add_convert_fusion.1), channel_id=1, source_target_pairs={{0,8},{4,12},{8,0},{12,4},{16,24},{20,28},{24,16},{28,20},{1,9},{5... | collective-permute-start | bytes 172040 | tf_op jit(solution)/shard_map/ppermute | solution.py:394
  55.2 2.2 %collective-permute-done.8 = bf16[224,128]{1,0:T(8,128)(2,1)S(1)} collective-permute-done((bf16[224,128]{1,0:T(8,128)(2,1)S(1)}, bf16[224,128]{1,0:T(8,128)(2,1)S(1)}, u32[]{:S(2)}, u32[]{:S(2)}) %collective-permute-start.8) | collective-permute-done | bytes 57376 | tf_op jit(solution)/shard_map/ppermute | solution.py:394
  57.4 6.2 %collective-permute-start.10 = (bf16[224,128]{1,0:T(8,128)(2,1)S(1)}, bf16[224,128]{1,0:T(8,128)(2,1)S(1)}, u32[]{:S(2)}, u32[]{:S(2)}) collective-permute-start(bf16[224,128]{1,0:T(8,128)(2,1)S(1)} %add_convert_fusion.mine), channel_id=1, source_target_pairs={{0,16},{4,20},{8,24},{12,28},{16,0},{20,4},{24,8},{28,12},{1,17},{... | collective-permute-start | bytes 172040 | tf_op jit(solution)/shard_map/ppermute | solution.py:394
  63.6 1.1 %volume.1.own = bf16[96,4096]{1,0:T(8,128)(2,1)S(1)} custom-call(bf16[2,21,96,128]{3,2,1,0:T(8,128)(2,1)S(1)} %pad_maximum_fusion.taps, bf16[96,2048]{1,0:T(8,128)(2,1)S(1)} %get-tuple-element.75.gpl1_i, bf16[96,2048]{1,0:T(8,128)(2,1)S(1)} %get-tuple-element.73.gpl1_lo, bf16[96,2048]{1,0:T(8,128)(2,1)S(1)} %get-tuple-element.74.gpl1_hi), custom_call_target="tpu_custom_call" | custom-call | bytes 1 | tf_op jit(solution)/shard_map/volume/pallas_call | solution.py:372
  64.7 1.0 %final.1 = bf16[96,4096]{1,0:T(8,128)(2,1)S(1)} custom-call(s32[1]{0:T(128)} %bitcast.odd, bf16[2,21,96,128]{3,2,1,0:T(8,128)(2,1)S(1)} %pad_maximum_fusion.taps, bf16[96,4096]{1,0:T(8,128)(2,1)S(1)} %volume.1.own, bf16[96,2048]{1,0:T(8,128)(2,1)S(1)} %collective-permute-done.5.first, bf16[96,2048]{1,0:T(8,128)(2,1)S(1)} %collective-permute-done.9.second), custom_call_target="tpu_custom_call" | custom-call | bytes 1 | tf_op jit(solution)/shard_map/final/pallas_call | solution.py:372
  65.7 1.0 %copy.12 = bf16[12,8,32,128]{3,2,1,0:T(8,128)(2,1)} copy(bf16[12,8,32,128]{3,1,2,0:T(8,128)(2,1)S(1)} %bitcast.18) | data formatting | bytes 1572864
  (36 shorter events, 3.6 us)
Async XLA Ops:
  2.1 11.9 %copy-start.1 = (bf16[1,96,4,8,128]{4,3,2,1,0:T(8,128)(2,1)S(1)}, bf16[1,96,4,8,128]{4,3,2,1,0:T(8,128)(2,1)}, u32[]{:S(2)}) copy-start(bf16[1,96,4,8,128]{4,3,2,1,0:T(8,128)(2,1)} %param.6) | copy-start | bytes 2359300
  2.9 17.0 %collective-permute-start = (bf16[96,1024]{1,0:T(8,128)(2,1)}, bf16[96,1024]{1,0:T(8,128)(2,1)S(1)}, u32[]{:S(2)}, u32[]{:S(2)}) collective-permute-start(bf16[96,1024]{1,0:T(8,128)(2,1)} %get-tuple-element.45), channel_id=1, source_target_pairs={{0,4},{4,0},{8,12},{12,8},{16,20},{20,16},{24,28},{28,24},{1,5},{5... | collective-permute-start | bytes 589832 | tf_op jit(solution)/shard_map/ppermute | solution.py:414
  5.8 14.1 %collective-permute-start.1 = (bf16[96,1024]{1,0:T(8,128)(2,1)}, bf16[96,1024]{1,0:T(8,128)(2,1)S(1)}, u32[]{:S(2)}, u32[]{:S(2)}) collective-permute-start(bf16[96,1024]{1,0:T(8,128)(2,1)} %get-tuple-element.46), channel_id=1, source_target_pairs={{4,8},{12,16},{20,24},{8,4},{16,12},{24,20},{5,9},{13,17},{21,25},... | collective-permute-start | bytes 589832 | tf_op jit(solution)/shard_map/ppermute | solution.py:414
  6.5 7.1 %copy-start.3 = (bf16[2,96,3]{1,0,2:T(2,128)(2,1)S(1)}, bf16[2,96,3]{1,0,2:T(2,128)(2,1)}, u32[]{:S(2)}) copy-start(bf16[2,96,3]{1,0,2:T(2,128)(2,1)} %param.8) | copy-start | bytes 3460
  6.5 7.3 %copy-start.2 = (bf16[2,96,3,3]{1,0,3,2:T(2,128)(2,1)S(1)}, bf16[2,96,3,3]{1,0,3,2:T(2,128)(2,1)}, u32[]{:S(2)}) copy-start(bf16[2,96,3,3]{1,0,3,2:T(2,128)(2,1)} %param.7) | copy-start | bytes 10372
  7.2 6.6 %copy-start = (bf16[2,96,96]{2,1,0:T(8,128)(2,1)S(1)}, bf16[2,96,96]{2,1,0:T(8,128)(2,1)}, u32[]{:S(2)}) copy-start(bf16[2,96,96]{2,1,0:T(8,128)(2,1)} %mix.5) | copy-start | bytes 110596
  7.2 16.5 %collective-permute-start.3 = (bf16[96,1024]{1,0:T(8,128)(2,1)}, bf16[96,1024]{1,0:T(8,128)(2,1)S(1)}, u32[]{:S(2)}, u32[]{:S(2)}) collective-permute-start(bf16[96,1024]{1,0:T(8,128)(2,1)} %get-tuple-element.86), channel_id=1, source_target_pairs={{4,8},{12,16},{20,24},{8,4},{16,12},{24,20},{5,9},{13,17},{21,25},... | collective-permute-start | bytes 589832 | tf_op jit(solution)/shard_map/ppermute | solution.py:414
  8.0 15.7 %collective-permute-start.2 = (bf16[96,1024]{1,0:T(8,128)(2,1)S(1)}, bf16[96,1024]{1,0:T(8,128)(2,1)S(1)}, u32[]{:S(2)}, u32[]{:S(2)}) collective-permute-start(bf16[96,1024]{1,0:T(8,128)(2,1)S(1)} %get-tuple-element.87), channel_id=1, source_target_pairs={{0,4},{4,0},{8,12},{12,8},{16,20},{20,16},{24,28},{28,24},{1,5},{5... | collective-permute-start | bytes 589832 | tf_op jit(solution)/shard_map/ppermute | solution.py:414
  28.9 9.8 %collective-permute-start.5 = (bf16[96,2048]{1,0:T(8,128)(2,1)S(1)}, bf16[96,2048]{1,0:T(8,128)(2,1)S(1)}, u32[]{:S(2)}, u32[]{:S(2)}) collective-permute-start(bf16[96,2048]{1,0:T(8,128)(2,1)S(1)} %get-tuple-element.77), channel_id=1, source_target_pairs={{0,4},{4,0},{8,12},{12,8},{16,20},{20,16},{24,28},{28,24},{1,5},{5... | collective-permute-start | bytes 1179656 | tf_op jit(solution)/shard_map/ppermute | solution.py:414
  36.4 1.3 %collective-permute-start.4 = (bf16[224,128]{1,0:T(8,128)(2,1)S(1)}, bf16[224,128]{1,0:T(8,128)(2,1)S(1)}, u32[]{:S(2)}, u32[]{:S(2)}) collective-permute-start(bf16[224,128]{1,0:T(8,128)(2,1)S(1)} %get-tuple-element.76), channel_id=1, source_target_pairs={{0,1},{1,0},{2,3},{3,2},{4,5},{5,4},{6,7},{7,6},{8,9},{9,8},{10,11... | collective-permute-start | bytes 172040 | tf_op jit(solution)/shard_map/ppermute | solution.py:394
  38.7 4.2 %collective-permute-start.6 = (bf16[224,128]{1,0:T(8,128)(2,1)S(1)}, bf16[224,128]{1,0:T(8,128)(2,1)S(1)}, u32[]{:S(2)}, u32[]{:S(2)}) collective-permute-start(bf16[224,128]{1,0:T(8,128)(2,1)S(1)} %add_convert_fusion.3), channel_id=1, source_target_pairs={{0,2},{1,3},{2,0},{3,1},{4,6},{5,7},{6,4},{7,5},{8,10},{9,11},{10,... | collective-permute-start | bytes 172040 | tf_op jit(solution)/shard_map/ppermute | solution.py:394
  42.9 9.1 %collective-permute-start.7 = (bf16[224,128]{1,0:T(8,128)(2,1)S(1)}, bf16[224,128]{1,0:T(8,128)(2,1)S(1)}, u32[]{:S(2)}, u32[]{:S(2)}) collective-permute-start(bf16[224,128]{1,0:T(8,128)(2,1)S(1)} %add_convert_fusion.2), channel_id=1, source_target_pairs={{0,4},{4,0},{8,12},{12,8},{16,20},{20,16},{24,28},{28,24},{1,5},{5... | collective-permute-start | bytes 172040 | tf_op jit(solution)/shard_map/ppermute | solution.py:394
  44.7 12.6 %collective-permute-start.9 = (bf16[96,2048]{1,0:T(8,128)(2,1)S(1)}, bf16[96,2048]{1,0:T(8,128)(2,1)S(1)}, u32[]{:S(2)}, u32[]{:S(2)}) collective-permute-start(bf16[96,2048]{1,0:T(8,128)(2,1)S(1)} %get-tuple-element.80), channel_id=1, source_target_pairs={{4,8},{12,16},{20,24},{8,4},{16,12},{24,20},{5,9},{13,17},{21,25},... | collective-permute-start | bytes 1179656 | tf_op jit(solution)/shard_map/ppermute | solution.py:414
  52.0 5.3 %collective-permute-start.8 = (bf16[224,128]{1,0:T(8,128)(2,1)S(1)}, bf16[224,128]{1,0:T(8,128)(2,1)S(1)}, u32[]{:S(2)}, u32[]{:S(2)}) collective-permute-start(bf16[224,128]{1,0:T(8,128)(2,1)S(1)} %add_convert_fusion.1), channel_id=1, source_target_pairs={{0,8},{4,12},{8,0},{12,4},{16,24},{20,28},{24,16},{28,20},{1,9},{5... | collective-permute-start | bytes 172040 | tf_op jit(solution)/shard_map/ppermute | solution.py:394
  57.4 9.4 %collective-permute-start.10 = (bf16[224,128]{1,0:T(8,128)(2,1)S(1)}, bf16[224,128]{1,0:T(8,128)(2,1)S(1)}, u32[]{:S(2)}, u32[]{:S(2)}) collective-permute-start(bf16[224,128]{1,0:T(8,128)(2,1)S(1)} %add_convert_fusion.mine), channel_id=1, source_target_pairs={{0,16},{4,20},{8,24},{12,28},{16,0},{20,4},{24,8},{28,12},{1,17},{... | collective-permute-start | bytes 172040 | tf_op jit(solution)/shard_map/ppermute | solution.py:394

commit v6 on v5

--- a/solution.py
+++ b/solution.py
@@ -353,13 +353,21 @@
     input_gradient(taps, 0, range(slab), arrived, result, None, start)
 
 
-def result_kernel(channels, mine, other, mixing, plane_taps, depth_taps):
+def added(*terms):
+    terms = [term.astype(F32) for term in terms]
+    while len(terms) > 1:
+        terms = [left + right for left, right in zip(terms[::2], terms[1::2])]
+    return terms[0]
+
+
+def result_kernel(channels, count, *refs):
+    terms, (mixing, plane_taps, depth_taps) = refs[:count], refs[count:]
     for block in range(2):
         rows = pl.ds(block * channels, channels)
-        total = mine[rows, :].astype(F32) + other[rows, :].astype(F32)
+        total = added(*(term[rows, :] for term in terms))
         mixing[block] = total[:, :channels]
         rows = pl.ds(2 * channels + GROUP * block, GROUP)
-        total = mine[rows, :].astype(F32) + other[rows, :].astype(F32)
+        total = added(*(term[rows, :] for term in terms))
         for t in range(9):
             plane_taps[t, block : block + 1, :] = total[t : t + 1, :channels]
         for t in range(3):
@@ -382,18 +390,18 @@
 
 
 def all_sum(mine, arrivals):
-    arrived, spot, other = [], 0, None
-    for axis in ("dp", "sp"):
-        count, step = lax.axis_size(axis), 1
-        while step < count:
-            if other is not None:
-                mine = (mine.astype(F32) + other.astype(F32)).astype(BF16)
-            if spot in arrivals:
-                mine, value = lax.optimization_barrier((mine, arrivals[spot]))
-                arrived.append(value)
-            other = lax.ppermute(mine, axis, [(i, i ^ step) for i in range(count)])
-            step, spot = step * 2, spot + 1
-    return mine, other, arrived
+    arrived, others = [], []
+    for spot, (axis, steps) in enumerate((("sp", (2, 4, 6)), ("dp", (1, 2, 3)), ("sp", (1,)))):
+        count = lax.axis_size(axis)
+        if others:
+            mine = added(mine, *others).astype(BF16)
+        for value in arrivals.get(spot, ()):
+            mine, value = lax.optimization_barrier((mine, value))
+            arrived.append(value)
+        others = [lax.ppermute(mine, axis, [(i, i ^ step) for i in range(count)]) for step in steps]
+    for value in arrivals.get(-1, ()):
+        arrived.append(value)
+    return (mine, *others), arrived
 
 
 def on_device(volume, cotangent, kernels_xy, kernels_z, mixing):
@@ -475,7 +483,7 @@
         [planes(inside), jax.ShapeDtypeStruct((2 * channels + 2 * GROUP, 128), BF16)],
         scratch=[scratch(inside), scratch(inside), pltpu.VMEM((2, 12, channels, ny), F32)],
     )
-    mine, other, arrived = all_sum(payload, {1: arrived[0], 4: arrived[1]})
+    terms, arrived = all_sum(payload, {1: arrived[:1], -1: arrived[1:]})
     (own,) = call(
         functools.partial(volume_kernel, sizes, slab),
         "volume",
@@ -491,9 +499,9 @@
         scalars=1,
     )
     mixing_grad, plane_grad, depth_grad = call(
-        functools.partial(result_kernel, channels),
+        functools.partial(result_kernel, channels, len(terms)),
         "result",
-        (mine, other),
+        terms,
         [sums(2, channels, channels), sums(9, 2, channels), sums(3, 2, channels)],
     )
     return (

time: 67.7 us -> 55.2 us (0.82)
  waiting for transfers between devices: 17.2 us -> 10.7 us
  starting transfers between devices: 26 us -> 20 us
    ppermute x5 -> x7, starting transfers between devices: 12.8 us -> 6.85 us  [all_sum(): lax.ppermute(mine, axis, [(i, i ^ step) for i in range(count)])]
    ppermute x5 -> x7, waiting for transfers between devices: 12.5 us -> 7.09 us  [all_sum(): lax.ppermute(mine, axis, [(i, i ^ step) for i in range(count)])]
    ppermute x3, waiting for transfers between devices: 4.6 us -> 3.61 us  [exchange(): lax.ppermute(sent[0], 'sp', firsts)]
  transfers between devices with their start and end apart: 11 -> 13, of which waited for: 6 -> 7; matrix products, arithmetic and copies ran while one was open for 5% -> 6% of each run, Pallas kernels for 18% -> 22%
where the time goes in v6:
time: 55.2 us; the launch traced here: 55 us
  starting transfers between devices  20 us (36%)
  Pallas kernels  18 us (33%)
  waiting for transfers between devices  10.7 us (19%)
  local copies, waits for them, and re-layouts  3.11 us (6%)
  other arithmetic  2.34 us (4%)
  between operations  0.9 us (2%)
    pallas_call x7, Pallas kernels, call(): pl.pallas_call(kernel, name=name, out_shape=outputs, in_specs=[smem] * sc...  18 us
    ppermute x3, starting transfers between devices, exchange(): lax.ppermute(sent[0], 'sp', firsts)  11 us
    ppermute x7, waiting for transfers between devices, all_sum(): lax.ppermute(mine, axis, [(i, i ^ step) for i in range(count)])  7.09 us
    ppermute x7, starting transfers between devices, all_sum(): lax.ppermute(mine, axis, [(i, i ^ step) for i in range(count)])  6.85 us
    ppermute x3, waiting for transfers between devices, exchange(): lax.ppermute(sent[0], 'sp', firsts)  3.61 us
    ppermute x3, starting transfers between devices, exchange(): lax.ppermute(sent[1], 'sp', seconds)  2.13 us
    select_n x2, other arithmetic, rims(): return (jnp.where(odd != 0, low, high), jnp.where(odd != 0, high, low))  1.47 us
    another operation x1, local copies, waits for them, and re-layouts, on_device(): vol = lax.optimization_barrier(volume[0].reshape(channels, -1))  1.43 us
  transfers between devices with their start and end apart: 13, of which 7 were waited for; matrix products, arithmetic and copies ran while one was open for 6% of the time, Pallas kernels for 22%

profile of v6, /device:TPU:0, one launch (start us, length us, event | category | flops | bytes accessed | tf_op | source)
XLA Modules:
  0.0 55.0 jit_solution(522636921409858018)
XLA Ops:
  0.6 1.4 %reshape_squeeze.6.vol = bf16[96,4096]{1,0:T(8,128)(2,1)S(1)} reshape(bf16[1,96,4,8,128]{4,3,2,1,0:T(8,128)(2,1)} %param.5) | data formatting | bytes 1572864 | tf_op jit(solution)/shard_map/reshape;squeeze | solution.py:424
  2.1 0.8 %broadcast_select_fusion.3 = (bf16[96,1024]{1,0:T(8,128)(2,1)}, bf16[96,1024]{1,0:T(8,128)(2,1)}) fusion(pred[]{:T(512)S(6)} %ne.41, bf16[96,4096]{1,0:T(8,128)(2,1)S(1)} %reshape_squeeze.6.vol), kind=kLoop, calls=%fused_computation.4 | loop fusion | flops 196608 | bytes 786433 | tf_op jit(solution)/shard_map/jit(_where)/select_n | solution.py:419
  2.9 3.0 %collective-permute-start = (bf16[96,1024]{1,0:T(8,128)(2,1)}, bf16[96,1024]{1,0:T(8,128)(2,1)S(1)}, u32[]{:S(2)}, u32[]{:S(2)}) collective-permute-start(bf16[96,1024]{1,0:T(8,128)(2,1)} %get-tuple-element.43), channel_id=1, source_target_pairs={{0,4},{4,0},{8,12},{12,8},{16,20},{20,16},{24,28},{28,24},{1,5},{5... | collective-permute-start | bytes 589832 | tf_op jit(solution)/shard_map/ppermute | solution.py:422
  6.5 0.7 %broadcast_select_fusion.1 = (bf16[96,1024]{1,0:T(8,128)(2,1)}, bf16[96,1024]{1,0:T(8,128)(2,1)S(1)}) fusion(pred[]{:T(512)S(6)} %ne.41, bf16[96,4096]{1,0:T(8,128)(2,1)S(1)} %reshape_squeeze.6.vol), kind=kLoop, calls=%fused_computation.2 | loop fusion | flops 196608 | bytes 786433 | tf_op jit(solution)/shard_map/jit(_where)/select_n | solution.py:419
  7.2 0.8 %collective-permute-start.3 = (bf16[96,1024]{1,0:T(8,128)(2,1)}, bf16[96,1024]{1,0:T(8,128)(2,1)S(1)}, u32[]{:S(2)}, u32[]{:S(2)}) collective-permute-start(bf16[96,1024]{1,0:T(8,128)(2,1)} %get-tuple-element.82), channel_id=1, source_target_pairs={{4,8},{12,16},{20,24},{8,4},{16,12},{24,20},{5,9},{13,17},{21,25},... | collective-permute-start | bytes 589832 | tf_op jit(solution)/shard_map/ppermute | solution.py:422
  8.0 5.6 %collective-permute-start.2 = (bf16[96,1024]{1,0:T(8,128)(2,1)S(1)}, bf16[96,1024]{1,0:T(8,128)(2,1)S(1)}, u32[]{:S(2)}, u32[]{:S(2)}) collective-permute-start(bf16[96,1024]{1,0:T(8,128)(2,1)S(1)} %get-tuple-element.83), channel_id=1, source_target_pairs={{0,4},{4,0},{8,12},{12,8},{16,20},{20,16},{24,28},{28,24},{1,5},{5... | collective-permute-start | bytes 589832 | tf_op jit(solution)/shard_map/ppermute | solution.py:422
  15.1 1.1 %inner.1 = (bf16[96,2048]{1,0:T(8,128)(2,1)S(1)}, bf16[96,2048]{1,0:T(8,128)(2,1)S(1)}, bf16[96,2048]{1,0:T(8,128)(2,1)S(1)}, bf16[96,2048]{1,0:T(8,128)(2,1)S(1)}) custom-call(bf16[96,4096]{1,0:T(8,128)(2,1)S(1)} %reshape_squeeze.6.vol, bf16[2,21,96,128]{3,2,1,0:T(8,128)(2,1)S(1)} %pad_maximum_fusion.taps, bf16[2,96,96]{2,1,0:T(8,128)(2,1)S(1)} %copy-done), custom_call_target="tpu_custom_call" | custom-call | bytes 4194304 | tf_op jit(solution)/shard_map/inner/pallas_call | solution.py:380
  16.3 3.6 %collective-permute-done.first = bf16[96,1024]{1,0:T(8,128)(2,1)S(1)} collective-permute-done((bf16[96,1024]{1,0:T(8,128)(2,1)}, bf16[96,1024]{1,0:T(8,128)(2,1)S(1)}, u32[]{:S(2)}, u32[]{:S(2)}) %collective-permute-start) | collective-permute-done | bytes 196640 | tf_op jit(solution)/shard_map/ppermute | solution.py:422
  19.9 3.8 %middle.1 = (bf16[96,1024]{1,0:T(8,128)(2,1)S(1)}, bf16[96,1024]{1,0:T(8,128)(2,1)S(1)}, bf16[96,2048]{1,0:T(8,128)(2,1)S(1)}, bf16[96,2048]{1,0:T(8,128)(2,1)S(...) custom-call(s32[1]{0:T(128)} %bitcast.odd, ...), custom_call_target="tpu_custom_call" | custom-call | bytes 12582912 | tf_op jit(solution)/shard_map/middle/pallas_call | solution.py:380
  23.8 5.1 %edge.1 = (bf16[96,1024]{1,0:T(8,128)(2,1)S(1)}, bf16[96,1024]{1,0:T(8,128)(2,1)S(1)}, bf16[96,2048]{1,0:T(8,128)(2,1)S(1)}, bf16[96,2048]{1,0:T(8,128)(2,1)S(1)...) custom-call(s32[1]{0:T(128)} %bitcast.odd, ...), custom_call_target="tpu_custom_call" | custom-call | bytes 18874368 | tf_op jit(solution)/shard_map/edge/pallas_call | solution.py:380
  28.9 2.5 %collective-permute-start.7 = (bf16[96,2048]{1,0:T(8,128)(2,1)S(1)}, bf16[96,2048]{1,0:T(8,128)(2,1)S(1)}, u32[]{:S(2)}, u32[]{:S(2)}) collective-permute-start(bf16[96,2048]{1,0:T(8,128)(2,1)S(1)} %get-tuple-element.75), channel_id=1, source_target_pairs={{0,4},{4,0},{8,12},{12,8},{16,20},{20,16},{24,28},{28,24},{1,5},{5... | collective-permute-start | bytes 1179656 | tf_op jit(solution)/shard_map/ppermute | solution.py:422
  31.3 5.0 %weights.1 = (bf16[96,2048]{1,0:T(8,128)(2,1)S(1)}, bf16[224,128]{1,0:T(8,128)(2,1)S(1)}) custom-call(bf16[96,4096]{1,0:T(8,128)(2,1)S(1)} %reshape_squeeze.6.vol, bf16[96,1024]{1,0:T(8,128)(2,1)S(1)} %get-tuple-element.46.lo1, bf16[96,1024]{1,0:T(8,128)(2,1)S(1)} %get-tuple-element.47.hi1, bf16[96,1024]{1,0:T(8,128)(2,1)S(1)} %get-tuple-element.52.lo2, ...), custom_call_target="tpu_custom_call" | custom-call | bytes 1 | tf_op jit(solution)/shard_map/weights/pallas_call | solution.py:380
  36.4 1.4 %collective-permute-start.6 = (bf16[224,128]{1,0:T(8,128)(2,1)S(1)}, bf16[224,128]{1,0:T(8,128)(2,1)S(1)}, u32[]{:S(2)}, u32[]{:S(2)}) collective-permute-start(bf16[224,128]{1,0:T(8,128)(2,1)S(1)} %get-tuple-element.74), channel_id=1, source_target_pairs={{0,24},{4,28},{8,16},{12,20},{16,8},{20,12},{24,0},{28,4},{1,25},{... | collective-permute-start | bytes 172040 | tf_op jit(solution)/shard_map/ppermute | solution.py:401
  37.8 1.7 %collective-permute-start.5 = (bf16[224,128]{1,0:T(8,128)(2,1)S(1)}, bf16[224,128]{1,0:T(8,128)(2,1)S(1)}, u32[]{:S(2)}, u32[]{:S(2)}) collective-permute-start(bf16[224,128]{1,0:T(8,128)(2,1)S(1)} %get-tuple-element.74), channel_id=1, source_target_pairs={{0,16},{4,20},{8,24},{12,28},{16,0},{20,4},{24,8},{28,12},{1,17},{... | collective-permute-start | bytes 172040 | tf_op jit(solution)/shard_map/ppermute | solution.py:401
  39.4 1.5 %collective-permute-start.4 = (bf16[224,128]{1,0:T(8,128)(2,1)S(1)}, bf16[224,128]{1,0:T(8,128)(2,1)S(1)}, u32[]{:S(2)}, u32[]{:S(2)}) collective-permute-start(bf16[224,128]{1,0:T(8,128)(2,1)S(1)} %get-tuple-element.74), channel_id=1, source_target_pairs={{0,8},{4,12},{8,0},{12,4},{16,24},{20,28},{24,16},{28,20},{1,9},{5... | collective-permute-start | bytes 172040 | tf_op jit(solution)/shard_map/ppermute | solution.py:401
  41.5 1.2 %collective-permute-done.6 = bf16[224,128]{1,0:T(8,128)(2,1)S(1)} collective-permute-done((bf16[224,128]{1,0:T(8,128)(2,1)S(1)}, bf16[224,128]{1,0:T(8,128)(2,1)S(1)}, u32[]{:S(2)}, u32[]{:S(2)}) %collective-permute-start.6) | collective-permute-done | bytes 57376 | tf_op jit(solution)/shard_map/ppermute | solution.py:401
  42.7 0.7 %collective-permute-done.5 = bf16[224,128]{1,0:T(8,128)(2,1)S(1)} collective-permute-done((bf16[224,128]{1,0:T(8,128)(2,1)S(1)}, bf16[224,128]{1,0:T(8,128)(2,1)S(1)}, u32[]{:S(2)}, u32[]{:S(2)}) %collective-permute-start.5) | collective-permute-done | bytes 57376 | tf_op jit(solution)/shard_map/ppermute | solution.py:401
  43.4 1.1 %collective-permute-done.4 = bf16[224,128]{1,0:T(8,128)(2,1)S(1)} collective-permute-done((bf16[224,128]{1,0:T(8,128)(2,1)S(1)}, bf16[224,128]{1,0:T(8,128)(2,1)S(1)}, u32[]{:S(2)}, u32[]{:S(2)}) %collective-permute-start.4) | collective-permute-done | bytes 57376 | tf_op jit(solution)/shard_map/ppermute | solution.py:401
  44.6 1.5 %collective-permute-start.10 = (bf16[224,128]{1,0:T(8,128)(2,1)S(1)}, bf16[224,128]{1,0:T(8,128)(2,1)S(1)}, u32[]{:S(2)}, u32[]{:S(2)}) collective-permute-start(bf16[224,128]{1,0:T(8,128)(2,1)S(1)} %add_convert_fusion.1), channel_id=1, source_target_pairs={{0,2},{1,3},{2,0},{3,1},{4,6},{5,7},{6,4},{7,5},{8,10},{9,11},{10,... | collective-permute-start | bytes 172040 | tf_op jit(solution)/shard_map/ppermute | solution.py:401
  46.5 2.3 %collective-permute-done.11 = bf16[224,128]{1,0:T(8,128)(2,1)S(1)} collective-permute-done((bf16[224,128]{1,0:T(8,128)(2,1)S(1)}, bf16[224,128]{1,0:T(8,128)(2,1)S(1)}, u32[]{:S(2)}, u32[]{:S(2)}) %collective-permute-start.11) | collective-permute-done | bytes 57376 | tf_op jit(solution)/shard_map/ppermute | solution.py:401
  48.8 1.3 %collective-permute-done.10 = bf16[224,128]{1,0:T(8,128)(2,1)S(1)} collective-permute-done((bf16[224,128]{1,0:T(8,128)(2,1)S(1)}, bf16[224,128]{1,0:T(8,128)(2,1)S(1)}, u32[]{:S(2)}, u32[]{:S(2)}) %collective-permute-start.10) | collective-permute-done | bytes 57376 | tf_op jit(solution)/shard_map/ppermute | solution.py:401
  50.6 1.1 %volume.1.own = bf16[96,4096]{1,0:T(8,128)(2,1)S(1)} custom-call(bf16[2,21,96,128]{3,2,1,0:T(8,128)(2,1)S(1)} %pad_maximum_fusion.taps, bf16[96,2048]{1,0:T(8,128)(2,1)S(1)} %get-tuple-element.73.gpl1_i, bf16[96,2048]{1,0:T(8,128)(2,1)S(1)} %get-tuple-element.71.gpl1_lo, bf16[96,2048]{1,0:T(8,128)(2,1)S(1)} %get-tuple-element.72.gpl1_hi), custom_call_target="tpu_custom_call" | custom-call | bytes 1 | tf_op jit(solution)/shard_map/volume/pallas_call | solution.py:380
  51.7 1.0 %final.1 = bf16[96,4096]{1,0:T(8,128)(2,1)S(1)} custom-call(s32[1]{0:T(128)} %bitcast.odd, bf16[2,21,96,128]{3,2,1,0:T(8,128)(2,1)S(1)} %pad_maximum_fusion.taps, bf16[96,4096]{1,0:T(8,128)(2,1)S(1)} %volume.1.own, bf16[96,2048]{1,0:T(8,128)(2,1)S(1)} %collective-permute-done.7.first, bf16[96,2048]{1,0:T(8,128)(2,1)S(1)} %collective-permute-done.8.second), custom_call_target="tpu_custom_call" | custom-call | bytes 1 | tf_op jit(solution)/shard_map/final/pallas_call | solution.py:380
  52.8 1.0 %copy.12 = bf16[12,8,32,128]{3,2,1,0:T(8,128)(2,1)} copy(bf16[12,8,32,128]{3,1,2,0:T(8,128)(2,1)S(1)} %bitcast.18) | data formatting | bytes 1572864
  (38 shorter events, 4.9 us)
Async XLA Ops:
  2.1 11.9 %copy-start.1 = (bf16[1,96,4,8,128]{4,3,2,1,0:T(8,128)(2,1)S(1)}, bf16[1,96,4,8,128]{4,3,2,1,0:T(8,128)(2,1)}, u32[]{:S(2)}) copy-start(bf16[1,96,4,8,128]{4,3,2,1,0:T(8,128)(2,1)} %param.6) | copy-start | bytes 2359300
  2.9 17.0 %collective-permute-start = (bf16[96,1024]{1,0:T(8,128)(2,1)}, bf16[96,1024]{1,0:T(8,128)(2,1)S(1)}, u32[]{:S(2)}, u32[]{:S(2)}) collective-permute-start(bf16[96,1024]{1,0:T(8,128)(2,1)} %get-tuple-element.43), channel_id=1, source_target_pairs={{0,4},{4,0},{8,12},{12,8},{16,20},{20,16},{24,28},{28,24},{1,5},{5... | collective-permute-start | bytes 589832 | tf_op jit(solution)/shard_map/ppermute | solution.py:422
  5.8 14.1 %collective-permute-start.1 = (bf16[96,1024]{1,0:T(8,128)(2,1)}, bf16[96,1024]{1,0:T(8,128)(2,1)S(1)}, u32[]{:S(2)}, u32[]{:S(2)}) collective-permute-start(bf16[96,1024]{1,0:T(8,128)(2,1)} %get-tuple-element.44), channel_id=1, source_target_pairs={{4,8},{12,16},{20,24},{8,4},{16,12},{24,20},{5,9},{13,17},{21,25},... | collective-permute-start | bytes 589832 | tf_op jit(solution)/shard_map/ppermute | solution.py:422
  6.5 7.1 %copy-start.3 = (bf16[2,96,3]{1,0,2:T(2,128)(2,1)S(1)}, bf16[2,96,3]{1,0,2:T(2,128)(2,1)}, u32[]{:S(2)}) copy-start(bf16[2,96,3]{1,0,2:T(2,128)(2,1)} %param.8) | copy-start | bytes 3460
  6.5 7.2 %copy-start.2 = (bf16[2,96,3,3]{1,0,3,2:T(2,128)(2,1)S(1)}, bf16[2,96,3,3]{1,0,3,2:T(2,128)(2,1)}, u32[]{:S(2)}) copy-start(bf16[2,96,3,3]{1,0,3,2:T(2,128)(2,1)} %param.7) | copy-start | bytes 10372
  7.2 6.6 %copy-start = (bf16[2,96,96]{2,1,0:T(8,128)(2,1)S(1)}, bf16[2,96,96]{2,1,0:T(8,128)(2,1)}, u32[]{:S(2)}) copy-start(bf16[2,96,96]{2,1,0:T(8,128)(2,1)} %mix.5) | copy-start | bytes 110596
  7.2 16.5 %collective-permute-start.3 = (bf16[96,1024]{1,0:T(8,128)(2,1)}, bf16[96,1024]{1,0:T(8,128)(2,1)S(1)}, u32[]{:S(2)}, u32[]{:S(2)}) collective-permute-start(bf16[96,1024]{1,0:T(8,128)(2,1)} %get-tuple-element.82), channel_id=1, source_target_pairs={{4,8},{12,16},{20,24},{8,4},{16,12},{24,20},{5,9},{13,17},{21,25},... | collective-permute-start | bytes 589832 | tf_op jit(solution)/shard_map/ppermute | solution.py:422
  8.0 15.7 %collective-permute-start.2 = (bf16[96,1024]{1,0:T(8,128)(2,1)S(1)}, bf16[96,1024]{1,0:T(8,128)(2,1)S(1)}, u32[]{:S(2)}, u32[]{:S(2)}) collective-permute-start(bf16[96,1024]{1,0:T(8,128)(2,1)S(1)} %get-tuple-element.83), channel_id=1, source_target_pairs={{0,4},{4,0},{8,12},{12,8},{16,20},{20,16},{24,28},{28,24},{1,5},{5... | collective-permute-start | bytes 589832 | tf_op jit(solution)/shard_map/ppermute | solution.py:422
  28.9 15.7 %collective-permute-start.7 = (bf16[96,2048]{1,0:T(8,128)(2,1)S(1)}, bf16[96,2048]{1,0:T(8,128)(2,1)S(1)}, u32[]{:S(2)}, u32[]{:S(2)}) collective-permute-start(bf16[96,2048]{1,0:T(8,128)(2,1)S(1)} %get-tuple-element.75), channel_id=1, source_target_pairs={{0,4},{4,0},{8,12},{12,8},{16,20},{20,16},{24,28},{28,24},{1,5},{5... | collective-permute-start | bytes 1179656 | tf_op jit(solution)/shard_map/ppermute | solution.py:422
  36.4 6.3 %collective-permute-start.6 = (bf16[224,128]{1,0:T(8,128)(2,1)S(1)}, bf16[224,128]{1,0:T(8,128)(2,1)S(1)}, u32[]{:S(2)}, u32[]{:S(2)}) collective-permute-start(bf16[224,128]{1,0:T(8,128)(2,1)S(1)} %get-tuple-element.74), channel_id=1, source_target_pairs={{0,24},{4,28},{8,16},{12,20},{16,8},{20,12},{24,0},{28,4},{1,25},{... | collective-permute-start | bytes 172040 | tf_op jit(solution)/shard_map/ppermute | solution.py:401
  37.8 5.7 %collective-permute-start.5 = (bf16[224,128]{1,0:T(8,128)(2,1)S(1)}, bf16[224,128]{1,0:T(8,128)(2,1)S(1)}, u32[]{:S(2)}, u32[]{:S(2)}) collective-permute-start(bf16[224,128]{1,0:T(8,128)(2,1)S(1)} %get-tuple-element.74), channel_id=1, source_target_pairs={{0,16},{4,20},{8,24},{12,28},{16,0},{20,4},{24,8},{28,12},{1,17},{... | collective-permute-start | bytes 172040 | tf_op jit(solution)/shard_map/ppermute | solution.py:401
  39.4 5.1 %collective-permute-start.4 = (bf16[224,128]{1,0:T(8,128)(2,1)S(1)}, bf16[224,128]{1,0:T(8,128)(2,1)S(1)}, u32[]{:S(2)}, u32[]{:S(2)}) collective-permute-start(bf16[224,128]{1,0:T(8,128)(2,1)S(1)} %get-tuple-element.74), channel_id=1, source_target_pairs={{0,8},{4,12},{8,0},{12,4},{16,24},{20,28},{24,16},{28,20},{1,9},{5... | collective-permute-start | bytes 172040 | tf_op jit(solution)/shard_map/ppermute | solution.py:401
  40.9 10.9 %collective-permute-start.8 = (bf16[96,2048]{1,0:T(8,128)(2,1)S(1)}, bf16[96,2048]{1,0:T(8,128)(2,1)S(1)}, u32[]{:S(2)}, u32[]{:S(2)}) collective-permute-start(bf16[96,2048]{1,0:T(8,128)(2,1)S(1)} %get-tuple-element.77), channel_id=1, source_target_pairs={{4,8},{12,16},{20,24},{8,4},{16,12},{24,20},{5,9},{13,17},{21,25},... | collective-permute-start | bytes 1179656 | tf_op jit(solution)/shard_map/ppermute | solution.py:422
  44.6 4.2 %collective-permute-start.11 = (bf16[224,128]{1,0:T(8,128)(2,1)S(1)}, bf16[224,128]{1,0:T(8,128)(2,1)S(1)}, u32[]{:S(2)}, u32[]{:S(2)}) collective-permute-start(bf16[224,128]{1,0:T(8,128)(2,1)S(1)} %add_convert_fusion.1), channel_id=1, source_target_pairs={{0,3},{1,2},{2,1},{3,0},{4,7},{5,6},{6,5},{7,4},{8,11},{9,10},{10,... | collective-permute-start | bytes 172040 | tf_op jit(solution)/shard_map/ppermute | solution.py:401
  44.6 5.4 %collective-permute-start.10 = (bf16[224,128]{1,0:T(8,128)(2,1)S(1)}, bf16[224,128]{1,0:T(8,128)(2,1)S(1)}, u32[]{:S(2)}, u32[]{:S(2)}) collective-permute-start(bf16[224,128]{1,0:T(8,128)(2,1)S(1)} %add_convert_fusion.1), channel_id=1, source_target_pairs={{0,2},{1,3},{2,0},{3,1},{4,6},{5,7},{6,4},{7,5},{8,10},{9,11},{10,... | collective-permute-start | bytes 172040 | tf_op jit(solution)/shard_map/ppermute | solution.py:401
  46.2 3.9 %collective-permute-start.9 = (bf16[224,128]{1,0:T(8,128)(2,1)S(1)}, bf16[224,128]{1,0:T(8,128)(2,1)S(1)}, u32[]{:S(2)}, u32[]{:S(2)}) collective-permute-start(bf16[224,128]{1,0:T(8,128)(2,1)S(1)} %add_convert_fusion.1), channel_id=1, source_target_pairs={{0,1},{1,0},{2,3},{3,2},{4,5},{5,4},{6,7},{7,6},{8,9},{9,8},{10,11... | collective-permute-start | bytes 172040 | tf_op jit(solution)/shard_map/ppermute | solution.py:401
  50.1 4.2 %collective-permute-start.12 = (bf16[224,128]{1,0:T(8,128)(2,1)S(1)}, bf16[224,128]{1,0:T(8,128)(2,1)S(1)}, u32[]{:S(2)}, u32[]{:S(2)}) collective-permute-start(bf16[224,128]{1,0:T(8,128)(2,1)S(1)} %add_convert_fusion.refs_0_), channel_id=1, source_target_pairs={{0,4},{4,0},{8,12},{12,8},{16,20},{20,16},{24,28},{28,24},{1,5},{5... | collective-permute-start | bytes 172040 | tf_op jit(solution)/shard_map/ppermute | solution.py:401

commit v7 on v6

--- a/solution.py
+++ b/solution.py
@@ -389,16 +389,29 @@
     )(*operands)
 
 
+def chunks(bits):
+    bits = list(bits)
+    return [bits[at : at + 2] for at in range(0, len(bits), 2)]
+
+
+def sum_groups(dp_bits, sp_bits):
+    return chunks(range(dp_bits + 1, dp_bits + sp_bits)) + chunks(range(dp_bits)) + [[dp_bits]]
+
+
 def all_sum(mine, arrivals):
     arrived, others = [], []
-    for spot, (axis, steps) in enumerate((("sp", (2, 4, 6)), ("dp", (1, 2, 3)), ("sp", (1,)))):
-        count = lax.axis_size(axis)
+    dp_bits, sp_bits = (lax.axis_size(axis).bit_length() - 1 for axis in ("dp", "sp"))
+    places = range(1 << (dp_bits + sp_bits))
+    for spot, bits in enumerate(sum_groups(dp_bits, sp_bits)):
         if others:
             mine = added(mine, *others).astype(BF16)
         for value in arrivals.get(spot, ()):
             mine, value = lax.optimization_barrier((mine, value))
             arrived.append(value)
-        others = [lax.ppermute(mine, axis, [(i, i ^ step) for i in range(count)]) for step in steps]
+        steps = [1 << bits[0]]
+        if len(bits) > 1:
+            steps += [1 << bits[1], (1 << bits[0]) + (1 << bits[1])]
+        others = [lax.ppermute(mine, ("sp", "dp"), [(i, i ^ step) for i in places]) for step in steps]
     for value in arrivals.get(-1, ()):
         arrived.append(value)
     return (mine, *others), arrived

time: 55.2 us -> 55.2 us (level)
  no operation moved by 1% of the time
where the time goes in v7:
time: 55.2 us; the launch traced here: 55 us
  starting transfers between devices  20 us (36%)
  Pallas kernels  18 us (33%)
  waiting for transfers between devices  10.7 us (19%)
  local copies, waits for them, and re-layouts  3.11 us (6%)
  other arithmetic  2.34 us (4%)
  between operations  0.9 us (2%)
    pallas_call x7, Pallas kernels, call(): pl.pallas_call(kernel, name=name, out_shape=outputs, in_specs=[smem] * sc...  18 us
    ppermute x3, starting transfers between devices, exchange(): lax.ppermute(sent[0], 'sp', firsts)  11 us
    ppermute x7, waiting for transfers between devices, all_sum(): lax.ppermute(mine, ('sp', 'dp'), [(i, i ^ step) for i in places])  7.09 us
    ppermute x7, starting transfers between devices, all_sum(): lax.ppermute(mine, ('sp', 'dp'), [(i, i ^ step) for i in places])  6.85 us
    ppermute x3, waiting for transfers between devices, exchange(): lax.ppermute(sent[0], 'sp', firsts)  3.61 us
    ppermute x3, starting transfers between devices, exchange(): lax.ppermute(sent[1], 'sp', seconds)  2.13 us
    select_n x2, other arithmetic, rims(): return (jnp.where(odd != 0, low, high), jnp.where(odd != 0, high, low))  1.47 us
    another operation x1, local copies, waits for them, and re-layouts, on_device(): vol = lax.optimization_barrier(volume[0].reshape(channels, -1))  1.43 us
  transfers between devices with their start and end apart: 13, of which 7 were waited for; matrix products, arithmetic and copies ran while one was open for 6% of the time, Pallas kernels for 22%

profile of v7, /device:TPU:0, one launch (start us, length us, event | category | flops | bytes accessed | tf_op | source)
XLA Modules:
  0.0 55.0 jit_solution(522636921409858018)
XLA Ops:
  0.6 1.4 %reshape_squeeze.6.vol = bf16[96,4096]{1,0:T(8,128)(2,1)S(1)} reshape(bf16[1,96,4,8,128]{4,3,2,1,0:T(8,128)(2,1)} %param.5) | data formatting | bytes 1572864 | tf_op jit(solution)/shard_map/reshape;squeeze | solution.py:437
  2.1 0.8 %broadcast_select_fusion.3 = (bf16[96,1024]{1,0:T(8,128)(2,1)}, bf16[96,1024]{1,0:T(8,128)(2,1)}) fusion(pred[]{:T(512)S(6)} %ne.41, bf16[96,4096]{1,0:T(8,128)(2,1)S(1)} %reshape_squeeze.6.vol), kind=kLoop, calls=%fused_computation.4 | loop fusion | flops 196608 | bytes 786433 | tf_op jit(solution)/shard_map/jit(_where)/select_n | solution.py:432
  2.9 3.0 %collective-permute-start = (bf16[96,1024]{1,0:T(8,128)(2,1)}, bf16[96,1024]{1,0:T(8,128)(2,1)S(1)}, u32[]{:S(2)}, u32[]{:S(2)}) collective-permute-start(bf16[96,1024]{1,0:T(8,128)(2,1)} %get-tuple-element.43), channel_id=1, source_target_pairs={{0,4},{4,0},{8,12},{12,8},{16,20},{20,16},{24,28},{28,24},{1,5},{5... | collective-permute-start | bytes 589832 | tf_op jit(solution)/shard_map/ppermute | solution.py:435
  6.5 0.7 %broadcast_select_fusion.1 = (bf16[96,1024]{1,0:T(8,128)(2,1)}, bf16[96,1024]{1,0:T(8,128)(2,1)S(1)}) fusion(pred[]{:T(512)S(6)} %ne.41, bf16[96,4096]{1,0:T(8,128)(2,1)S(1)} %reshape_squeeze.6.vol), kind=kLoop, calls=%fused_computation.2 | loop fusion | flops 196608 | bytes 786433 | tf_op jit(solution)/shard_map/jit(_where)/select_n | solution.py:432
  7.2 0.8 %collective-permute-start.3 = (bf16[96,1024]{1,0:T(8,128)(2,1)}, bf16[96,1024]{1,0:T(8,128)(2,1)S(1)}, u32[]{:S(2)}, u32[]{:S(2)}) collective-permute-start(bf16[96,1024]{1,0:T(8,128)(2,1)} %get-tuple-element.82), channel_id=1, source_target_pairs={{4,8},{12,16},{20,24},{8,4},{16,12},{24,20},{5,9},{13,17},{21,25},... | collective-permute-start | bytes 589832 | tf_op jit(solution)/shard_map/ppermute | solution.py:435
  8.0 5.6 %collective-permute-start.2 = (bf16[96,1024]{1,0:T(8,128)(2,1)S(1)}, bf16[96,1024]{1,0:T(8,128)(2,1)S(1)}, u32[]{:S(2)}, u32[]{:S(2)}) collective-permute-start(bf16[96,1024]{1,0:T(8,128)(2,1)S(1)} %get-tuple-element.83), channel_id=1, source_target_pairs={{0,4},{4,0},{8,12},{12,8},{16,20},{20,16},{24,28},{28,24},{1,5},{5... | collective-permute-start | bytes 589832 | tf_op jit(solution)/shard_map/ppermute | solution.py:435
  15.1 1.1 %inner.1 = (bf16[96,2048]{1,0:T(8,128)(2,1)S(1)}, bf16[96,2048]{1,0:T(8,128)(2,1)S(1)}, bf16[96,2048]{1,0:T(8,128)(2,1)S(1)}, bf16[96,2048]{1,0:T(8,128)(2,1)S(1)}) custom-call(bf16[96,4096]{1,0:T(8,128)(2,1)S(1)} %reshape_squeeze.6.vol, bf16[2,21,96,128]{3,2,1,0:T(8,128)(2,1)S(1)} %pad_maximum_fusion.taps, bf16[2,96,96]{2,1,0:T(8,128)(2,1)S(1)} %copy-done), custom_call_target="tpu_custom_call" | custom-call | bytes 4194304 | tf_op jit(solution)/shard_map/inner/pallas_call | solution.py:380
  16.3 3.6 %collective-permute-done.first = bf16[96,1024]{1,0:T(8,128)(2,1)S(1)} collective-permute-done((bf16[96,1024]{1,0:T(8,128)(2,1)}, bf16[96,1024]{1,0:T(8,128)(2,1)S(1)}, u32[]{:S(2)}, u32[]{:S(2)}) %collective-permute-start) | collective-permute-done | bytes 196640 | tf_op jit(solution)/shard_map/ppermute | solution.py:435
  19.9 3.8 %middle.1 = (bf16[96,1024]{1,0:T(8,128)(2,1)S(1)}, bf16[96,1024]{1,0:T(8,128)(2,1)S(1)}, bf16[96,2048]{1,0:T(8,128)(2,1)S(1)}, bf16[96,2048]{1,0:T(8,128)(2,1)S(...) custom-call(s32[1]{0:T(128)} %bitcast.odd, ...), custom_call_target="tpu_custom_call" | custom-call | bytes 12582912 | tf_op jit(solution)/shard_map/middle/pallas_call | solution.py:380
  23.8 5.1 %edge.1 = (bf16[96,1024]{1,0:T(8,128)(2,1)S(1)}, bf16[96,1024]{1,0:T(8,128)(2,1)S(1)}, bf16[96,2048]{1,0:T(8,128)(2,1)S(1)}, bf16[96,2048]{1,0:T(8,128)(2,1)S(1)...) custom-call(s32[1]{0:T(128)} %bitcast.odd, ...), custom_call_target="tpu_custom_call" | custom-call | bytes 18874368 | tf_op jit(solution)/shard_map/edge/pallas_call | solution.py:380
  28.9 2.5 %collective-permute-start.7 = (bf16[96,2048]{1,0:T(8,128)(2,1)S(1)}, bf16[96,2048]{1,0:T(8,128)(2,1)S(1)}, u32[]{:S(2)}, u32[]{:S(2)}) collective-permute-start(bf16[96,2048]{1,0:T(8,128)(2,1)S(1)} %get-tuple-element.75), channel_id=1, source_target_pairs={{0,4},{4,0},{8,12},{12,8},{16,20},{20,16},{24,28},{28,24},{1,5},{5... | collective-permute-start | bytes 1179656 | tf_op jit(solution)/shard_map/ppermute | solution.py:435
  31.3 5.0 %weights.1 = (bf16[96,2048]{1,0:T(8,128)(2,1)S(1)}, bf16[224,128]{1,0:T(8,128)(2,1)S(1)}) custom-call(bf16[96,4096]{1,0:T(8,128)(2,1)S(1)} %reshape_squeeze.6.vol, bf16[96,1024]{1,0:T(8,128)(2,1)S(1)} %get-tuple-element.46.lo1, bf16[96,1024]{1,0:T(8,128)(2,1)S(1)} %get-tuple-element.47.hi1, bf16[96,1024]{1,0:T(8,128)(2,1)S(1)} %get-tuple-element.52.lo2, ...), custom_call_target="tpu_custom_call" | custom-call | bytes 1 | tf_op jit(solution)/shard_map/weights/pallas_call | solution.py:380
  36.4 1.4 %collective-permute-start.6 = (bf16[224,128]{1,0:T(8,128)(2,1)S(1)}, bf16[224,128]{1,0:T(8,128)(2,1)S(1)}, u32[]{:S(2)}, u32[]{:S(2)}) collective-permute-start(bf16[224,128]{1,0:T(8,128)(2,1)S(1)} %get-tuple-element.74), channel_id=1, source_target_pairs={{0,24},{1,25},{2,26},{3,27},{4,28},{5,29},{6,30},{7,31},{8,16},{9,... | collective-permute-start | bytes 172040 | tf_op jit(solution)/shard_map/ppermute | solution.py:414
  37.8 1.7 %collective-permute-start.5 = (bf16[224,128]{1,0:T(8,128)(2,1)S(1)}, bf16[224,128]{1,0:T(8,128)(2,1)S(1)}, u32[]{:S(2)}, u32[]{:S(2)}) collective-permute-start(bf16[224,128]{1,0:T(8,128)(2,1)S(1)} %get-tuple-element.74), channel_id=1, source_target_pairs={{0,16},{1,17},{2,18},{3,19},{4,20},{5,21},{6,22},{7,23},{8,24},{9,... | collective-permute-start | bytes 172040 | tf_op jit(solution)/shard_map/ppermute | solution.py:414
  39.4 1.5 %collective-permute-start.4 = (bf16[224,128]{1,0:T(8,128)(2,1)S(1)}, bf16[224,128]{1,0:T(8,128)(2,1)S(1)}, u32[]{:S(2)}, u32[]{:S(2)}) collective-permute-start(bf16[224,128]{1,0:T(8,128)(2,1)S(1)} %get-tuple-element.74), channel_id=1, source_target_pairs={{0,8},{1,9},{2,10},{3,11},{4,12},{5,13},{6,14},{7,15},{8,0},{9,1},... | collective-permute-start | bytes 172040 | tf_op jit(solution)/shard_map/ppermute | solution.py:414
  41.5 1.2 %collective-permute-done.6 = bf16[224,128]{1,0:T(8,128)(2,1)S(1)} collective-permute-done((bf16[224,128]{1,0:T(8,128)(2,1)S(1)}, bf16[224,128]{1,0:T(8,128)(2,1)S(1)}, u32[]{:S(2)}, u32[]{:S(2)}) %collective-permute-start.6) | collective-permute-done | bytes 57376 | tf_op jit(solution)/shard_map/ppermute | solution.py:414
  42.7 0.7 %collective-permute-done.5 = bf16[224,128]{1,0:T(8,128)(2,1)S(1)} collective-permute-done((bf16[224,128]{1,0:T(8,128)(2,1)S(1)}, bf16[224,128]{1,0:T(8,128)(2,1)S(1)}, u32[]{:S(2)}, u32[]{:S(2)}) %collective-permute-start.5) | collective-permute-done | bytes 57376 | tf_op jit(solution)/shard_map/ppermute | solution.py:414
  43.4 1.1 %collective-permute-done.4 = bf16[224,128]{1,0:T(8,128)(2,1)S(1)} collective-permute-done((bf16[224,128]{1,0:T(8,128)(2,1)S(1)}, bf16[224,128]{1,0:T(8,128)(2,1)S(1)}, u32[]{:S(2)}, u32[]{:S(2)}) %collective-permute-start.4) | collective-permute-done | bytes 57376 | tf_op jit(solution)/shard_map/ppermute | solution.py:414
  44.6 1.5 %collective-permute-start.10 = (bf16[224,128]{1,0:T(8,128)(2,1)S(1)}, bf16[224,128]{1,0:T(8,128)(2,1)S(1)}, u32[]{:S(2)}, u32[]{:S(2)}) collective-permute-start(bf16[224,128]{1,0:T(8,128)(2,1)S(1)} %add_convert_fusion.1), channel_id=1, source_target_pairs={{0,2},{1,3},{2,0},{3,1},{4,6},{5,7},{6,4},{7,5},{8,10},{9,11},{10,... | collective-permute-start | bytes 172040 | tf_op jit(solution)/shard_map/ppermute | solution.py:414
  46.5 2.3 %collective-permute-done.11 = bf16[224,128]{1,0:T(8,128)(2,1)S(1)} collective-permute-done((bf16[224,128]{1,0:T(8,128)(2,1)S(1)}, bf16[224,128]{1,0:T(8,128)(2,1)S(1)}, u32[]{:S(2)}, u32[]{:S(2)}) %collective-permute-start.11) | collective-permute-done | bytes 57376 | tf_op jit(solution)/shard_map/ppermute | solution.py:414
  48.8 1.3 %collective-permute-done.10 = bf16[224,128]{1,0:T(8,128)(2,1)S(1)} collective-permute-done((bf16[224,128]{1,0:T(8,128)(2,1)S(1)}, bf16[224,128]{1,0:T(8,128)(2,1)S(1)}, u32[]{:S(2)}, u32[]{:S(2)}) %collective-permute-start.10) | collective-permute-done | bytes 57376 | tf_op jit(solution)/shard_map/ppermute | solution.py:414
  50.6 1.1 %volume.1.own = bf16[96,4096]{1,0:T(8,128)(2,1)S(1)} custom-call(bf16[2,21,96,128]{3,2,1,0:T(8,128)(2,1)S(1)} %pad_maximum_fusion.taps, bf16[96,2048]{1,0:T(8,128)(2,1)S(1)} %get-tuple-element.73.gpl1_i, bf16[96,2048]{1,0:T(8,128)(2,1)S(1)} %get-tuple-element.71.gpl1_lo, bf16[96,2048]{1,0:T(8,128)(2,1)S(1)} %get-tuple-element.72.gpl1_hi), custom_call_target="tpu_custom_call" | custom-call | bytes 1 | tf_op jit(solution)/shard_map/volume/pallas_call | solution.py:380
  51.7 1.0 %final.1 = bf16[96,4096]{1,0:T(8,128)(2,1)S(1)} custom-call(s32[1]{0:T(128)} %bitcast.odd, bf16[2,21,96,128]{3,2,1,0:T(8,128)(2,1)S(1)} %pad_maximum_fusion.taps, bf16[96,4096]{1,0:T(8,128)(2,1)S(1)} %volume.1.own, bf16[96,2048]{1,0:T(8,128)(2,1)S(1)} %collective-permute-done.7.first, bf16[96,2048]{1,0:T(8,128)(2,1)S(1)} %collective-permute-done.8.second), custom_call_target="tpu_custom_call" | custom-call | bytes 1 | tf_op jit(solution)/shard_map/final/pallas_call | solution.py:380
  52.8 1.0 %copy.12 = bf16[12,8,32,128]{3,2,1,0:T(8,128)(2,1)} copy(bf16[12,8,32,128]{3,1,2,0:T(8,128)(2,1)S(1)} %bitcast.18) | data formatting | bytes 1572864
  (38 shorter events, 4.9 us)
Async XLA Ops:
  2.1 11.9 %copy-start.1 = (bf16[1,96,4,8,128]{4,3,2,1,0:T(8,128)(2,1)S(1)}, bf16[1,96,4,8,128]{4,3,2,1,0:T(8,128)(2,1)}, u32[]{:S(2)}) copy-start(bf16[1,96,4,8,128]{4,3,2,1,0:T(8,128)(2,1)} %param.6) | copy-start | bytes 2359300
  2.9 17.0 %collective-permute-start = (bf16[96,1024]{1,0:T(8,128)(2,1)}, bf16[96,1024]{1,0:T(8,128)(2,1)S(1)}, u32[]{:S(2)}, u32[]{:S(2)}) collective-permute-start(bf16[96,1024]{1,0:T(8,128)(2,1)} %get-tuple-element.43), channel_id=1, source_target_pairs={{0,4},{4,0},{8,12},{12,8},{16,20},{20,16},{24,28},{28,24},{1,5},{5... | collective-permute-start | bytes 589832 | tf_op jit(solution)/shard_map/ppermute | solution.py:435
  5.8 14.1 %collective-permute-start.1 = (bf16[96,1024]{1,0:T(8,128)(2,1)}, bf16[96,1024]{1,0:T(8,128)(2,1)S(1)}, u32[]{:S(2)}, u32[]{:S(2)}) collective-permute-start(bf16[96,1024]{1,0:T(8,128)(2,1)} %get-tuple-element.44), channel_id=1, source_target_pairs={{4,8},{12,16},{20,24},{8,4},{16,12},{24,20},{5,9},{13,17},{21,25},... | collective-permute-start | bytes 589832 | tf_op jit(solution)/shard_map/ppermute | solution.py:435
  6.5 7.1 %copy-start.3 = (bf16[2,96,3]{1,0,2:T(2,128)(2,1)S(1)}, bf16[2,96,3]{1,0,2:T(2,128)(2,1)}, u32[]{:S(2)}) copy-start(bf16[2,96,3]{1,0,2:T(2,128)(2,1)} %param.8) | copy-start | bytes 3460
  6.5 7.2 %copy-start.2 = (bf16[2,96,3,3]{1,0,3,2:T(2,128)(2,1)S(1)}, bf16[2,96,3,3]{1,0,3,2:T(2,128)(2,1)}, u32[]{:S(2)}) copy-start(bf16[2,96,3,3]{1,0,3,2:T(2,128)(2,1)} %param.7) | copy-start | bytes 10372
  7.2 6.6 %copy-start = (bf16[2,96,96]{2,1,0:T(8,128)(2,1)S(1)}, bf16[2,96,96]{2,1,0:T(8,128)(2,1)}, u32[]{:S(2)}) copy-start(bf16[2,96,96]{2,1,0:T(8,128)(2,1)} %mix.5) | copy-start | bytes 110596
  7.2 16.5 %collective-permute-start.3 = (bf16[96,1024]{1,0:T(8,128)(2,1)}, bf16[96,1024]{1,0:T(8,128)(2,1)S(1)}, u32[]{:S(2)}, u32[]{:S(2)}) collective-permute-start(bf16[96,1024]{1,0:T(8,128)(2,1)} %get-tuple-element.82), channel_id=1, source_target_pairs={{4,8},{12,16},{20,24},{8,4},{16,12},{24,20},{5,9},{13,17},{21,25},... | collective-permute-start | bytes 589832 | tf_op jit(solution)/shard_map/ppermute | solution.py:435
  8.0 15.7 %collective-permute-start.2 = (bf16[96,1024]{1,0:T(8,128)(2,1)S(1)}, bf16[96,1024]{1,0:T(8,128)(2,1)S(1)}, u32[]{:S(2)}, u32[]{:S(2)}) collective-permute-start(bf16[96,1024]{1,0:T(8,128)(2,1)S(1)} %get-tuple-element.83), channel_id=1, source_target_pairs={{0,4},{4,0},{8,12},{12,8},{16,20},{20,16},{24,28},{28,24},{1,5},{5... | collective-permute-start | bytes 589832 | tf_op jit(solution)/shard_map/ppermute | solution.py:435
  28.9 15.7 %collective-permute-start.7 = (bf16[96,2048]{1,0:T(8,128)(2,1)S(1)}, bf16[96,2048]{1,0:T(8,128)(2,1)S(1)}, u32[]{:S(2)}, u32[]{:S(2)}) collective-permute-start(bf16[96,2048]{1,0:T(8,128)(2,1)S(1)} %get-tuple-element.75), channel_id=1, source_target_pairs={{0,4},{4,0},{8,12},{12,8},{16,20},{20,16},{24,28},{28,24},{1,5},{5... | collective-permute-start | bytes 1179656 | tf_op jit(solution)/shard_map/ppermute | solution.py:435
  36.4 6.3 %collective-permute-start.6 = (bf16[224,128]{1,0:T(8,128)(2,1)S(1)}, bf16[224,128]{1,0:T(8,128)(2,1)S(1)}, u32[]{:S(2)}, u32[]{:S(2)}) collective-permute-start(bf16[224,128]{1,0:T(8,128)(2,1)S(1)} %get-tuple-element.74), channel_id=1, source_target_pairs={{0,24},{1,25},{2,26},{3,27},{4,28},{5,29},{6,30},{7,31},{8,16},{9,... | collective-permute-start | bytes 172040 | tf_op jit(solution)/shard_map/ppermute | solution.py:414
  37.8 5.7 %collective-permute-start.5 = (bf16[224,128]{1,0:T(8,128)(2,1)S(1)}, bf16[224,128]{1,0:T(8,128)(2,1)S(1)}, u32[]{:S(2)}, u32[]{:S(2)}) collective-permute-start(bf16[224,128]{1,0:T(8,128)(2,1)S(1)} %get-tuple-element.74), channel_id=1, source_target_pairs={{0,16},{1,17},{2,18},{3,19},{4,20},{5,21},{6,22},{7,23},{8,24},{9,... | collective-permute-start | bytes 172040 | tf_op jit(solution)/shard_map/ppermute | solution.py:414
  39.4 5.1 %collective-permute-start.4 = (bf16[224,128]{1,0:T(8,128)(2,1)S(1)}, bf16[224,128]{1,0:T(8,128)(2,1)S(1)}, u32[]{:S(2)}, u32[]{:S(2)}) collective-permute-start(bf16[224,128]{1,0:T(8,128)(2,1)S(1)} %get-tuple-element.74), channel_id=1, source_target_pairs={{0,8},{1,9},{2,10},{3,11},{4,12},{5,13},{6,14},{7,15},{8,0},{9,1},... | collective-permute-start | bytes 172040 | tf_op jit(solution)/shard_map/ppermute | solution.py:414
  40.9 10.9 %collective-permute-start.8 = (bf16[96,2048]{1,0:T(8,128)(2,1)S(1)}, bf16[96,2048]{1,0:T(8,128)(2,1)S(1)}, u32[]{:S(2)}, u32[]{:S(2)}) collective-permute-start(bf16[96,2048]{1,0:T(8,128)(2,1)S(1)} %get-tuple-element.77), channel_id=1, source_target_pairs={{4,8},{12,16},{20,24},{8,4},{16,12},{24,20},{5,9},{13,17},{21,25},... | collective-permute-start | bytes 1179656 | tf_op jit(solution)/shard_map/ppermute | solution.py:435
  44.6 4.2 %collective-permute-start.11 = (bf16[224,128]{1,0:T(8,128)(2,1)S(1)}, bf16[224,128]{1,0:T(8,128)(2,1)S(1)}, u32[]{:S(2)}, u32[]{:S(2)}) collective-permute-start(bf16[224,128]{1,0:T(8,128)(2,1)S(1)} %add_convert_fusion.1), channel_id=1, source_target_pairs={{0,3},{1,2},{2,1},{3,0},{4,7},{5,6},{6,5},{7,4},{8,11},{9,10},{10,... | collective-permute-start | bytes 172040 | tf_op jit(solution)/shard_map/ppermute | solution.py:414
  44.6 5.4 %collective-permute-start.10 = (bf16[224,128]{1,0:T(8,128)(2,1)S(1)}, bf16[224,128]{1,0:T(8,128)(2,1)S(1)}, u32[]{:S(2)}, u32[]{:S(2)}) collective-permute-start(bf16[224,128]{1,0:T(8,128)(2,1)S(1)} %add_convert_fusion.1), channel_id=1, source_target_pairs={{0,2},{1,3},{2,0},{3,1},{4,6},{5,7},{6,4},{7,5},{8,10},{9,11},{10,... | collective-permute-start | bytes 172040 | tf_op jit(solution)/shard_map/ppermute | solution.py:414
  46.2 3.9 %collective-permute-start.9 = (bf16[224,128]{1,0:T(8,128)(2,1)S(1)}, bf16[224,128]{1,0:T(8,128)(2,1)S(1)}, u32[]{:S(2)}, u32[]{:S(2)}) collective-permute-start(bf16[224,128]{1,0:T(8,128)(2,1)S(1)} %add_convert_fusion.1), channel_id=1, source_target_pairs={{0,1},{1,0},{2,3},{3,2},{4,5},{5,4},{6,7},{7,6},{8,9},{9,8},{10,11... | collective-permute-start | bytes 172040 | tf_op jit(solution)/shard_map/ppermute | solution.py:414
  50.1 4.2 %collective-permute-start.12 = (bf16[224,128]{1,0:T(8,128)(2,1)S(1)}, bf16[224,128]{1,0:T(8,128)(2,1)S(1)}, u32[]{:S(2)}, u32[]{:S(2)}) collective-permute-start(bf16[224,128]{1,0:T(8,128)(2,1)S(1)} %add_convert_fusion.refs_0_), channel_id=1, source_target_pairs={{0,4},{1,5},{2,6},{3,7},{4,0},{5,1},{6,2},{7,3},{8,12},{9,13},{10,... | collective-permute-start | bytes 172040 | tf_op jit(solution)/shard_map/ppermute | solution.py:414

commit v8 on v7

--- a/solution.py
+++ b/solution.py
@@ -222,6 +222,19 @@
         )
         total = term if total is None else total + term
     return total
+
+
+def rim_kernel(low, high, vol, first, second, plane_a, plane_b, arrived):
+    odd = lax.rem(lax.axis_index("sp"), 2) != 0
+    copies = [
+        pltpu.make_async_copy(vol.at[0, :, jnp.where(odd, low, high)], plane_a, arrived.at[0]),
+        pltpu.make_async_copy(vol.at[0, :, jnp.where(odd, high, low)], plane_b, arrived.at[1]),
+    ]
+    for copy in copies:
+        copy.start()
+    for copy, plane, out in zip(copies, (plane_a, plane_b), (first, second)):
+        copy.wait()
+        out[...] = plane[...].astype(F32).reshape(out.shape).astype(BF16)
 
 
 def sort_sides(odd, first, second, low, high):
@@ -426,19 +439,26 @@
     firsts = [(i, i ^ 1) for i in range(ranks)]
     seconds = [(i, i + 1) for i in range(1, ranks - 1, 2)] + [(i + 1, i) for i in range(1, ranks - 1, 2)]
 
-    def rims(slab_planes, low, high):
-        low = slab_planes[:, low * plane : (low + 1) * plane]
-        high = slab_planes[:, high * plane : (high + 1) * plane]
-        return jnp.where(odd != 0, low, high), jnp.where(odd != 0, high, low)
+    def rims(volume, low, high, cost):
+        return pl.pallas_call(
+            functools.partial(rim_kernel, low, high),
+            name="rims",
+            out_shape=[jax.ShapeDtypeStruct((channels, plane), BF16)] * 2,
+            in_specs=[pl.BlockSpec(memory_space=pl.ANY)],
+            out_specs=[pl.BlockSpec(memory_space=pltpu.VMEM)] * 2,
+            scratch_shapes=[pltpu.VMEM((channels, nz, ny), BF16)] * 2 + [pltpu.SemaphoreType.DMA((2,))],
+            compiler_params=pltpu.CompilerParams(vmem_limit_bytes=16 << 20),
+            cost_estimate=pl.CostEstimate(flops=0, bytes_accessed=cost, transcendentals=0),
+        )(volume)
 
     def exchange(sent):
         return lax.ppermute(sent[0], "sp", firsts), lax.ppermute(sent[1], "sp", seconds)
 
-    vol = lax.optimization_barrier(volume[0].reshape(channels, -1))
-    near = rims(vol, 0, slab - 1)
-    later, *near = lax.optimization_barrier((vol, *near))
-    near = exchange(near)
-    far = exchange(rims(later, 1, slab - 2))
+    near = rims(volume, 0, slab - 1, 1)
+    later, *near = lax.optimization_barrier((volume, *near))
+    far = rims(later, 1, slab - 2, 3 << 20)
+    near, far = exchange(near), exchange(far)
+    vol = volume[0].reshape(channels, -1)
     cot = cotangent[0].reshape(channels, -1)
     taps = wide_taps(kernels_xy, kernels_z, ny)
     mix, mix_t = mixing, jnp.swapaxes(mixing, 1, 2)

time: 55.2 us -> 54.4 us (0.986)
  local copies, waits for them, and re-layouts: 3.11 us -> 4.84 us
  other arithmetic: 2.34 us -> 0.87 us
  starting transfers between devices: 20 us -> 19 us
  waiting for transfers between devices: 10.7 us -> 9.98 us
  Pallas kernels: 18 us -> 18.6 us
    unnamed x10 -> x12, local copies, waits for them, and re-layouts: 1.16 us -> 2.9 us
    select_n x2 -> x0, other arithmetic: 1.47 us -> none  [rims(): return (jnp.where(odd != 0, low, high), jnp.where(odd != 0, high, low))]
    another operation x1, local copies, waits for them, and re-layouts: 0.33 us -> 1.43 us  [on_device(): cot = cotangent[0].reshape(channels, -1)]
    another operation x1, local copies, waits for them, and re-layouts: 1.43 us -> 0.33 us  [on_device(): vol = volume[0].reshape(channels, -1)]
    ppermute x3, starting transfers between devices: 11 us -> 9.92 us  [exchange(): lax.ppermute(sent[0], 'sp', firsts)]
    ppermute x3, waiting for transfers between devices: 3.61 us -> 3.02 us  [exchange(): lax.ppermute(sent[0], 'sp', firsts)]
  transfers between devices with their start and end apart: 13 -> 13, of which waited for: 7 -> 7; matrix products, arithmetic and copies ran while one was open for 6% -> 7% of each run, Pallas kernels for 22% -> 23%
where the time goes in v8:
time: 54.4 us; the launch traced here: 54.1 us
  starting transfers between devices  19 us (35%)
  Pallas kernels  18.6 us (34%)
  waiting for transfers between devices  9.98 us (18%)
  local copies, waits for them, and re-layouts  4.84 us (9%)
  between operations  0.91 us (2%)
  other arithmetic  0.87 us (2%)
    pallas_call x7, Pallas kernels, call(): pl.pallas_call(kernel, name=name, out_shape=outputs, in_specs=[smem] * sc...  18 us
    ppermute x3, starting transfers between devices, exchange(): lax.ppermute(sent[0], 'sp', firsts)  9.92 us
    ppermute x7, starting transfers between devices, all_sum(): lax.ppermute(mine, ('sp', 'dp'), [(i, i ^ step) for i in places])  7.04 us
    ppermute x7, waiting for transfers between devices, all_sum(): lax.ppermute(mine, ('sp', 'dp'), [(i, i ^ step) for i in places])  6.96 us
    ppermute x3, waiting for transfers between devices, exchange(): lax.ppermute(sent[0], 'sp', firsts)  3.02 us
    unnamed x12, local copies, waits for them, and re-layouts  2.9 us
    ppermute x3, starting transfers between devices, exchange(): lax.ppermute(sent[1], 'sp', seconds)  2 us
    another operation x1, local copies, waits for them, and re-layouts, on_device(): cot = cotangent[0].reshape(channels, -1)  1.43 us
  transfers between devices with their start and end apart: 13, of which 7 were waited for; matrix products, arithmetic and copies ran while one was open for 7% of the time, Pallas kernels for 23%

profile of v8, /device:TPU:0, one launch (start us, length us, event | category | flops | bytes accessed | tf_op | source)
XLA Modules:
  0.0 54.1 jit_solution(2599891589446390706)
XLA Ops:
  0.6 1.1 %copy-done = bf16[1,96,4,8,128]{4,3,2,1,0:T(8,128)(2,1)S(1)} copy-done((bf16[1,96,4,8,128]{4,3,2,1,0:T(8,128)(2,1)S(1)}, bf16[1,96,4,8,128]{4,3,2,1,0:T(8,128)(2,1)}, u32[]{:S(2)}) %copy-start) | copy-done | bytes 786456
  2.0 3.0 %collective-permute-start = (bf16[96,1024]{1,0:T(8,128)(2,1)S(1)}, bf16[96,1024]{1,0:T(8,128)(2,1)S(1)}, u32[]{:S(2)}, u32[]{:S(2)}) collective-permute-start(bf16[96,1024]{1,0:T(8,128)(2,1)S(1)} %get-tuple-element.49), channel_id=1, source_target_pairs={{0,4},{4,0},{8,12},{12,8},{16,20},{20,16},{24,28},{28,24},{1,5},{5... | collective-permute-start | bytes 589832 | tf_op jit(solution)/shard_map/ppermute | solution.py:455
  6.0 4.3 %collective-permute-start.2 = (bf16[96,1024]{1,0:T(8,128)(2,1)S(1)}, bf16[96,1024]{1,0:T(8,128)(2,1)S(1)}, u32[]{:S(2)}, u32[]{:S(2)}) collective-permute-start(bf16[96,1024]{1,0:T(8,128)(2,1)S(1)} %get-tuple-element.55), channel_id=1, source_target_pairs={{0,4},{4,0},{8,12},{12,8},{16,20},{20,16},{24,28},{28,24},{1,5},{5... | collective-permute-start | bytes 589832 | tf_op jit(solution)/shard_map/ppermute | solution.py:455
  12.4 1.4 %reshape_squeeze.7.cot = bf16[96,4096]{1,0:T(8,128)(2,1)S(1)} reshape(bf16[1,96,4,8,128]{4,3,2,1,0:T(8,128)(2,1)} %param.6) | data formatting | bytes 1572864 | tf_op jit(solution)/shard_map/reshape;squeeze | solution.py:462
  14.6 1.1 %inner.1 = (bf16[96,2048]{1,0:T(8,128)(2,1)S(1)}, bf16[96,2048]{1,0:T(8,128)(2,1)S(1)}, bf16[96,2048]{1,0:T(8,128)(2,1)S(1)}, bf16[96,2048]{1,0:T(8,128)(2,1)S(1)}) custom-call(bf16[96,4096]{1,0:T(8,128)(2,1)S(1)} %reshape_squeeze.6.vol, bf16[2,21,96,128]{3,2,1,0:T(8,128)(2,1)S(1)} %pad_maximum_fusion.taps, bf16[2,96,96]{2,1,0:T(8,128)(2,1)S(1)} %copy-done.2), custom_call_target="tpu_custom_call" | custom-call | bytes 4194304 | tf_op jit(solution)/shard_map/inner/pallas_call | solution.py:393
  15.8 3.0 %collective-permute-done.first = bf16[96,1024]{1,0:T(8,128)(2,1)S(1)} collective-permute-done((bf16[96,1024]{1,0:T(8,128)(2,1)S(1)}, bf16[96,1024]{1,0:T(8,128)(2,1)S(1)}, u32[]{:S(2)}, u32[]{:S(2)}) %collective-permute-start) | collective-permute-done | bytes 196640 | tf_op jit(solution)/shard_map/ppermute | solution.py:455
  18.8 3.8 %middle.1 = (bf16[96,1024]{1,0:T(8,128)(2,1)S(1)}, bf16[96,1024]{1,0:T(8,128)(2,1)S(1)}, bf16[96,2048]{1,0:T(8,128)(2,1)S(1)}, bf16[96,2048]{1,0:T(8,128)(2,1)S(...) custom-call(s32[1]{0:T(128)} %bitcast.odd, ...), custom_call_target="tpu_custom_call" | custom-call | bytes 12582912 | tf_op jit(solution)/shard_map/middle/pallas_call | solution.py:393
  22.7 5.2 %edge.1 = (bf16[96,1024]{1,0:T(8,128)(2,1)S(1)}, bf16[96,1024]{1,0:T(8,128)(2,1)S(1)}, bf16[96,2048]{1,0:T(8,128)(2,1)S(1)}, bf16[96,2048]{1,0:T(8,128)(2,1)S(1)...) custom-call(s32[1]{0:T(128)} %bitcast.odd, ...), custom_call_target="tpu_custom_call" | custom-call | bytes 18874368 | tf_op jit(solution)/shard_map/edge/pallas_call | solution.py:393
  27.9 2.6 %collective-permute-start.7 = (bf16[96,2048]{1,0:T(8,128)(2,1)S(1)}, bf16[96,2048]{1,0:T(8,128)(2,1)S(1)}, u32[]{:S(2)}, u32[]{:S(2)}) collective-permute-start(bf16[96,2048]{1,0:T(8,128)(2,1)S(1)} %get-tuple-element.83), channel_id=1, source_target_pairs={{0,4},{4,0},{8,12},{12,8},{16,20},{20,16},{24,28},{28,24},{1,5},{5... | collective-permute-start | bytes 1179656 | tf_op jit(solution)/shard_map/ppermute | solution.py:455
  30.4 5.0 %weights.1 = (bf16[96,2048]{1,0:T(8,128)(2,1)S(1)}, bf16[224,128]{1,0:T(8,128)(2,1)S(1)}) custom-call(bf16[96,4096]{1,0:T(8,128)(2,1)S(1)} %reshape_squeeze.6.vol, bf16[96,1024]{1,0:T(8,128)(2,1)S(1)} %get-tuple-element.52.lo1, bf16[96,1024]{1,0:T(8,128)(2,1)S(1)} %get-tuple-element.53.hi1, bf16[96,1024]{1,0:T(8,128)(2,1)S(1)} %get-tuple-element.60.lo2, ...), custom_call_target="tpu_custom_call" | custom-call | bytes 1 | tf_op jit(solution)/shard_map/weights/pallas_call | solution.py:393
  35.5 1.6 %collective-permute-start.6 = (bf16[224,128]{1,0:T(8,128)(2,1)S(1)}, bf16[224,128]{1,0:T(8,128)(2,1)S(1)}, u32[]{:S(2)}, u32[]{:S(2)}) collective-permute-start(bf16[224,128]{1,0:T(8,128)(2,1)S(1)} %get-tuple-element.82), channel_id=1, source_target_pairs={{0,24},{1,25},{2,26},{3,27},{4,28},{5,29},{6,30},{7,31},{8,16},{9,... | collective-permute-start | bytes 172040 | tf_op jit(solution)/shard_map/ppermute | solution.py:427
  37.1 1.4 %collective-permute-start.5 = (bf16[224,128]{1,0:T(8,128)(2,1)S(1)}, bf16[224,128]{1,0:T(8,128)(2,1)S(1)}, u32[]{:S(2)}, u32[]{:S(2)}) collective-permute-start(bf16[224,128]{1,0:T(8,128)(2,1)S(1)} %get-tuple-element.82), channel_id=1, source_target_pairs={{0,16},{1,17},{2,18},{3,19},{4,20},{5,21},{6,22},{7,23},{8,24},{9,... | collective-permute-start | bytes 172040 | tf_op jit(solution)/shard_map/ppermute | solution.py:427
  38.5 1.5 %collective-permute-start.4 = (bf16[224,128]{1,0:T(8,128)(2,1)S(1)}, bf16[224,128]{1,0:T(8,128)(2,1)S(1)}, u32[]{:S(2)}, u32[]{:S(2)}) collective-permute-start(bf16[224,128]{1,0:T(8,128)(2,1)S(1)} %get-tuple-element.82), channel_id=1, source_target_pairs={{0,8},{1,9},{2,10},{3,11},{4,12},{5,13},{6,14},{7,15},{8,0},{9,1},... | collective-permute-start | bytes 172040 | tf_op jit(solution)/shard_map/ppermute | solution.py:427
  39.9 0.7 %collective-permute-start.8 = (bf16[96,2048]{1,0:T(8,128)(2,1)S(1)}, bf16[96,2048]{1,0:T(8,128)(2,1)S(1)}, u32[]{:S(2)}, u32[]{:S(2)}) collective-permute-start(bf16[96,2048]{1,0:T(8,128)(2,1)S(1)} %get-tuple-element.85), channel_id=1, source_target_pairs={{4,8},{12,16},{20,24},{8,4},{16,12},{24,20},{5,9},{13,17},{21,25},... | collective-permute-start | bytes 1179656 | tf_op jit(solution)/shard_map/ppermute | solution.py:455
  40.6 1.5 %collective-permute-done.6 = bf16[224,128]{1,0:T(8,128)(2,1)S(1)} collective-permute-done((bf16[224,128]{1,0:T(8,128)(2,1)S(1)}, bf16[224,128]{1,0:T(8,128)(2,1)S(1)}, u32[]{:S(2)}, u32[]{:S(2)}) %collective-permute-start.6) | collective-permute-done | bytes 57376 | tf_op jit(solution)/shard_map/ppermute | solution.py:427
  42.5 1.2 %collective-permute-done.4 = bf16[224,128]{1,0:T(8,128)(2,1)S(1)} collective-permute-done((bf16[224,128]{1,0:T(8,128)(2,1)S(1)}, bf16[224,128]{1,0:T(8,128)(2,1)S(1)}, u32[]{:S(2)}, u32[]{:S(2)}) %collective-permute-start.4) | collective-permute-done | bytes 57376 | tf_op jit(solution)/shard_map/ppermute | solution.py:427
  43.8 1.5 %collective-permute-start.10 = (bf16[224,128]{1,0:T(8,128)(2,1)S(1)}, bf16[224,128]{1,0:T(8,128)(2,1)S(1)}, u32[]{:S(2)}, u32[]{:S(2)}) collective-permute-start(bf16[224,128]{1,0:T(8,128)(2,1)S(1)} %add_convert_fusion.1), channel_id=1, source_target_pairs={{0,2},{1,3},{2,0},{3,1},{4,6},{5,7},{6,4},{7,5},{8,10},{9,11},{10,... | collective-permute-start | bytes 172040 | tf_op jit(solution)/shard_map/ppermute | solution.py:427
  45.6 2.4 %collective-permute-done.11 = bf16[224,128]{1,0:T(8,128)(2,1)S(1)} collective-permute-done((bf16[224,128]{1,0:T(8,128)(2,1)S(1)}, bf16[224,128]{1,0:T(8,128)(2,1)S(1)}, u32[]{:S(2)}, u32[]{:S(2)}) %collective-permute-start.11) | collective-permute-done | bytes 57376 | tf_op jit(solution)/shard_map/ppermute | solution.py:427
  48.0 1.2 %collective-permute-done.10 = bf16[224,128]{1,0:T(8,128)(2,1)S(1)} collective-permute-done((bf16[224,128]{1,0:T(8,128)(2,1)S(1)}, bf16[224,128]{1,0:T(8,128)(2,1)S(1)}, u32[]{:S(2)}, u32[]{:S(2)}) %collective-permute-start.10) | collective-permute-done | bytes 57376 | tf_op jit(solution)/shard_map/ppermute | solution.py:427
  49.2 0.7 %collective-permute-start.12 = (bf16[224,128]{1,0:T(8,128)(2,1)S(1)}, bf16[224,128]{1,0:T(8,128)(2,1)S(1)}, u32[]{:S(2)}, u32[]{:S(2)}) collective-permute-start(bf16[224,128]{1,0:T(8,128)(2,1)S(1)} %add_convert_fusion.refs_0_), channel_id=1, source_target_pairs={{0,4},{1,5},{2,6},{3,7},{4,0},{5,1},{6,2},{7,3},{8,12},{9,13},{10,... | collective-permute-start | bytes 172040 | tf_op jit(solution)/shard_map/ppermute | solution.py:427
  49.9 1.1 %volume.1.own = bf16[96,4096]{1,0:T(8,128)(2,1)S(1)} custom-call(bf16[2,21,96,128]{3,2,1,0:T(8,128)(2,1)S(1)} %pad_maximum_fusion.taps, bf16[96,2048]{1,0:T(8,128)(2,1)S(1)} %get-tuple-element.81.gpl1_i, bf16[96,2048]{1,0:T(8,128)(2,1)S(1)} %get-tuple-element.79.gpl1_lo, bf16[96,2048]{1,0:T(8,128)(2,1)S(1)} %get-tuple-element.80.gpl1_hi), custom_call_target="tpu_custom_call" | custom-call | bytes 1 | tf_op jit(solution)/shard_map/volume/pallas_call | solution.py:393
  51.1 1.0 %final.1 = bf16[96,4096]{1,0:T(8,128)(2,1)S(1)} custom-call(s32[1]{0:T(128)} %bitcast.odd, bf16[2,21,96,128]{3,2,1,0:T(8,128)(2,1)S(1)} %pad_maximum_fusion.taps, bf16[96,4096]{1,0:T(8,128)(2,1)S(1)} %volume.1.own, bf16[96,2048]{1,0:T(8,128)(2,1)S(1)} %collective-permute-done.7.first, bf16[96,2048]{1,0:T(8,128)(2,1)S(1)} %collective-permute-done.8.second), custom_call_target="tpu_custom_call" | custom-call | bytes 1 | tf_op jit(solution)/shard_map/final/pallas_call | solution.py:393
  52.1 1.0 %copy.12 = bf16[12,8,32,128]{3,2,1,0:T(8,128)(2,1)} copy(bf16[12,8,32,128]{3,1,2,0:T(8,128)(2,1)S(1)} %bitcast.18) | data formatting | bytes 1572864
  53.5 0.7 %result.1 = (f32[2,96,96]{2,1,0:T(8,128)}, f32[9,2,96]{2,1,0:T(2,128)}, f32[3,2,96]{2,1,0:T(2,128)}) custom-call(bf16[224,128]{1,0:T(8,128)(2,1)S(1)} %add_convert_fusion.refs_0_, bf16[224,128]{1,0:T(8,128)(2,1)S(1)} %collective-permute-done.12.refs_1_), custom_call_target="tpu_custom_call" | custom-call | bytes 1 | tf_op jit(solution)/shard_map/result/pallas_call | solution.py:393
  (40 shorter events, 5.1 us)
Async XLA Ops:
  0.6 1.1 %copy-start = (bf16[1,96,4,8,128]{4,3,2,1,0:T(8,128)(2,1)S(1)}, bf16[1,96,4,8,128]{4,3,2,1,0:T(8,128)(2,1)}, u32[]{:S(2)}) copy-start(bf16[1,96,4,8,128]{4,3,2,1,0:T(8,128)(2,1)} %vol.2) | copy-start | bytes 2359300
  1.8 9.3 %copy-start.1 = (bf16[1,96,4,8,128]{4,3,2,1,0:T(8,128)(2,1)S(1)}, bf16[1,96,4,8,128]{4,3,2,1,0:T(8,128)(2,1)}, u32[]{:S(2)}) copy-start(bf16[1,96,4,8,128]{4,3,2,1,0:T(8,128)(2,1)} %vol.2) | copy-start | bytes 2359300
  2.0 16.8 %collective-permute-start = (bf16[96,1024]{1,0:T(8,128)(2,1)S(1)}, bf16[96,1024]{1,0:T(8,128)(2,1)S(1)}, u32[]{:S(2)}, u32[]{:S(2)}) collective-permute-start(bf16[96,1024]{1,0:T(8,128)(2,1)S(1)} %get-tuple-element.49), channel_id=1, source_target_pairs={{0,4},{4,0},{8,12},{12,8},{16,20},{20,16},{24,28},{28,24},{1,5},{5... | collective-permute-start | bytes 589832 | tf_op jit(solution)/shard_map/ppermute | solution.py:455
  5.1 13.7 %collective-permute-start.1 = (bf16[96,1024]{1,0:T(8,128)(2,1)S(1)}, bf16[96,1024]{1,0:T(8,128)(2,1)S(1)}, u32[]{:S(2)}, u32[]{:S(2)}) collective-permute-start(bf16[96,1024]{1,0:T(8,128)(2,1)S(1)} %get-tuple-element.50), channel_id=1, source_target_pairs={{4,8},{12,16},{20,24},{8,4},{16,12},{24,20},{5,9},{13,17},{21,25},... | collective-permute-start | bytes 589832 | tf_op jit(solution)/shard_map/ppermute | solution.py:455
  6.0 16.6 %collective-permute-start.2 = (bf16[96,1024]{1,0:T(8,128)(2,1)S(1)}, bf16[96,1024]{1,0:T(8,128)(2,1)S(1)}, u32[]{:S(2)}, u32[]{:S(2)}) collective-permute-start(bf16[96,1024]{1,0:T(8,128)(2,1)S(1)} %get-tuple-element.55), channel_id=1, source_target_pairs={{0,4},{4,0},{8,12},{12,8},{16,20},{20,16},{24,28},{28,24},{1,5},{5... | collective-permute-start | bytes 589832 | tf_op jit(solution)/shard_map/ppermute | solution.py:455
  10.4 12.3 %collective-permute-start.3 = (bf16[96,1024]{1,0:T(8,128)(2,1)S(1)}, bf16[96,1024]{1,0:T(8,128)(2,1)S(1)}, u32[]{:S(2)}, u32[]{:S(2)}) collective-permute-start(bf16[96,1024]{1,0:T(8,128)(2,1)S(1)} %get-tuple-element.56), channel_id=1, source_target_pairs={{4,8},{12,16},{20,24},{8,4},{16,12},{24,20},{5,9},{13,17},{21,25},... | collective-permute-start | bytes 589832 | tf_op jit(solution)/shard_map/ppermute | solution.py:455
  11.1 0.7 %copy-start.4 = (bf16[2,96,3]{1,0,2:T(2,128)(2,1)S(1)}, bf16[2,96,3]{1,0,2:T(2,128)(2,1)}, u32[]{:S(2)}) copy-start(bf16[2,96,3]{1,0,2:T(2,128)(2,1)} %param.8) | copy-start | bytes 3460
  11.1 0.8 %copy-start.3 = (bf16[2,96,3,3]{1,0,3,2:T(2,128)(2,1)S(1)}, bf16[2,96,3,3]{1,0,3,2:T(2,128)(2,1)}, u32[]{:S(2)}) copy-start(bf16[2,96,3,3]{1,0,3,2:T(2,128)(2,1)} %param.7) | copy-start | bytes 10372
  11.4 0.8 %copy-start.2 = (bf16[2,96,96]{2,1,0:T(8,128)(2,1)S(1)}, bf16[2,96,96]{2,1,0:T(8,128)(2,1)}, u32[]{:S(2)}) copy-start(bf16[2,96,96]{2,1,0:T(8,128)(2,1)} %mix.5) | copy-start | bytes 110596
  27.9 15.8 %collective-permute-start.7 = (bf16[96,2048]{1,0:T(8,128)(2,1)S(1)}, bf16[96,2048]{1,0:T(8,128)(2,1)S(1)}, u32[]{:S(2)}, u32[]{:S(2)}) collective-permute-start(bf16[96,2048]{1,0:T(8,128)(2,1)S(1)} %get-tuple-element.83), channel_id=1, source_target_pairs={{0,4},{4,0},{8,12},{12,8},{16,20},{20,16},{24,28},{28,24},{1,5},{5... | collective-permute-start | bytes 1179656 | tf_op jit(solution)/shard_map/ppermute | solution.py:455
  35.5 6.7 %collective-permute-start.6 = (bf16[224,128]{1,0:T(8,128)(2,1)S(1)}, bf16[224,128]{1,0:T(8,128)(2,1)S(1)}, u32[]{:S(2)}, u32[]{:S(2)}) collective-permute-start(bf16[224,128]{1,0:T(8,128)(2,1)S(1)} %get-tuple-element.82), channel_id=1, source_target_pairs={{0,24},{1,25},{2,26},{3,27},{4,28},{5,29},{6,30},{7,31},{8,16},{9,... | collective-permute-start | bytes 172040 | tf_op jit(solution)/shard_map/ppermute | solution.py:427
  37.1 5.4 %collective-permute-start.5 = (bf16[224,128]{1,0:T(8,128)(2,1)S(1)}, bf16[224,128]{1,0:T(8,128)(2,1)S(1)}, u32[]{:S(2)}, u32[]{:S(2)}) collective-permute-start(bf16[224,128]{1,0:T(8,128)(2,1)S(1)} %get-tuple-element.82), channel_id=1, source_target_pairs={{0,16},{1,17},{2,18},{3,19},{4,20},{5,21},{6,22},{7,23},{8,24},{9,... | collective-permute-start | bytes 172040 | tf_op jit(solution)/shard_map/ppermute | solution.py:427
  38.5 5.2 %collective-permute-start.4 = (bf16[224,128]{1,0:T(8,128)(2,1)S(1)}, bf16[224,128]{1,0:T(8,128)(2,1)S(1)}, u32[]{:S(2)}, u32[]{:S(2)}) collective-permute-start(bf16[224,128]{1,0:T(8,128)(2,1)S(1)} %get-tuple-element.82), channel_id=1, source_target_pairs={{0,8},{1,9},{2,10},{3,11},{4,12},{5,13},{6,14},{7,15},{8,0},{9,1},... | collective-permute-start | bytes 172040 | tf_op jit(solution)/shard_map/ppermute | solution.py:427
  39.9 11.1 %collective-permute-start.8 = (bf16[96,2048]{1,0:T(8,128)(2,1)S(1)}, bf16[96,2048]{1,0:T(8,128)(2,1)S(1)}, u32[]{:S(2)}, u32[]{:S(2)}) collective-permute-start(bf16[96,2048]{1,0:T(8,128)(2,1)S(1)} %get-tuple-element.85), channel_id=1, source_target_pairs={{4,8},{12,16},{20,24},{8,4},{16,12},{24,20},{5,9},{13,17},{21,25},... | collective-permute-start | bytes 1179656 | tf_op jit(solution)/shard_map/ppermute | solution.py:455
  43.7 4.3 %collective-permute-start.11 = (bf16[224,128]{1,0:T(8,128)(2,1)S(1)}, bf16[224,128]{1,0:T(8,128)(2,1)S(1)}, u32[]{:S(2)}, u32[]{:S(2)}) collective-permute-start(bf16[224,128]{1,0:T(8,128)(2,1)S(1)} %add_convert_fusion.1), channel_id=1, source_target_pairs={{0,3},{1,2},{2,1},{3,0},{4,7},{5,6},{6,5},{7,4},{8,11},{9,10},{10,... | collective-permute-start | bytes 172040 | tf_op jit(solution)/shard_map/ppermute | solution.py:427
  43.8 5.4 %collective-permute-start.10 = (bf16[224,128]{1,0:T(8,128)(2,1)S(1)}, bf16[224,128]{1,0:T(8,128)(2,1)S(1)}, u32[]{:S(2)}, u32[]{:S(2)}) collective-permute-start(bf16[224,128]{1,0:T(8,128)(2,1)S(1)} %add_convert_fusion.1), channel_id=1, source_target_pairs={{0,2},{1,3},{2,0},{3,1},{4,6},{5,7},{6,4},{7,5},{8,10},{9,11},{10,... | collective-permute-start | bytes 172040 | tf_op jit(solution)/shard_map/ppermute | solution.py:427
  45.3 3.9 %collective-permute-start.9 = (bf16[224,128]{1,0:T(8,128)(2,1)S(1)}, bf16[224,128]{1,0:T(8,128)(2,1)S(1)}, u32[]{:S(2)}, u32[]{:S(2)}) collective-permute-start(bf16[224,128]{1,0:T(8,128)(2,1)S(1)} %add_convert_fusion.1), channel_id=1, source_target_pairs={{0,1},{1,0},{2,3},{3,2},{4,5},{5,4},{6,7},{7,6},{8,9},{9,8},{10,11... | collective-permute-start | bytes 172040 | tf_op jit(solution)/shard_map/ppermute | solution.py:427
  49.2 4.2 %collective-permute-start.12 = (bf16[224,128]{1,0:T(8,128)(2,1)S(1)}, bf16[224,128]{1,0:T(8,128)(2,1)S(1)}, u32[]{:S(2)}, u32[]{:S(2)}) collective-permute-start(bf16[224,128]{1,0:T(8,128)(2,1)S(1)} %add_convert_fusion.refs_0_), channel_id=1, source_target_pairs={{0,4},{1,5},{2,6},{3,7},{4,0},{5,1},{6,2},{7,3},{8,12},{9,13},{10,... | collective-permute-start | bytes 172040 | tf_op jit(solution)/shard_map/ppermute | solution.py:427

commit v9 on v8

--- a/solution.py
+++ b/solution.py
@@ -181,30 +181,33 @@
 
     def body(rows):
         lane = lax.broadcasted_iota(jnp.int32, (GROUP, ny), 1)
-        sums = [None] * 12
-
-        def add(tap, term):
-            sums[tap] = term if sums[tap] is None else sums[tap] + term
-
+        sums = [None] * 12 if before is None else [before[t, rows, :] for t in range(12)]
         for index in indices:
+            part = [None] * 12
+
+            def add(tap, term):
+                part[tap] = term if part[tap] is None else part[tap] + term
+
             for z in range(nz):
-                grad = grad_planar.get(index, z, rows)
+                grad = grad_planar.tile(index, z, rows)[...]
                 shifted = (pltpu.roll(grad, ny - 1, 1), grad, pltpu.roll(grad, 1, 1))
                 for i in range(3):
                     if index + i - 1 in source:
-                        value = source.get(index + i - 1, z, rows)
+                        value = source.tile(index + i - 1, z, rows)[...]
                         for j in range(3):
                             add(3 * i + j, shifted[j] * value)
-                grad = grad_axial.get(index, z, rows)
+                grad = grad_axial.tile(index, z, rows)[...]
                 for t in range(3):
                     if 0 <= z + t - 1 < nz:
-                        add(9 + t, grad * planar.get(index, z + t - 1, rows))
+                        add(9 + t, grad * planar.tile(index, z + t - 1, rows)[...])
+            for t in range(12):
+                if part[t] is not None:
+                    term = part[t].astype(F32)
+                    sums[t] = term if sums[t] is None else sums[t] + term
         for i in range(3):
             sums[3 * i] = jnp.where(lane != ny - 1, sums[3 * i], 0.0)
             sums[3 * i + 2] = jnp.where(lane != 0, sums[3 * i + 2], 0.0)
         for t in range(12):
-            if before is not None:
-                sums[t] = sums[t] + before[t, rows, :]
             sums_ref[t, rows, :] = sums[t]
 
     over_groups(source.channels, body)

time: 54.4 us -> 53.5 us (0.983)
  Pallas kernels: 18.6 us -> 17.4 us
    pallas_call x7, Pallas kernels: 18 us -> 16.9 us  [call(): pl.pallas_call(kernel, name=name, out_shape=outputs, in_specs=[smem] * sc...]
  transfers between devices with their start and end apart: 13 -> 13, of which waited for: 7 -> 7; matrix products, arithmetic and copies ran while one was open for 7% -> 7% of each run, Pallas kernels for 23% -> 21%
where the time goes in v9:
time: 53.5 us; the launch traced here: 53.2 us
  starting transfers between devices  18.7 us (35%)
  Pallas kernels  17.4 us (33%)
  waiting for transfers between devices  10.3 us (19%)
  local copies, waits for them, and re-layouts  4.84 us (9%)
  between operations  0.91 us (2%)
  other arithmetic  0.87 us (2%)
    pallas_call x7, Pallas kernels, call(): pl.pallas_call(kernel, name=name, out_shape=outputs, in_specs=[smem] * sc...  16.9 us
    ppermute x3, starting transfers between devices, exchange(): lax.ppermute(sent[0], 'sp', firsts)  9.92 us
    ppermute x7, waiting for transfers between devices, all_sum(): lax.ppermute(mine, ('sp', 'dp'), [(i, i ^ step) for i in places])  7.31 us
    ppermute x7, starting transfers between devices, all_sum(): lax.ppermute(mine, ('sp', 'dp'), [(i, i ^ step) for i in places])  6.83 us
    ppermute x3, waiting for transfers between devices, exchange(): lax.ppermute(sent[0], 'sp', firsts)  3.02 us
    unnamed x12, local copies, waits for them, and re-layouts  2.9 us
    ppermute x3, starting transfers between devices, exchange(): lax.ppermute(sent[1], 'sp', seconds)  2 us
    another operation x1, local copies, waits for them, and re-layouts, on_device(): cot = cotangent[0].reshape(channels, -1)  1.43 us
  transfers between devices with their start and end apart: 13, of which 7 were waited for; matrix products, arithmetic and copies ran while one was open for 7% of the time, Pallas kernels for 21%

profile of v9, /device:TPU:0, one launch (start us, length us, event | category | flops | bytes accessed | tf_op | source)
XLA Modules:
  0.0 53.2 jit_solution(10814424660451361539)
XLA Ops:
  0.6 1.1 %copy-done = bf16[1,96,4,8,128]{4,3,2,1,0:T(8,128)(2,1)S(1)} copy-done((bf16[1,96,4,8,128]{4,3,2,1,0:T(8,128)(2,1)S(1)}, bf16[1,96,4,8,128]{4,3,2,1,0:T(8,128)(2,1)}, u32[]{:S(2)}) %copy-start) | copy-done | bytes 786456
  2.0 3.0 %collective-permute-start = (bf16[96,1024]{1,0:T(8,128)(2,1)S(1)}, bf16[96,1024]{1,0:T(8,128)(2,1)S(1)}, u32[]{:S(2)}, u32[]{:S(2)}) collective-permute-start(bf16[96,1024]{1,0:T(8,128)(2,1)S(1)} %get-tuple-element.49), channel_id=1, source_target_pairs={{0,4},{4,0},{8,12},{12,8},{16,20},{20,16},{24,28},{28,24},{1,5},{5... | collective-permute-start | bytes 589832 | tf_op jit(solution)/shard_map/ppermute | solution.py:458
  5.1 0.7 %collective-permute-start.1 = (bf16[96,1024]{1,0:T(8,128)(2,1)S(1)}, bf16[96,1024]{1,0:T(8,128)(2,1)S(1)}, u32[]{:S(2)}, u32[]{:S(2)}) collective-permute-start(bf16[96,1024]{1,0:T(8,128)(2,1)S(1)} %get-tuple-element.50), channel_id=1, source_target_pairs={{4,8},{12,16},{20,24},{8,4},{16,12},{24,20},{5,9},{13,17},{21,25},... | collective-permute-start | bytes 589832 | tf_op jit(solution)/shard_map/ppermute | solution.py:458
  6.0 4.3 %collective-permute-start.2 = (bf16[96,1024]{1,0:T(8,128)(2,1)S(1)}, bf16[96,1024]{1,0:T(8,128)(2,1)S(1)}, u32[]{:S(2)}, u32[]{:S(2)}) collective-permute-start(bf16[96,1024]{1,0:T(8,128)(2,1)S(1)} %get-tuple-element.55), channel_id=1, source_target_pairs={{0,4},{4,0},{8,12},{12,8},{16,20},{20,16},{24,28},{28,24},{1,5},{5... | collective-permute-start | bytes 589832 | tf_op jit(solution)/shard_map/ppermute | solution.py:458
  12.4 1.4 %reshape_squeeze.7.cot = bf16[96,4096]{1,0:T(8,128)(2,1)S(1)} reshape(bf16[1,96,4,8,128]{4,3,2,1,0:T(8,128)(2,1)} %param.6) | data formatting | bytes 1572864 | tf_op jit(solution)/shard_map/reshape;squeeze | solution.py:465
  14.6 1.1 %inner.1 = (bf16[96,2048]{1,0:T(8,128)(2,1)S(1)}, bf16[96,2048]{1,0:T(8,128)(2,1)S(1)}, bf16[96,2048]{1,0:T(8,128)(2,1)S(1)}, bf16[96,2048]{1,0:T(8,128)(2,1)S(1)}) custom-call(bf16[96,4096]{1,0:T(8,128)(2,1)S(1)} %reshape_squeeze.6.vol, bf16[2,21,96,128]{3,2,1,0:T(8,128)(2,1)S(1)} %pad_maximum_fusion.taps, bf16[2,96,96]{2,1,0:T(8,128)(2,1)S(1)} %copy-done.2), custom_call_target="tpu_custom_call" | custom-call | bytes 4194304 | tf_op jit(solution)/shard_map/inner/pallas_call | solution.py:396
  15.8 3.0 %collective-permute-done.first = bf16[96,1024]{1,0:T(8,128)(2,1)S(1)} collective-permute-done((bf16[96,1024]{1,0:T(8,128)(2,1)S(1)}, bf16[96,1024]{1,0:T(8,128)(2,1)S(1)}, u32[]{:S(2)}, u32[]{:S(2)}) %collective-permute-start) | collective-permute-done | bytes 196640 | tf_op jit(solution)/shard_map/ppermute | solution.py:458
  18.8 3.6 %middle.1 = (bf16[96,1024]{1,0:T(8,128)(2,1)S(1)}, bf16[96,1024]{1,0:T(8,128)(2,1)S(1)}, bf16[96,2048]{1,0:T(8,128)(2,1)S(1)}, bf16[96,2048]{1,0:T(8,128)(2,1)S(...) custom-call(s32[1]{0:T(128)} %bitcast.odd, ...), custom_call_target="tpu_custom_call" | custom-call | bytes 12582912 | tf_op jit(solution)/shard_map/middle/pallas_call | solution.py:396
  22.5 5.2 %edge.1 = (bf16[96,1024]{1,0:T(8,128)(2,1)S(1)}, bf16[96,1024]{1,0:T(8,128)(2,1)S(1)}, bf16[96,2048]{1,0:T(8,128)(2,1)S(1)}, bf16[96,2048]{1,0:T(8,128)(2,1)S(1)...) custom-call(s32[1]{0:T(128)} %bitcast.odd, ...), custom_call_target="tpu_custom_call" | custom-call | bytes 18874368 | tf_op jit(solution)/shard_map/edge/pallas_call | solution.py:396
  27.6 2.6 %collective-permute-start.7 = (bf16[96,2048]{1,0:T(8,128)(2,1)S(1)}, bf16[96,2048]{1,0:T(8,128)(2,1)S(1)}, u32[]{:S(2)}, u32[]{:S(2)}) collective-permute-start(bf16[96,2048]{1,0:T(8,128)(2,1)S(1)} %get-tuple-element.83), channel_id=1, source_target_pairs={{0,4},{4,0},{8,12},{12,8},{16,20},{20,16},{24,28},{28,24},{1,5},{5... | collective-permute-start | bytes 1179656 | tf_op jit(solution)/shard_map/ppermute | solution.py:458
  30.2 4.1 %weights.1 = (bf16[96,2048]{1,0:T(8,128)(2,1)S(1)}, bf16[224,128]{1,0:T(8,128)(2,1)S(1)}) custom-call(bf16[96,4096]{1,0:T(8,128)(2,1)S(1)} %reshape_squeeze.6.vol, bf16[96,1024]{1,0:T(8,128)(2,1)S(1)} %get-tuple-element.52.lo1, bf16[96,1024]{1,0:T(8,128)(2,1)S(1)} %get-tuple-element.53.hi1, bf16[96,1024]{1,0:T(8,128)(2,1)S(1)} %get-tuple-element.60.lo2, ...), custom_call_target="tpu_custom_call" | custom-call | bytes 1 | tf_op jit(solution)/shard_map/weights/pallas_call | solution.py:396
  34.3 1.6 %collective-permute-start.6 = (bf16[224,128]{1,0:T(8,128)(2,1)S(1)}, bf16[224,128]{1,0:T(8,128)(2,1)S(1)}, u32[]{:S(2)}, u32[]{:S(2)}) collective-permute-start(bf16[224,128]{1,0:T(8,128)(2,1)S(1)} %get-tuple-element.82), channel_id=1, source_target_pairs={{0,24},{1,25},{2,26},{3,27},{4,28},{5,29},{6,30},{7,31},{8,16},{9,... | collective-permute-start | bytes 172040 | tf_op jit(solution)/shard_map/ppermute | solution.py:430
  35.9 1.4 %collective-permute-start.5 = (bf16[224,128]{1,0:T(8,128)(2,1)S(1)}, bf16[224,128]{1,0:T(8,128)(2,1)S(1)}, u32[]{:S(2)}, u32[]{:S(2)}) collective-permute-start(bf16[224,128]{1,0:T(8,128)(2,1)S(1)} %get-tuple-element.82), channel_id=1, source_target_pairs={{0,16},{1,17},{2,18},{3,19},{4,20},{5,21},{6,22},{7,23},{8,24},{9,... | collective-permute-start | bytes 172040 | tf_op jit(solution)/shard_map/ppermute | solution.py:430
  37.3 1.5 %collective-permute-start.4 = (bf16[224,128]{1,0:T(8,128)(2,1)S(1)}, bf16[224,128]{1,0:T(8,128)(2,1)S(1)}, u32[]{:S(2)}, u32[]{:S(2)}) collective-permute-start(bf16[224,128]{1,0:T(8,128)(2,1)S(1)} %get-tuple-element.82), channel_id=1, source_target_pairs={{0,8},{1,9},{2,10},{3,11},{4,12},{5,13},{6,14},{7,15},{8,0},{9,1},... | collective-permute-start | bytes 172040 | tf_op jit(solution)/shard_map/ppermute | solution.py:430
  38.8 0.7 %collective-permute-start.8 = (bf16[96,2048]{1,0:T(8,128)(2,1)S(1)}, bf16[96,2048]{1,0:T(8,128)(2,1)S(1)}, u32[]{:S(2)}, u32[]{:S(2)}) collective-permute-start(bf16[96,2048]{1,0:T(8,128)(2,1)S(1)} %get-tuple-element.85), channel_id=1, source_target_pairs={{4,8},{12,16},{20,24},{8,4},{16,12},{24,20},{5,9},{13,17},{21,25},... | collective-permute-start | bytes 1179656 | tf_op jit(solution)/shard_map/ppermute | solution.py:458
  39.5 1.4 %collective-permute-done.6 = bf16[224,128]{1,0:T(8,128)(2,1)S(1)} collective-permute-done((bf16[224,128]{1,0:T(8,128)(2,1)S(1)}, bf16[224,128]{1,0:T(8,128)(2,1)S(1)}, u32[]{:S(2)}, u32[]{:S(2)}) %collective-permute-start.6) | collective-permute-done | bytes 57376 | tf_op jit(solution)/shard_map/ppermute | solution.py:430
  41.5 1.2 %collective-permute-done.4 = bf16[224,128]{1,0:T(8,128)(2,1)S(1)} collective-permute-done((bf16[224,128]{1,0:T(8,128)(2,1)S(1)}, bf16[224,128]{1,0:T(8,128)(2,1)S(1)}, u32[]{:S(2)}, u32[]{:S(2)}) %collective-permute-start.4) | collective-permute-done | bytes 57376 | tf_op jit(solution)/shard_map/ppermute | solution.py:430
  42.8 1.6 %collective-permute-start.10 = (bf16[224,128]{1,0:T(8,128)(2,1)S(1)}, bf16[224,128]{1,0:T(8,128)(2,1)S(1)}, u32[]{:S(2)}, u32[]{:S(2)}) collective-permute-start(bf16[224,128]{1,0:T(8,128)(2,1)S(1)} %add_convert_fusion.1), channel_id=1, source_target_pairs={{0,2},{1,3},{2,0},{3,1},{4,6},{5,7},{6,4},{7,5},{8,10},{9,11},{10,... | collective-permute-start | bytes 172040 | tf_op jit(solution)/shard_map/ppermute | solution.py:430
  44.6 2.3 %collective-permute-done.11 = bf16[224,128]{1,0:T(8,128)(2,1)S(1)} collective-permute-done((bf16[224,128]{1,0:T(8,128)(2,1)S(1)}, bf16[224,128]{1,0:T(8,128)(2,1)S(1)}, u32[]{:S(2)}, u32[]{:S(2)}) %collective-permute-start.11) | collective-permute-done | bytes 57376 | tf_op jit(solution)/shard_map/ppermute | solution.py:430
  46.9 1.3 %collective-permute-done.10 = bf16[224,128]{1,0:T(8,128)(2,1)S(1)} collective-permute-done((bf16[224,128]{1,0:T(8,128)(2,1)S(1)}, bf16[224,128]{1,0:T(8,128)(2,1)S(1)}, u32[]{:S(2)}, u32[]{:S(2)}) %collective-permute-start.10) | collective-permute-done | bytes 57376 | tf_op jit(solution)/shard_map/ppermute | solution.py:430
  48.7 1.1 %volume.1.own = bf16[96,4096]{1,0:T(8,128)(2,1)S(1)} custom-call(bf16[2,21,96,128]{3,2,1,0:T(8,128)(2,1)S(1)} %pad_maximum_fusion.taps, bf16[96,2048]{1,0:T(8,128)(2,1)S(1)} %get-tuple-element.81.gpl1_i, bf16[96,2048]{1,0:T(8,128)(2,1)S(1)} %get-tuple-element.79.gpl1_lo, bf16[96,2048]{1,0:T(8,128)(2,1)S(1)} %get-tuple-element.80.gpl1_hi), custom_call_target="tpu_custom_call" | custom-call | bytes 1 | tf_op jit(solution)/shard_map/volume/pallas_call | solution.py:396
  49.9 1.0 %final.1 = bf16[96,4096]{1,0:T(8,128)(2,1)S(1)} custom-call(s32[1]{0:T(128)} %bitcast.odd, bf16[2,21,96,128]{3,2,1,0:T(8,128)(2,1)S(1)} %pad_maximum_fusion.taps, bf16[96,4096]{1,0:T(8,128)(2,1)S(1)} %volume.1.own, bf16[96,2048]{1,0:T(8,128)(2,1)S(1)} %collective-permute-done.7.first, bf16[96,2048]{1,0:T(8,128)(2,1)S(1)} %collective-permute-done.8.second), custom_call_target="tpu_custom_call" | custom-call | bytes 1 | tf_op jit(solution)/shard_map/final/pallas_call | solution.py:396
  50.9 1.0 %copy.12 = bf16[12,8,32,128]{3,2,1,0:T(8,128)(2,1)} copy(bf16[12,8,32,128]{3,1,2,0:T(8,128)(2,1)S(1)} %bitcast.18) | data formatting | bytes 1572864
  52.5 0.7 %result.1 = (f32[2,96,96]{2,1,0:T(8,128)}, f32[9,2,96]{2,1,0:T(2,128)}, f32[3,2,96]{2,1,0:T(2,128)}) custom-call(bf16[224,128]{1,0:T(8,128)(2,1)S(1)} %add_convert_fusion.refs_0_, bf16[224,128]{1,0:T(8,128)(2,1)S(1)} %collective-permute-done.12.refs_1_), custom_call_target="tpu_custom_call" | custom-call | bytes 1 | tf_op jit(solution)/shard_map/result/pallas_call | solution.py:396
  (40 shorter events, 5.3 us)
Async XLA Ops:
  0.6 1.1 %copy-start = (bf16[1,96,4,8,128]{4,3,2,1,0:T(8,128)(2,1)S(1)}, bf16[1,96,4,8,128]{4,3,2,1,0:T(8,128)(2,1)}, u32[]{:S(2)}) copy-start(bf16[1,96,4,8,128]{4,3,2,1,0:T(8,128)(2,1)} %vol.2) | copy-start | bytes 2359300
  1.8 9.3 %copy-start.1 = (bf16[1,96,4,8,128]{4,3,2,1,0:T(8,128)(2,1)S(1)}, bf16[1,96,4,8,128]{4,3,2,1,0:T(8,128)(2,1)}, u32[]{:S(2)}) copy-start(bf16[1,96,4,8,128]{4,3,2,1,0:T(8,128)(2,1)} %vol.2) | copy-start | bytes 2359300
  2.0 16.8 %collective-permute-start = (bf16[96,1024]{1,0:T(8,128)(2,1)S(1)}, bf16[96,1024]{1,0:T(8,128)(2,1)S(1)}, u32[]{:S(2)}, u32[]{:S(2)}) collective-permute-start(bf16[96,1024]{1,0:T(8,128)(2,1)S(1)} %get-tuple-element.49), channel_id=1, source_target_pairs={{0,4},{4,0},{8,12},{12,8},{16,20},{20,16},{24,28},{28,24},{1,5},{5... | collective-permute-start | bytes 589832 | tf_op jit(solution)/shard_map/ppermute | solution.py:458
  5.1 13.7 %collective-permute-start.1 = (bf16[96,1024]{1,0:T(8,128)(2,1)S(1)}, bf16[96,1024]{1,0:T(8,128)(2,1)S(1)}, u32[]{:S(2)}, u32[]{:S(2)}) collective-permute-start(bf16[96,1024]{1,0:T(8,128)(2,1)S(1)} %get-tuple-element.50), channel_id=1, source_target_pairs={{4,8},{12,16},{20,24},{8,4},{16,12},{24,20},{5,9},{13,17},{21,25},... | collective-permute-start | bytes 589832 | tf_op jit(solution)/shard_map/ppermute | solution.py:458
  6.0 16.4 %collective-permute-start.2 = (bf16[96,1024]{1,0:T(8,128)(2,1)S(1)}, bf16[96,1024]{1,0:T(8,128)(2,1)S(1)}, u32[]{:S(2)}, u32[]{:S(2)}) collective-permute-start(bf16[96,1024]{1,0:T(8,128)(2,1)S(1)} %get-tuple-element.55), channel_id=1, source_target_pairs={{0,4},{4,0},{8,12},{12,8},{16,20},{20,16},{24,28},{28,24},{1,5},{5... | collective-permute-start | bytes 589832 | tf_op jit(solution)/shard_map/ppermute | solution.py:458
  10.4 12.1 %collective-permute-start.3 = (bf16[96,1024]{1,0:T(8,128)(2,1)S(1)}, bf16[96,1024]{1,0:T(8,128)(2,1)S(1)}, u32[]{:S(2)}, u32[]{:S(2)}) collective-permute-start(bf16[96,1024]{1,0:T(8,128)(2,1)S(1)} %get-tuple-element.56), channel_id=1, source_target_pairs={{4,8},{12,16},{20,24},{8,4},{16,12},{24,20},{5,9},{13,17},{21,25},... | collective-permute-start | bytes 589832 | tf_op jit(solution)/shard_map/ppermute | solution.py:458
  11.1 0.7 %copy-start.4 = (bf16[2,96,3]{1,0,2:T(2,128)(2,1)S(1)}, bf16[2,96,3]{1,0,2:T(2,128)(2,1)}, u32[]{:S(2)}) copy-start(bf16[2,96,3]{1,0,2:T(2,128)(2,1)} %param.8) | copy-start | bytes 3460
  11.1 0.8 %copy-start.3 = (bf16[2,96,3,3]{1,0,3,2:T(2,128)(2,1)S(1)}, bf16[2,96,3,3]{1,0,3,2:T(2,128)(2,1)}, u32[]{:S(2)}) copy-start(bf16[2,96,3,3]{1,0,3,2:T(2,128)(2,1)} %param.7) | copy-start | bytes 10372
  11.4 0.8 %copy-start.2 = (bf16[2,96,96]{2,1,0:T(8,128)(2,1)S(1)}, bf16[2,96,96]{2,1,0:T(8,128)(2,1)}, u32[]{:S(2)}) copy-start(bf16[2,96,96]{2,1,0:T(8,128)(2,1)} %mix.5) | copy-start | bytes 110596
  27.6 15.1 %collective-permute-start.7 = (bf16[96,2048]{1,0:T(8,128)(2,1)S(1)}, bf16[96,2048]{1,0:T(8,128)(2,1)S(1)}, u32[]{:S(2)}, u32[]{:S(2)}) collective-permute-start(bf16[96,2048]{1,0:T(8,128)(2,1)S(1)} %get-tuple-element.83), channel_id=1, source_target_pairs={{0,4},{4,0},{8,12},{12,8},{16,20},{20,16},{24,28},{28,24},{1,5},{5... | collective-permute-start | bytes 1179656 | tf_op jit(solution)/shard_map/ppermute | solution.py:458
  34.3 6.5 %collective-permute-start.6 = (bf16[224,128]{1,0:T(8,128)(2,1)S(1)}, bf16[224,128]{1,0:T(8,128)(2,1)S(1)}, u32[]{:S(2)}, u32[]{:S(2)}) collective-permute-start(bf16[224,128]{1,0:T(8,128)(2,1)S(1)} %get-tuple-element.82), channel_id=1, source_target_pairs={{0,24},{1,25},{2,26},{3,27},{4,28},{5,29},{6,30},{7,31},{8,16},{9,... | collective-permute-start | bytes 172040 | tf_op jit(solution)/shard_map/ppermute | solution.py:430
  35.9 5.6 %collective-permute-start.5 = (bf16[224,128]{1,0:T(8,128)(2,1)S(1)}, bf16[224,128]{1,0:T(8,128)(2,1)S(1)}, u32[]{:S(2)}, u32[]{:S(2)}) collective-permute-start(bf16[224,128]{1,0:T(8,128)(2,1)S(1)} %get-tuple-element.82), channel_id=1, source_target_pairs={{0,16},{1,17},{2,18},{3,19},{4,20},{5,21},{6,22},{7,23},{8,24},{9,... | collective-permute-start | bytes 172040 | tf_op jit(solution)/shard_map/ppermute | solution.py:430
  37.3 5.3 %collective-permute-start.4 = (bf16[224,128]{1,0:T(8,128)(2,1)S(1)}, bf16[224,128]{1,0:T(8,128)(2,1)S(1)}, u32[]{:S(2)}, u32[]{:S(2)}) collective-permute-start(bf16[224,128]{1,0:T(8,128)(2,1)S(1)} %get-tuple-element.82), channel_id=1, source_target_pairs={{0,8},{1,9},{2,10},{3,11},{4,12},{5,13},{6,14},{7,15},{8,0},{9,1},... | collective-permute-start | bytes 172040 | tf_op jit(solution)/shard_map/ppermute | solution.py:430
  38.8 11.1 %collective-permute-start.8 = (bf16[96,2048]{1,0:T(8,128)(2,1)S(1)}, bf16[96,2048]{1,0:T(8,128)(2,1)S(1)}, u32[]{:S(2)}, u32[]{:S(2)}) collective-permute-start(bf16[96,2048]{1,0:T(8,128)(2,1)S(1)} %get-tuple-element.85), channel_id=1, source_target_pairs={{4,8},{12,16},{20,24},{8,4},{16,12},{24,20},{5,9},{13,17},{21,25},... | collective-permute-start | bytes 1179656 | tf_op jit(solution)/shard_map/ppermute | solution.py:458
  42.7 4.2 %collective-permute-start.11 = (bf16[224,128]{1,0:T(8,128)(2,1)S(1)}, bf16[224,128]{1,0:T(8,128)(2,1)S(1)}, u32[]{:S(2)}, u32[]{:S(2)}) collective-permute-start(bf16[224,128]{1,0:T(8,128)(2,1)S(1)} %add_convert_fusion.1), channel_id=1, source_target_pairs={{0,3},{1,2},{2,1},{3,0},{4,7},{5,6},{6,5},{7,4},{8,11},{9,10},{10,... | collective-permute-start | bytes 172040 | tf_op jit(solution)/shard_map/ppermute | solution.py:430
  42.8 5.4 %collective-permute-start.10 = (bf16[224,128]{1,0:T(8,128)(2,1)S(1)}, bf16[224,128]{1,0:T(8,128)(2,1)S(1)}, u32[]{:S(2)}, u32[]{:S(2)}) collective-permute-start(bf16[224,128]{1,0:T(8,128)(2,1)S(1)} %add_convert_fusion.1), channel_id=1, source_target_pairs={{0,2},{1,3},{2,0},{3,1},{4,6},{5,7},{6,4},{7,5},{8,10},{9,11},{10,... | collective-permute-start | bytes 172040 | tf_op jit(solution)/shard_map/ppermute | solution.py:430
  44.3 3.9 %collective-permute-start.9 = (bf16[224,128]{1,0:T(8,128)(2,1)S(1)}, bf16[224,128]{1,0:T(8,128)(2,1)S(1)}, u32[]{:S(2)}, u32[]{:S(2)}) collective-permute-start(bf16[224,128]{1,0:T(8,128)(2,1)S(1)} %add_convert_fusion.1), channel_id=1, source_target_pairs={{0,1},{1,0},{2,3},{3,2},{4,5},{5,4},{6,7},{7,6},{8,9},{9,8},{10,11... | collective-permute-start | bytes 172040 | tf_op jit(solution)/shard_map/ppermute | solution.py:430
  48.2 4.2 %collective-permute-start.12 = (bf16[224,128]{1,0:T(8,128)(2,1)S(1)}, bf16[224,128]{1,0:T(8,128)(2,1)S(1)}, u32[]{:S(2)}, u32[]{:S(2)}) collective-permute-start(bf16[224,128]{1,0:T(8,128)(2,1)S(1)} %add_convert_fusion.refs_0_), channel_id=1, source_target_pairs={{0,4},{1,5},{2,6},{3,7},{4,0},{5,1},{6,2},{7,3},{8,12},{9,13},{10,... | collective-permute-start | bytes 172040 | tf_op jit(solution)/shard_map/ppermute | solution.py:430

commit v10 on v9

--- a/solution.py
+++ b/solution.py
@@ -39,12 +39,12 @@
         self.tile(index, z, rows)[...] = value.astype(BF16)
 
 
-def over_groups(channels, body):
+def over_groups(channels, body, unroll=3):
     def step(group, carry):
         body(pl.ds(pl.multiple_of(group * GROUP, GROUP), GROUP))
         return carry
 
-    lax.fori_loop(0, channels // GROUP, step, 0, unroll=3)
+    lax.fori_loop(0, channels // GROUP, step, 0, unroll=unroll)
 
 
 def spread(taps_ref, block, rows, first, count):
@@ -100,7 +100,7 @@
                 planar.put(index, z, rows, values[z])
                 axial.put(index, z, rows, depth_conv(depth, values, z))
 
-    over_groups(source.channels, body)
+    over_groups(source.channels, body, 6)
 
 
 def mixed(mix_ref, block, indices, source, use):
@@ -150,13 +150,13 @@
     nz = grad_axial.nz
 
     def body(rows):
-        depth = spread(taps_ref, block, rows, 18, 3)[::-1]
+        depth = [taps_ref[block, t, rows, :] for t in (20, 19, 18)]
         for index in indices:
-            values = [grad_axial.get(index, z, rows) for z in range(nz)]
+            values = [grad_axial.tile(index, z, rows)[...] for z in range(nz)]
             for z in range(nz):
                 grad_planar.put(index, z, rows, depth_conv(depth, values, z))
 
-    over_groups(grad_axial.channels, body)
+    over_groups(grad_axial.channels, body, 6)
 
 
 def input_gradient(taps_ref, block, indices, grad_planar, target, slope, start=None):
@@ -173,7 +173,7 @@
                     value = value + start.get(index, z, rows)
                 target.put(index, z, rows, value)
 
-    over_groups(grad_planar.channels, body)
+    over_groups(grad_planar.channels, body, 6)
 
 
 def tap_sums(indices, grad_planar, source, grad_axial, planar, sums_ref, before=None):
@@ -210,7 +210,7 @@
         for t in range(12):
             sums_ref[t, rows, :] = sums[t]
 
-    over_groups(source.channels, body)
+    over_groups(source.channels, body, 6)
 
 
 def mixing_sum(indices, grad_pre, axial):

time: 53.5 us -> 52.4 us (0.979)
  Pallas kernels: 17.4 us -> 16.2 us
    pallas_call x7, Pallas kernels: 16.9 us -> 15.6 us  [call(): pl.pallas_call(kernel, name=name, out_shape=outputs, in_specs=[smem] * sc...]
  transfers between devices with their start and end apart: 13 -> 13, of which waited for: 7 -> 6; matrix products, arithmetic and copies ran while one was open for 7% -> 8% of each run, Pallas kernels for 21% -> 20%
where the time goes in v10:
time: 52.4 us; the launch traced here: 52.1 us
  starting transfers between devices  19.1 us (36%)
  Pallas kernels  16.2 us (31%)
  waiting for transfers between devices  10.2 us (19%)
  local copies, waits for them, and re-layouts  4.84 us (9%)
  between operations  0.89 us (2%)
  other arithmetic  0.87 us (2%)
    pallas_call x7, Pallas kernels, call(): pl.pallas_call(kernel, name=name, out_shape=outputs, in_specs=[smem] * sc...  15.6 us
    ppermute x3, starting transfers between devices, exchange(): lax.ppermute(sent[0], 'sp', firsts)  9.92 us
    ppermute x7, starting transfers between devices, all_sum(): lax.ppermute(mine, ('sp', 'dp'), [(i, i ^ step) for i in places])  7.22 us
    ppermute x7, waiting for transfers between devices, all_sum(): lax.ppermute(mine, ('sp', 'dp'), [(i, i ^ step) for i in places])  7.09 us
    ppermute x3, waiting for transfers between devices, exchange(): lax.ppermute(sent[0], 'sp', firsts)  3.14 us
    unnamed x12, local copies, waits for them, and re-layouts  2.9 us
    ppermute x3, starting transfers between devices, exchange(): lax.ppermute(sent[1], 'sp', seconds)  2 us
    another operation x1, local copies, waits for them, and re-layouts, on_device(): cot = cotangent[0].reshape(channels, -1)  1.43 us
  transfers between devices with their start and end apart: 13, of which 6 were waited for; matrix products, arithmetic and copies ran while one was open for 8% of the time, Pallas kernels for 20%

profile of v10, /device:TPU:0, one launch (start us, length us, event | category | flops | bytes accessed | tf_op | source)
XLA Modules:
  0.0 52.1 jit_solution(6033306656232702154)
XLA Ops:
  0.6 1.1 %copy-done = bf16[1,96,4,8,128]{4,3,2,1,0:T(8,128)(2,1)S(1)} copy-done((bf16[1,96,4,8,128]{4,3,2,1,0:T(8,128)(2,1)S(1)}, bf16[1,96,4,8,128]{4,3,2,1,0:T(8,128)(2,1)}, u32[]{:S(2)}) %copy-start) | copy-done | bytes 786456
  2.0 3.0 %collective-permute-start = (bf16[96,1024]{1,0:T(8,128)(2,1)S(1)}, bf16[96,1024]{1,0:T(8,128)(2,1)S(1)}, u32[]{:S(2)}, u32[]{:S(2)}) collective-permute-start(bf16[96,1024]{1,0:T(8,128)(2,1)S(1)} %get-tuple-element.49), channel_id=1, source_target_pairs={{0,4},{4,0},{8,12},{12,8},{16,20},{20,16},{24,28},{28,24},{1,5},{5... | collective-permute-start | bytes 589832 | tf_op jit(solution)/shard_map/ppermute | solution.py:458
  6.0 4.3 %collective-permute-start.2 = (bf16[96,1024]{1,0:T(8,128)(2,1)S(1)}, bf16[96,1024]{1,0:T(8,128)(2,1)S(1)}, u32[]{:S(2)}, u32[]{:S(2)}) collective-permute-start(bf16[96,1024]{1,0:T(8,128)(2,1)S(1)} %get-tuple-element.55), channel_id=1, source_target_pairs={{0,4},{4,0},{8,12},{12,8},{16,20},{20,16},{24,28},{28,24},{1,5},{5... | collective-permute-start | bytes 589832 | tf_op jit(solution)/shard_map/ppermute | solution.py:458
  12.4 1.4 %reshape_squeeze.7.cot = bf16[96,4096]{1,0:T(8,128)(2,1)S(1)} reshape(bf16[1,96,4,8,128]{4,3,2,1,0:T(8,128)(2,1)} %param.6) | data formatting | bytes 1572864 | tf_op jit(solution)/shard_map/reshape;squeeze | solution.py:465
  14.6 1.1 %inner.1 = (bf16[96,2048]{1,0:T(8,128)(2,1)S(1)}, bf16[96,2048]{1,0:T(8,128)(2,1)S(1)}, bf16[96,2048]{1,0:T(8,128)(2,1)S(1)}, bf16[96,2048]{1,0:T(8,128)(2,1)S(1)}) custom-call(bf16[96,4096]{1,0:T(8,128)(2,1)S(1)} %reshape_squeeze.6.vol, bf16[2,21,96,128]{3,2,1,0:T(8,128)(2,1)S(1)} %pad_maximum_fusion.taps, bf16[2,96,96]{2,1,0:T(8,128)(2,1)S(1)} %copy-done.2), custom_call_target="tpu_custom_call" | custom-call | bytes 4194304 | tf_op jit(solution)/shard_map/inner/pallas_call | solution.py:396
  15.7 3.1 %collective-permute-done.first = bf16[96,1024]{1,0:T(8,128)(2,1)S(1)} collective-permute-done((bf16[96,1024]{1,0:T(8,128)(2,1)S(1)}, bf16[96,1024]{1,0:T(8,128)(2,1)S(1)}, u32[]{:S(2)}, u32[]{:S(2)}) %collective-permute-start) | collective-permute-done | bytes 196640 | tf_op jit(solution)/shard_map/ppermute | solution.py:458
  18.8 3.0 %middle.1 = (bf16[96,1024]{1,0:T(8,128)(2,1)S(1)}, bf16[96,1024]{1,0:T(8,128)(2,1)S(1)}, bf16[96,2048]{1,0:T(8,128)(2,1)S(1)}, bf16[96,2048]{1,0:T(8,128)(2,1)S(...) custom-call(s32[1]{0:T(128)} %bitcast.odd, ...), custom_call_target="tpu_custom_call" | custom-call | bytes 12582912 | tf_op jit(solution)/shard_map/middle/pallas_call | solution.py:396
  21.9 4.7 %edge.1 = (bf16[96,1024]{1,0:T(8,128)(2,1)S(1)}, bf16[96,1024]{1,0:T(8,128)(2,1)S(1)}, bf16[96,2048]{1,0:T(8,128)(2,1)S(1)}, bf16[96,2048]{1,0:T(8,128)(2,1)S(1)...) custom-call(s32[1]{0:T(128)} %bitcast.odd, ...), custom_call_target="tpu_custom_call" | custom-call | bytes 18874368 | tf_op jit(solution)/shard_map/edge/pallas_call | solution.py:396
  26.5 2.5 %collective-permute-start.7 = (bf16[96,2048]{1,0:T(8,128)(2,1)S(1)}, bf16[96,2048]{1,0:T(8,128)(2,1)S(1)}, u32[]{:S(2)}, u32[]{:S(2)}) collective-permute-start(bf16[96,2048]{1,0:T(8,128)(2,1)S(1)} %get-tuple-element.83), channel_id=1, source_target_pairs={{0,4},{4,0},{8,12},{12,8},{16,20},{20,16},{24,28},{28,24},{1,5},{5... | collective-permute-start | bytes 1179656 | tf_op jit(solution)/shard_map/ppermute | solution.py:458
  29.1 4.2 %weights.1 = (bf16[96,2048]{1,0:T(8,128)(2,1)S(1)}, bf16[224,128]{1,0:T(8,128)(2,1)S(1)}) custom-call(bf16[96,4096]{1,0:T(8,128)(2,1)S(1)} %reshape_squeeze.6.vol, bf16[96,1024]{1,0:T(8,128)(2,1)S(1)} %get-tuple-element.52.lo1, bf16[96,1024]{1,0:T(8,128)(2,1)S(1)} %get-tuple-element.53.hi1, bf16[96,1024]{1,0:T(8,128)(2,1)S(1)} %get-tuple-element.60.lo2, ...), custom_call_target="tpu_custom_call" | custom-call | bytes 1 | tf_op jit(solution)/shard_map/weights/pallas_call | solution.py:396
  33.3 2.1 %collective-permute-start.6 = (bf16[224,128]{1,0:T(8,128)(2,1)S(1)}, bf16[224,128]{1,0:T(8,128)(2,1)S(1)}, u32[]{:S(2)}, u32[]{:S(2)}) collective-permute-start(bf16[224,128]{1,0:T(8,128)(2,1)S(1)} %get-tuple-element.82), channel_id=1, source_target_pairs={{0,24},{1,25},{2,26},{3,27},{4,28},{5,29},{6,30},{7,31},{8,16},{9,... | collective-permute-start | bytes 172040 | tf_op jit(solution)/shard_map/ppermute | solution.py:430
  35.4 0.9 %collective-permute-start.5 = (bf16[224,128]{1,0:T(8,128)(2,1)S(1)}, bf16[224,128]{1,0:T(8,128)(2,1)S(1)}, u32[]{:S(2)}, u32[]{:S(2)}) collective-permute-start(bf16[224,128]{1,0:T(8,128)(2,1)S(1)} %get-tuple-element.82), channel_id=1, source_target_pairs={{0,16},{1,17},{2,18},{3,19},{4,20},{5,21},{6,22},{7,23},{8,24},{9,... | collective-permute-start | bytes 172040 | tf_op jit(solution)/shard_map/ppermute | solution.py:430
  36.3 1.4 %collective-permute-start.4 = (bf16[224,128]{1,0:T(8,128)(2,1)S(1)}, bf16[224,128]{1,0:T(8,128)(2,1)S(1)}, u32[]{:S(2)}, u32[]{:S(2)}) collective-permute-start(bf16[224,128]{1,0:T(8,128)(2,1)S(1)} %get-tuple-element.82), channel_id=1, source_target_pairs={{0,8},{1,9},{2,10},{3,11},{4,12},{5,13},{6,14},{7,15},{8,0},{9,1},... | collective-permute-start | bytes 172040 | tf_op jit(solution)/shard_map/ppermute | solution.py:430
  37.7 0.7 %collective-permute-start.8 = (bf16[96,2048]{1,0:T(8,128)(2,1)S(1)}, bf16[96,2048]{1,0:T(8,128)(2,1)S(1)}, u32[]{:S(2)}, u32[]{:S(2)}) collective-permute-start(bf16[96,2048]{1,0:T(8,128)(2,1)S(1)} %get-tuple-element.85), channel_id=1, source_target_pairs={{4,8},{12,16},{20,24},{8,4},{16,12},{24,20},{5,9},{13,17},{21,25},... | collective-permute-start | bytes 1179656 | tf_op jit(solution)/shard_map/ppermute | solution.py:458
  38.4 0.9 %collective-permute-done.6 = bf16[224,128]{1,0:T(8,128)(2,1)S(1)} collective-permute-done((bf16[224,128]{1,0:T(8,128)(2,1)S(1)}, bf16[224,128]{1,0:T(8,128)(2,1)S(1)}, u32[]{:S(2)}, u32[]{:S(2)}) %collective-permute-start.6) | collective-permute-done | bytes 57376 | tf_op jit(solution)/shard_map/ppermute | solution.py:430
  39.3 2.4 %collective-permute-done.5 = bf16[224,128]{1,0:T(8,128)(2,1)S(1)} collective-permute-done((bf16[224,128]{1,0:T(8,128)(2,1)S(1)}, bf16[224,128]{1,0:T(8,128)(2,1)S(1)}, u32[]{:S(2)}, u32[]{:S(2)}) %collective-permute-start.5) | collective-permute-done | bytes 57376 | tf_op jit(solution)/shard_map/ppermute | solution.py:430
  41.8 1.6 %collective-permute-start.10 = (bf16[224,128]{1,0:T(8,128)(2,1)S(1)}, bf16[224,128]{1,0:T(8,128)(2,1)S(1)}, u32[]{:S(2)}, u32[]{:S(2)}) collective-permute-start(bf16[224,128]{1,0:T(8,128)(2,1)S(1)} %add_convert_fusion.1), channel_id=1, source_target_pairs={{0,2},{1,3},{2,0},{3,1},{4,6},{5,7},{6,4},{7,5},{8,10},{9,11},{10,... | collective-permute-start | bytes 172040 | tf_op jit(solution)/shard_map/ppermute | solution.py:430
  43.6 2.3 %collective-permute-done.11 = bf16[224,128]{1,0:T(8,128)(2,1)S(1)} collective-permute-done((bf16[224,128]{1,0:T(8,128)(2,1)S(1)}, bf16[224,128]{1,0:T(8,128)(2,1)S(1)}, u32[]{:S(2)}, u32[]{:S(2)}) %collective-permute-start.11) | collective-permute-done | bytes 57376 | tf_op jit(solution)/shard_map/ppermute | solution.py:430
  45.9 1.3 %collective-permute-done.10 = bf16[224,128]{1,0:T(8,128)(2,1)S(1)} collective-permute-done((bf16[224,128]{1,0:T(8,128)(2,1)S(1)}, bf16[224,128]{1,0:T(8,128)(2,1)S(1)}, u32[]{:S(2)}, u32[]{:S(2)}) %collective-permute-start.10) | collective-permute-done | bytes 57376 | tf_op jit(solution)/shard_map/ppermute | solution.py:430
  47.2 0.9 %collective-permute-start.12 = (bf16[224,128]{1,0:T(8,128)(2,1)S(1)}, bf16[224,128]{1,0:T(8,128)(2,1)S(1)}, u32[]{:S(2)}, u32[]{:S(2)}) collective-permute-start(bf16[224,128]{1,0:T(8,128)(2,1)S(1)} %add_convert_fusion.refs_0_), channel_id=1, source_target_pairs={{0,4},{1,5},{2,6},{3,7},{4,0},{5,1},{6,2},{7,3},{8,12},{9,13},{10,... | collective-permute-start | bytes 172040 | tf_op jit(solution)/shard_map/ppermute | solution.py:430
  48.1 1.1 %volume.1.own = bf16[96,4096]{1,0:T(8,128)(2,1)S(1)} custom-call(bf16[2,21,96,128]{3,2,1,0:T(8,128)(2,1)S(1)} %pad_maximum_fusion.taps, bf16[96,2048]{1,0:T(8,128)(2,1)S(1)} %get-tuple-element.81.gpl1_i, bf16[96,2048]{1,0:T(8,128)(2,1)S(1)} %get-tuple-element.79.gpl1_lo, bf16[96,2048]{1,0:T(8,128)(2,1)S(1)} %get-tuple-element.80.gpl1_hi), custom_call_target="tpu_custom_call" | custom-call | bytes 1 | tf_op jit(solution)/shard_map/volume/pallas_call | solution.py:396
  49.3 0.9 %final.1 = bf16[96,4096]{1,0:T(8,128)(2,1)S(1)} custom-call(s32[1]{0:T(128)} %bitcast.odd, bf16[2,21,96,128]{3,2,1,0:T(8,128)(2,1)S(1)} %pad_maximum_fusion.taps, bf16[96,4096]{1,0:T(8,128)(2,1)S(1)} %volume.1.own, bf16[96,2048]{1,0:T(8,128)(2,1)S(1)} %collective-permute-done.7.first, bf16[96,2048]{1,0:T(8,128)(2,1)S(1)} %collective-permute-done.8.second), custom_call_target="tpu_custom_call" | custom-call | bytes 1 | tf_op jit(solution)/shard_map/final/pallas_call | solution.py:396
  50.2 1.0 %copy.12 = bf16[12,8,32,128]{3,2,1,0:T(8,128)(2,1)} copy(bf16[12,8,32,128]{3,1,2,0:T(8,128)(2,1)S(1)} %bitcast.18) | data formatting | bytes 1572864
  51.5 0.7 %result.1 = (f32[2,96,96]{2,1,0:T(8,128)}, f32[9,2,96]{2,1,0:T(2,128)}, f32[3,2,96]{2,1,0:T(2,128)}) custom-call(bf16[224,128]{1,0:T(8,128)(2,1)S(1)} %add_convert_fusion.refs_0_, bf16[224,128]{1,0:T(8,128)(2,1)S(1)} %collective-permute-done.12.refs_1_), custom_call_target="tpu_custom_call" | custom-call | bytes 1 | tf_op jit(solution)/shard_map/result/pallas_call | solution.py:396
  (40 shorter events, 4.6 us)
Async XLA Ops:
  0.6 1.1 %copy-start = (bf16[1,96,4,8,128]{4,3,2,1,0:T(8,128)(2,1)S(1)}, bf16[1,96,4,8,128]{4,3,2,1,0:T(8,128)(2,1)}, u32[]{:S(2)}) copy-start(bf16[1,96,4,8,128]{4,3,2,1,0:T(8,128)(2,1)} %vol.2) | copy-start | bytes 2359300
  1.8 9.3 %copy-start.1 = (bf16[1,96,4,8,128]{4,3,2,1,0:T(8,128)(2,1)S(1)}, bf16[1,96,4,8,128]{4,3,2,1,0:T(8,128)(2,1)}, u32[]{:S(2)}) copy-start(bf16[1,96,4,8,128]{4,3,2,1,0:T(8,128)(2,1)} %vol.2) | copy-start | bytes 2359300
  2.0 16.8 %collective-permute-start = (bf16[96,1024]{1,0:T(8,128)(2,1)S(1)}, bf16[96,1024]{1,0:T(8,128)(2,1)S(1)}, u32[]{:S(2)}, u32[]{:S(2)}) collective-permute-start(bf16[96,1024]{1,0:T(8,128)(2,1)S(1)} %get-tuple-element.49), channel_id=1, source_target_pairs={{0,4},{4,0},{8,12},{12,8},{16,20},{20,16},{24,28},{28,24},{1,5},{5... | collective-permute-start | bytes 589832 | tf_op jit(solution)/shard_map/ppermute | solution.py:458
  5.1 13.7 %collective-permute-start.1 = (bf16[96,1024]{1,0:T(8,128)(2,1)S(1)}, bf16[96,1024]{1,0:T(8,128)(2,1)S(1)}, u32[]{:S(2)}, u32[]{:S(2)}) collective-permute-start(bf16[96,1024]{1,0:T(8,128)(2,1)S(1)} %get-tuple-element.50), channel_id=1, source_target_pairs={{4,8},{12,16},{20,24},{8,4},{16,12},{24,20},{5,9},{13,17},{21,25},... | collective-permute-start | bytes 589832 | tf_op jit(solution)/shard_map/ppermute | solution.py:458
  6.0 15.8 %collective-permute-start.2 = (bf16[96,1024]{1,0:T(8,128)(2,1)S(1)}, bf16[96,1024]{1,0:T(8,128)(2,1)S(1)}, u32[]{:S(2)}, u32[]{:S(2)}) collective-permute-start(bf16[96,1024]{1,0:T(8,128)(2,1)S(1)} %get-tuple-element.55), channel_id=1, source_target_pairs={{0,4},{4,0},{8,12},{12,8},{16,20},{20,16},{24,28},{28,24},{1,5},{5... | collective-permute-start | bytes 589832 | tf_op jit(solution)/shard_map/ppermute | solution.py:458
  10.4 11.5 %collective-permute-start.3 = (bf16[96,1024]{1,0:T(8,128)(2,1)S(1)}, bf16[96,1024]{1,0:T(8,128)(2,1)S(1)}, u32[]{:S(2)}, u32[]{:S(2)}) collective-permute-start(bf16[96,1024]{1,0:T(8,128)(2,1)S(1)} %get-tuple-element.56), channel_id=1, source_target_pairs={{4,8},{12,16},{20,24},{8,4},{16,12},{24,20},{5,9},{13,17},{21,25},... | collective-permute-start | bytes 589832 | tf_op jit(solution)/shard_map/ppermute | solution.py:458
  11.1 0.7 %copy-start.4 = (bf16[2,96,3]{1,0,2:T(2,128)(2,1)S(1)}, bf16[2,96,3]{1,0,2:T(2,128)(2,1)}, u32[]{:S(2)}) copy-start(bf16[2,96,3]{1,0,2:T(2,128)(2,1)} %param.8) | copy-start | bytes 3460
  11.1 0.8 %copy-start.3 = (bf16[2,96,3,3]{1,0,3,2:T(2,128)(2,1)S(1)}, bf16[2,96,3,3]{1,0,3,2:T(2,128)(2,1)}, u32[]{:S(2)}) copy-start(bf16[2,96,3,3]{1,0,3,2:T(2,128)(2,1)} %param.7) | copy-start | bytes 10372
  11.4 0.8 %copy-start.2 = (bf16[2,96,96]{2,1,0:T(8,128)(2,1)S(1)}, bf16[2,96,96]{2,1,0:T(8,128)(2,1)}, u32[]{:S(2)}) copy-start(bf16[2,96,96]{2,1,0:T(8,128)(2,1)} %mix.5) | copy-start | bytes 110596
  26.5 15.1 %collective-permute-start.7 = (bf16[96,2048]{1,0:T(8,128)(2,1)S(1)}, bf16[96,2048]{1,0:T(8,128)(2,1)S(1)}, u32[]{:S(2)}, u32[]{:S(2)}) collective-permute-start(bf16[96,2048]{1,0:T(8,128)(2,1)S(1)} %get-tuple-element.83), channel_id=1, source_target_pairs={{0,4},{4,0},{8,12},{12,8},{16,20},{20,16},{24,28},{28,24},{1,5},{5... | collective-permute-start | bytes 1179656 | tf_op jit(solution)/shard_map/ppermute | solution.py:458
  33.3 6.0 %collective-permute-start.6 = (bf16[224,128]{1,0:T(8,128)(2,1)S(1)}, bf16[224,128]{1,0:T(8,128)(2,1)S(1)}, u32[]{:S(2)}, u32[]{:S(2)}) collective-permute-start(bf16[224,128]{1,0:T(8,128)(2,1)S(1)} %get-tuple-element.82), channel_id=1, source_target_pairs={{0,24},{1,25},{2,26},{3,27},{4,28},{5,29},{6,30},{7,31},{8,16},{9,... | collective-permute-start | bytes 172040 | tf_op jit(solution)/shard_map/ppermute | solution.py:430
  35.4 6.2 %collective-permute-start.5 = (bf16[224,128]{1,0:T(8,128)(2,1)S(1)}, bf16[224,128]{1,0:T(8,128)(2,1)S(1)}, u32[]{:S(2)}, u32[]{:S(2)}) collective-permute-start(bf16[224,128]{1,0:T(8,128)(2,1)S(1)} %get-tuple-element.82), channel_id=1, source_target_pairs={{0,16},{1,17},{2,18},{3,19},{4,20},{5,21},{6,22},{7,23},{8,24},{9,... | collective-permute-start | bytes 172040 | tf_op jit(solution)/shard_map/ppermute | solution.py:430
  36.3 5.3 %collective-permute-start.4 = (bf16[224,128]{1,0:T(8,128)(2,1)S(1)}, bf16[224,128]{1,0:T(8,128)(2,1)S(1)}, u32[]{:S(2)}, u32[]{:S(2)}) collective-permute-start(bf16[224,128]{1,0:T(8,128)(2,1)S(1)} %get-tuple-element.82), channel_id=1, source_target_pairs={{0,8},{1,9},{2,10},{3,11},{4,12},{5,13},{6,14},{7,15},{8,0},{9,1},... | collective-permute-start | bytes 172040 | tf_op jit(solution)/shard_map/ppermute | solution.py:430
  37.7 11.6 %collective-permute-start.8 = (bf16[96,2048]{1,0:T(8,128)(2,1)S(1)}, bf16[96,2048]{1,0:T(8,128)(2,1)S(1)}, u32[]{:S(2)}, u32[]{:S(2)}) collective-permute-start(bf16[96,2048]{1,0:T(8,128)(2,1)S(1)} %get-tuple-element.85), channel_id=1, source_target_pairs={{4,8},{12,16},{20,24},{8,4},{16,12},{24,20},{5,9},{13,17},{21,25},... | collective-permute-start | bytes 1179656 | tf_op jit(solution)/shard_map/ppermute | solution.py:458
  41.7 4.2 %collective-permute-start.11 = (bf16[224,128]{1,0:T(8,128)(2,1)S(1)}, bf16[224,128]{1,0:T(8,128)(2,1)S(1)}, u32[]{:S(2)}, u32[]{:S(2)}) collective-permute-start(bf16[224,128]{1,0:T(8,128)(2,1)S(1)} %add_convert_fusion.1), channel_id=1, source_target_pairs={{0,3},{1,2},{2,1},{3,0},{4,7},{5,6},{6,5},{7,4},{8,11},{9,10},{10,... | collective-permute-start | bytes 172040 | tf_op jit(solution)/shard_map/ppermute | solution.py:430
  41.8 5.4 %collective-permute-start.10 = (bf16[224,128]{1,0:T(8,128)(2,1)S(1)}, bf16[224,128]{1,0:T(8,128)(2,1)S(1)}, u32[]{:S(2)}, u32[]{:S(2)}) collective-permute-start(bf16[224,128]{1,0:T(8,128)(2,1)S(1)} %add_convert_fusion.1), channel_id=1, source_target_pairs={{0,2},{1,3},{2,0},{3,1},{4,6},{5,7},{6,4},{7,5},{8,10},{9,11},{10,... | collective-permute-start | bytes 172040 | tf_op jit(solution)/shard_map/ppermute | solution.py:430
  43.3 3.9 %collective-permute-start.9 = (bf16[224,128]{1,0:T(8,128)(2,1)S(1)}, bf16[224,128]{1,0:T(8,128)(2,1)S(1)}, u32[]{:S(2)}, u32[]{:S(2)}) collective-permute-start(bf16[224,128]{1,0:T(8,128)(2,1)S(1)} %add_convert_fusion.1), channel_id=1, source_target_pairs={{0,1},{1,0},{2,3},{3,2},{4,5},{5,4},{6,7},{7,6},{8,9},{9,8},{10,11... | collective-permute-start | bytes 172040 | tf_op jit(solution)/shard_map/ppermute | solution.py:430
  47.2 4.2 %collective-permute-start.12 = (bf16[224,128]{1,0:T(8,128)(2,1)S(1)}, bf16[224,128]{1,0:T(8,128)(2,1)S(1)}, u32[]{:S(2)}, u32[]{:S(2)}) collective-permute-start(bf16[224,128]{1,0:T(8,128)(2,1)S(1)} %add_convert_fusion.refs_0_), channel_id=1, source_target_pairs={{0,4},{1,5},{2,6},{3,7},{4,0},{5,1},{6,2},{7,3},{8,12},{9,13},{10,... | collective-permute-start | bytes 172040 | tf_op jit(solution)/shard_map/ppermute | solution.py:430

commit v11 on v10

--- a/solution.py
+++ b/solution.py
@@ -52,7 +52,8 @@
 
 
 def plane_taps(taps_ref, block, rows, flip):
-    taps = spread(taps_ref, block, rows, 9 if flip else 0, 9)
+    first = 9 if flip else 0
+    taps = [taps_ref[block, t, rows, :] for t in range(first, first + 9)]
     return [taps[3 * i : 3 * i + 3] for i in range(3)]
 
 
@@ -72,11 +73,11 @@
     sums = [None, None, None]
     for i in range(3):
         if index + i - 1 in source:
-            value = source.get(index + i - 1, z, rows)
+            value = source.tile(index + i - 1, z, rows)[...]
             for j in range(3):
                 term = taps[i][j] * value
                 sums[j] = term if sums[j] is None else sums[j] + term
-    return sums[1] + pltpu.roll(sums[0], 1, 1) + pltpu.roll(sums[2], ny - 1, 1)
+    return sums[1].astype(F32) + pltpu.roll(sums[0], 1, 1).astype(F32) + pltpu.roll(sums[2], ny - 1, 1).astype(F32)
 
 
 def depth_conv(taps, values, z):

time: 52.4 us -> 52.4 us (level)
  transfers between devices with their start and end apart: 13 -> 13, of which waited for: 6 -> 6; matrix products, arithmetic and copies ran while one was open for 8% -> 8% of each run, Pallas kernels for 20% -> 21%
where the time goes in v11:
time: 52.4 us; the launch traced here: 52.1 us
  starting transfers between devices  19.1 us (36%)
  Pallas kernels  16.2 us (31%)
  waiting for transfers between devices  10.1 us (19%)
  local copies, waits for them, and re-layouts  4.84 us (9%)
  between operations  0.9 us (2%)
  other arithmetic  0.87 us (2%)
    pallas_call x7, Pallas kernels, call(): pl.pallas_call(kernel, name=name, out_shape=outputs, in_specs=[smem] * sc...  15.7 us
    ppermute x3, starting transfers between devices, exchange(): lax.ppermute(sent[0], 'sp', firsts)  9.92 us
    ppermute x7, starting transfers between devices, all_sum(): lax.ppermute(mine, ('sp', 'dp'), [(i, i ^ step) for i in places])  7.2 us
    ppermute x7, waiting for transfers between devices, all_sum(): lax.ppermute(mine, ('sp', 'dp'), [(i, i ^ step) for i in places])  7.05 us
    ppermute x3, waiting for transfers between devices, exchange(): lax.ppermute(sent[0], 'sp', firsts)  3.09 us
    unnamed x12, local copies, waits for them, and re-layouts  2.9 us
    ppermute x3, starting transfers between devices, exchange(): lax.ppermute(sent[1], 'sp', seconds)  2 us
    another operation x1, local copies, waits for them, and re-layouts, on_device(): cot = cotangent[0].reshape(channels, -1)  1.43 us
  transfers between devices with their start and end apart: 13, of which 6 were waited for; matrix products, arithmetic and copies ran while one was open for 8% of the time, Pallas kernels for 21%

profile of v11, /device:TPU:0, one launch (start us, length us, event | category | flops | bytes accessed | tf_op | source)
XLA Modules:
  0.0 52.1 jit_solution(225343830075345269)
XLA Ops:
  0.6 1.1 %copy-done = bf16[1,96,4,8,128]{4,3,2,1,0:T(8,128)(2,1)S(1)} copy-done((bf16[1,96,4,8,128]{4,3,2,1,0:T(8,128)(2,1)S(1)}, bf16[1,96,4,8,128]{4,3,2,1,0:T(8,128)(2,1)}, u32[]{:S(2)}) %copy-start) | copy-done | bytes 786456
  2.0 3.0 %collective-permute-start = (bf16[96,1024]{1,0:T(8,128)(2,1)S(1)}, bf16[96,1024]{1,0:T(8,128)(2,1)S(1)}, u32[]{:S(2)}, u32[]{:S(2)}) collective-permute-start(bf16[96,1024]{1,0:T(8,128)(2,1)S(1)} %get-tuple-element.49), channel_id=1, source_target_pairs={{0,4},{4,0},{8,12},{12,8},{16,20},{20,16},{24,28},{28,24},{1,5},{5... | collective-permute-start | bytes 589832 | tf_op jit(solution)/shard_map/ppermute | solution.py:459
  6.0 4.3 %collective-permute-start.2 = (bf16[96,1024]{1,0:T(8,128)(2,1)S(1)}, bf16[96,1024]{1,0:T(8,128)(2,1)S(1)}, u32[]{:S(2)}, u32[]{:S(2)}) collective-permute-start(bf16[96,1024]{1,0:T(8,128)(2,1)S(1)} %get-tuple-element.55), channel_id=1, source_target_pairs={{0,4},{4,0},{8,12},{12,8},{16,20},{20,16},{24,28},{28,24},{1,5},{5... | collective-permute-start | bytes 589832 | tf_op jit(solution)/shard_map/ppermute | solution.py:459
  12.4 1.4 %reshape_squeeze.7.cot = bf16[96,4096]{1,0:T(8,128)(2,1)S(1)} reshape(bf16[1,96,4,8,128]{4,3,2,1,0:T(8,128)(2,1)} %param.6) | data formatting | bytes 1572864 | tf_op jit(solution)/shard_map/reshape;squeeze | solution.py:466
  14.6 1.1 %inner.1 = (bf16[96,2048]{1,0:T(8,128)(2,1)S(1)}, bf16[96,2048]{1,0:T(8,128)(2,1)S(1)}, bf16[96,2048]{1,0:T(8,128)(2,1)S(1)}, bf16[96,2048]{1,0:T(8,128)(2,1)S(1)}) custom-call(bf16[96,4096]{1,0:T(8,128)(2,1)S(1)} %reshape_squeeze.6.vol, bf16[2,21,96,128]{3,2,1,0:T(8,128)(2,1)S(1)} %pad_maximum_fusion.taps, bf16[2,96,96]{2,1,0:T(8,128)(2,1)S(1)} %copy-done.2), custom_call_target="tpu_custom_call" | custom-call | bytes 4194304 | tf_op jit(solution)/shard_map/inner/pallas_call | solution.py:397
  15.7 3.1 %collective-permute-done.first = bf16[96,1024]{1,0:T(8,128)(2,1)S(1)} collective-permute-done((bf16[96,1024]{1,0:T(8,128)(2,1)S(1)}, bf16[96,1024]{1,0:T(8,128)(2,1)S(1)}, u32[]{:S(2)}, u32[]{:S(2)}) %collective-permute-start) | collective-permute-done | bytes 196640 | tf_op jit(solution)/shard_map/ppermute | solution.py:459
  18.8 3.1 %middle.1 = (bf16[96,1024]{1,0:T(8,128)(2,1)S(1)}, bf16[96,1024]{1,0:T(8,128)(2,1)S(1)}, bf16[96,2048]{1,0:T(8,128)(2,1)S(1)}, bf16[96,2048]{1,0:T(8,128)(2,1)S(...) custom-call(s32[1]{0:T(128)} %bitcast.odd, ...), custom_call_target="tpu_custom_call" | custom-call | bytes 12582912 | tf_op jit(solution)/shard_map/middle/pallas_call | solution.py:397
  21.9 4.6 %edge.1 = (bf16[96,1024]{1,0:T(8,128)(2,1)S(1)}, bf16[96,1024]{1,0:T(8,128)(2,1)S(1)}, bf16[96,2048]{1,0:T(8,128)(2,1)S(1)}, bf16[96,2048]{1,0:T(8,128)(2,1)S(1)...) custom-call(s32[1]{0:T(128)} %bitcast.odd, ...), custom_call_target="tpu_custom_call" | custom-call | bytes 18874368 | tf_op jit(solution)/shard_map/edge/pallas_call | solution.py:397
  26.5 2.5 %collective-permute-start.7 = (bf16[96,2048]{1,0:T(8,128)(2,1)S(1)}, bf16[96,2048]{1,0:T(8,128)(2,1)S(1)}, u32[]{:S(2)}, u32[]{:S(2)}) collective-permute-start(bf16[96,2048]{1,0:T(8,128)(2,1)S(1)} %get-tuple-element.83), channel_id=1, source_target_pairs={{0,4},{4,0},{8,12},{12,8},{16,20},{20,16},{24,28},{28,24},{1,5},{5... | collective-permute-start | bytes 1179656 | tf_op jit(solution)/shard_map/ppermute | solution.py:459
  29.1 4.2 %weights.1 = (bf16[96,2048]{1,0:T(8,128)(2,1)S(1)}, bf16[224,128]{1,0:T(8,128)(2,1)S(1)}) custom-call(bf16[96,4096]{1,0:T(8,128)(2,1)S(1)} %reshape_squeeze.6.vol, bf16[96,1024]{1,0:T(8,128)(2,1)S(1)} %get-tuple-element.52.lo1, bf16[96,1024]{1,0:T(8,128)(2,1)S(1)} %get-tuple-element.53.hi1, bf16[96,1024]{1,0:T(8,128)(2,1)S(1)} %get-tuple-element.60.lo2, ...), custom_call_target="tpu_custom_call" | custom-call | bytes 1 | tf_op jit(solution)/shard_map/weights/pallas_call | solution.py:397
  33.3 2.0 %collective-permute-start.6 = (bf16[224,128]{1,0:T(8,128)(2,1)S(1)}, bf16[224,128]{1,0:T(8,128)(2,1)S(1)}, u32[]{:S(2)}, u32[]{:S(2)}) collective-permute-start(bf16[224,128]{1,0:T(8,128)(2,1)S(1)} %get-tuple-element.82), channel_id=1, source_target_pairs={{0,24},{1,25},{2,26},{3,27},{4,28},{5,29},{6,30},{7,31},{8,16},{9,... | collective-permute-start | bytes 172040 | tf_op jit(solution)/shard_map/ppermute | solution.py:431
  35.3 0.9 %collective-permute-start.5 = (bf16[224,128]{1,0:T(8,128)(2,1)S(1)}, bf16[224,128]{1,0:T(8,128)(2,1)S(1)}, u32[]{:S(2)}, u32[]{:S(2)}) collective-permute-start(bf16[224,128]{1,0:T(8,128)(2,1)S(1)} %get-tuple-element.82), channel_id=1, source_target_pairs={{0,16},{1,17},{2,18},{3,19},{4,20},{5,21},{6,22},{7,23},{8,24},{9,... | collective-permute-start | bytes 172040 | tf_op jit(solution)/shard_map/ppermute | solution.py:431
  36.2 1.5 %collective-permute-start.4 = (bf16[224,128]{1,0:T(8,128)(2,1)S(1)}, bf16[224,128]{1,0:T(8,128)(2,1)S(1)}, u32[]{:S(2)}, u32[]{:S(2)}) collective-permute-start(bf16[224,128]{1,0:T(8,128)(2,1)S(1)} %get-tuple-element.82), channel_id=1, source_target_pairs={{0,8},{1,9},{2,10},{3,11},{4,12},{5,13},{6,14},{7,15},{8,0},{9,1},... | collective-permute-start | bytes 172040 | tf_op jit(solution)/shard_map/ppermute | solution.py:431
  37.7 0.7 %collective-permute-start.8 = (bf16[96,2048]{1,0:T(8,128)(2,1)S(1)}, bf16[96,2048]{1,0:T(8,128)(2,1)S(1)}, u32[]{:S(2)}, u32[]{:S(2)}) collective-permute-start(bf16[96,2048]{1,0:T(8,128)(2,1)S(1)} %get-tuple-element.85), channel_id=1, source_target_pairs={{4,8},{12,16},{20,24},{8,4},{16,12},{24,20},{5,9},{13,17},{21,25},... | collective-permute-start | bytes 1179656 | tf_op jit(solution)/shard_map/ppermute | solution.py:459
  38.4 1.0 %collective-permute-done.6 = bf16[224,128]{1,0:T(8,128)(2,1)S(1)} collective-permute-done((bf16[224,128]{1,0:T(8,128)(2,1)S(1)}, bf16[224,128]{1,0:T(8,128)(2,1)S(1)}, u32[]{:S(2)}, u32[]{:S(2)}) %collective-permute-start.6) | collective-permute-done | bytes 57376 | tf_op jit(solution)/shard_map/ppermute | solution.py:431
  39.4 2.2 %collective-permute-done.5 = bf16[224,128]{1,0:T(8,128)(2,1)S(1)} collective-permute-done((bf16[224,128]{1,0:T(8,128)(2,1)S(1)}, bf16[224,128]{1,0:T(8,128)(2,1)S(1)}, u32[]{:S(2)}, u32[]{:S(2)}) %collective-permute-start.5) | collective-permute-done | bytes 57376 | tf_op jit(solution)/shard_map/ppermute | solution.py:431
  41.7 1.6 %collective-permute-start.10 = (bf16[224,128]{1,0:T(8,128)(2,1)S(1)}, bf16[224,128]{1,0:T(8,128)(2,1)S(1)}, u32[]{:S(2)}, u32[]{:S(2)}) collective-permute-start(bf16[224,128]{1,0:T(8,128)(2,1)S(1)} %add_convert_fusion.1), channel_id=1, source_target_pairs={{0,2},{1,3},{2,0},{3,1},{4,6},{5,7},{6,4},{7,5},{8,10},{9,11},{10,... | collective-permute-start | bytes 172040 | tf_op jit(solution)/shard_map/ppermute | solution.py:431
  43.5 2.3 %collective-permute-done.11 = bf16[224,128]{1,0:T(8,128)(2,1)S(1)} collective-permute-done((bf16[224,128]{1,0:T(8,128)(2,1)S(1)}, bf16[224,128]{1,0:T(8,128)(2,1)S(1)}, u32[]{:S(2)}, u32[]{:S(2)}) %collective-permute-start.11) | collective-permute-done | bytes 57376 | tf_op jit(solution)/shard_map/ppermute | solution.py:431
  45.9 1.3 %collective-permute-done.10 = bf16[224,128]{1,0:T(8,128)(2,1)S(1)} collective-permute-done((bf16[224,128]{1,0:T(8,128)(2,1)S(1)}, bf16[224,128]{1,0:T(8,128)(2,1)S(1)}, u32[]{:S(2)}, u32[]{:S(2)}) %collective-permute-start.10) | collective-permute-done | bytes 57376 | tf_op jit(solution)/shard_map/ppermute | solution.py:431
  47.2 0.9 %collective-permute-start.12 = (bf16[224,128]{1,0:T(8,128)(2,1)S(1)}, bf16[224,128]{1,0:T(8,128)(2,1)S(1)}, u32[]{:S(2)}, u32[]{:S(2)}) collective-permute-start(bf16[224,128]{1,0:T(8,128)(2,1)S(1)} %add_convert_fusion.refs_0_), channel_id=1, source_target_pairs={{0,4},{1,5},{2,6},{3,7},{4,0},{5,1},{6,2},{7,3},{8,12},{9,13},{10,... | collective-permute-start | bytes 172040 | tf_op jit(solution)/shard_map/ppermute | solution.py:431
  48.0 1.2 %volume.1.own = bf16[96,4096]{1,0:T(8,128)(2,1)S(1)} custom-call(bf16[2,21,96,128]{3,2,1,0:T(8,128)(2,1)S(1)} %pad_maximum_fusion.taps, bf16[96,2048]{1,0:T(8,128)(2,1)S(1)} %get-tuple-element.81.gpl1_i, bf16[96,2048]{1,0:T(8,128)(2,1)S(1)} %get-tuple-element.79.gpl1_lo, bf16[96,2048]{1,0:T(8,128)(2,1)S(1)} %get-tuple-element.80.gpl1_hi), custom_call_target="tpu_custom_call" | custom-call | bytes 1 | tf_op jit(solution)/shard_map/volume/pallas_call | solution.py:397
  49.2 0.8 %final.1 = bf16[96,4096]{1,0:T(8,128)(2,1)S(1)} custom-call(s32[1]{0:T(128)} %bitcast.odd, bf16[2,21,96,128]{3,2,1,0:T(8,128)(2,1)S(1)} %pad_maximum_fusion.taps, bf16[96,4096]{1,0:T(8,128)(2,1)S(1)} %volume.1.own, bf16[96,2048]{1,0:T(8,128)(2,1)S(1)} %collective-permute-done.7.first, bf16[96,2048]{1,0:T(8,128)(2,1)S(1)} %collective-permute-done.8.second), custom_call_target="tpu_custom_call" | custom-call | bytes 1 | tf_op jit(solution)/shard_map/final/pallas_call | solution.py:397
  50.1 1.0 %copy.12 = bf16[12,8,32,128]{3,2,1,0:T(8,128)(2,1)} copy(bf16[12,8,32,128]{3,1,2,0:T(8,128)(2,1)S(1)} %bitcast.18) | data formatting | bytes 1572864
  51.4 0.7 %result.1 = (f32[2,96,96]{2,1,0:T(8,128)}, f32[9,2,96]{2,1,0:T(2,128)}, f32[3,2,96]{2,1,0:T(2,128)}) custom-call(bf16[224,128]{1,0:T(8,128)(2,1)S(1)} %add_convert_fusion.refs_0_, bf16[224,128]{1,0:T(8,128)(2,1)S(1)} %collective-permute-done.12.refs_1_), custom_call_target="tpu_custom_call" | custom-call | bytes 1 | tf_op jit(solution)/shard_map/result/pallas_call | solution.py:397
  (40 shorter events, 4.7 us)
Async XLA Ops:
  0.6 1.1 %copy-start = (bf16[1,96,4,8,128]{4,3,2,1,0:T(8,128)(2,1)S(1)}, bf16[1,96,4,8,128]{4,3,2,1,0:T(8,128)(2,1)}, u32[]{:S(2)}) copy-start(bf16[1,96,4,8,128]{4,3,2,1,0:T(8,128)(2,1)} %vol.2) | copy-start | bytes 2359300
  1.8 9.3 %copy-start.1 = (bf16[1,96,4,8,128]{4,3,2,1,0:T(8,128)(2,1)S(1)}, bf16[1,96,4,8,128]{4,3,2,1,0:T(8,128)(2,1)}, u32[]{:S(2)}) copy-start(bf16[1,96,4,8,128]{4,3,2,1,0:T(8,128)(2,1)} %vol.2) | copy-start | bytes 2359300
  2.0 16.8 %collective-permute-start = (bf16[96,1024]{1,0:T(8,128)(2,1)S(1)}, bf16[96,1024]{1,0:T(8,128)(2,1)S(1)}, u32[]{:S(2)}, u32[]{:S(2)}) collective-permute-start(bf16[96,1024]{1,0:T(8,128)(2,1)S(1)} %get-tuple-element.49), channel_id=1, source_target_pairs={{0,4},{4,0},{8,12},{12,8},{16,20},{20,16},{24,28},{28,24},{1,5},{5... | collective-permute-start | bytes 589832 | tf_op jit(solution)/shard_map/ppermute | solution.py:459
  5.1 13.7 %collective-permute-start.1 = (bf16[96,1024]{1,0:T(8,128)(2,1)S(1)}, bf16[96,1024]{1,0:T(8,128)(2,1)S(1)}, u32[]{:S(2)}, u32[]{:S(2)}) collective-permute-start(bf16[96,1024]{1,0:T(8,128)(2,1)S(1)} %get-tuple-element.50), channel_id=1, source_target_pairs={{4,8},{12,16},{20,24},{8,4},{16,12},{24,20},{5,9},{13,17},{21,25},... | collective-permute-start | bytes 589832 | tf_op jit(solution)/shard_map/ppermute | solution.py:459
  6.0 15.9 %collective-permute-start.2 = (bf16[96,1024]{1,0:T(8,128)(2,1)S(1)}, bf16[96,1024]{1,0:T(8,128)(2,1)S(1)}, u32[]{:S(2)}, u32[]{:S(2)}) collective-permute-start(bf16[96,1024]{1,0:T(8,128)(2,1)S(1)} %get-tuple-element.55), channel_id=1, source_target_pairs={{0,4},{4,0},{8,12},{12,8},{16,20},{20,16},{24,28},{28,24},{1,5},{5... | collective-permute-start | bytes 589832 | tf_op jit(solution)/shard_map/ppermute | solution.py:459
  10.4 11.6 %collective-permute-start.3 = (bf16[96,1024]{1,0:T(8,128)(2,1)S(1)}, bf16[96,1024]{1,0:T(8,128)(2,1)S(1)}, u32[]{:S(2)}, u32[]{:S(2)}) collective-permute-start(bf16[96,1024]{1,0:T(8,128)(2,1)S(1)} %get-tuple-element.56), channel_id=1, source_target_pairs={{4,8},{12,16},{20,24},{8,4},{16,12},{24,20},{5,9},{13,17},{21,25},... | collective-permute-start | bytes 589832 | tf_op jit(solution)/shard_map/ppermute | solution.py:459
  11.1 0.7 %copy-start.4 = (bf16[2,96,3]{1,0,2:T(2,128)(2,1)S(1)}, bf16[2,96,3]{1,0,2:T(2,128)(2,1)}, u32[]{:S(2)}) copy-start(bf16[2,96,3]{1,0,2:T(2,128)(2,1)} %param.8) | copy-start | bytes 3460
  11.1 0.8 %copy-start.3 = (bf16[2,96,3,3]{1,0,3,2:T(2,128)(2,1)S(1)}, bf16[2,96,3,3]{1,0,3,2:T(2,128)(2,1)}, u32[]{:S(2)}) copy-start(bf16[2,96,3,3]{1,0,3,2:T(2,128)(2,1)} %param.7) | copy-start | bytes 10372
  11.4 0.8 %copy-start.2 = (bf16[2,96,96]{2,1,0:T(8,128)(2,1)S(1)}, bf16[2,96,96]{2,1,0:T(8,128)(2,1)}, u32[]{:S(2)}) copy-start(bf16[2,96,96]{2,1,0:T(8,128)(2,1)} %mix.5) | copy-start | bytes 110596
  26.5 15.1 %collective-permute-start.7 = (bf16[96,2048]{1,0:T(8,128)(2,1)S(1)}, bf16[96,2048]{1,0:T(8,128)(2,1)S(1)}, u32[]{:S(2)}, u32[]{:S(2)}) collective-permute-start(bf16[96,2048]{1,0:T(8,128)(2,1)S(1)} %get-tuple-element.83), channel_id=1, source_target_pairs={{0,4},{4,0},{8,12},{12,8},{16,20},{20,16},{24,28},{28,24},{1,5},{5... | collective-permute-start | bytes 1179656 | tf_op jit(solution)/shard_map/ppermute | solution.py:459
  33.3 6.1 %collective-permute-start.6 = (bf16[224,128]{1,0:T(8,128)(2,1)S(1)}, bf16[224,128]{1,0:T(8,128)(2,1)S(1)}, u32[]{:S(2)}, u32[]{:S(2)}) collective-permute-start(bf16[224,128]{1,0:T(8,128)(2,1)S(1)} %get-tuple-element.82), channel_id=1, source_target_pairs={{0,24},{1,25},{2,26},{3,27},{4,28},{5,29},{6,30},{7,31},{8,16},{9,... | collective-permute-start | bytes 172040 | tf_op jit(solution)/shard_map/ppermute | solution.py:431
  35.3 6.3 %collective-permute-start.5 = (bf16[224,128]{1,0:T(8,128)(2,1)S(1)}, bf16[224,128]{1,0:T(8,128)(2,1)S(1)}, u32[]{:S(2)}, u32[]{:S(2)}) collective-permute-start(bf16[224,128]{1,0:T(8,128)(2,1)S(1)} %get-tuple-element.82), channel_id=1, source_target_pairs={{0,16},{1,17},{2,18},{3,19},{4,20},{5,21},{6,22},{7,23},{8,24},{9,... | collective-permute-start | bytes 172040 | tf_op jit(solution)/shard_map/ppermute | solution.py:431
  36.2 5.3 %collective-permute-start.4 = (bf16[224,128]{1,0:T(8,128)(2,1)S(1)}, bf16[224,128]{1,0:T(8,128)(2,1)S(1)}, u32[]{:S(2)}, u32[]{:S(2)}) collective-permute-start(bf16[224,128]{1,0:T(8,128)(2,1)S(1)} %get-tuple-element.82), channel_id=1, source_target_pairs={{0,8},{1,9},{2,10},{3,11},{4,12},{5,13},{6,14},{7,15},{8,0},{9,1},... | collective-permute-start | bytes 172040 | tf_op jit(solution)/shard_map/ppermute | solution.py:431
  37.7 11.5 %collective-permute-start.8 = (bf16[96,2048]{1,0:T(8,128)(2,1)S(1)}, bf16[96,2048]{1,0:T(8,128)(2,1)S(1)}, u32[]{:S(2)}, u32[]{:S(2)}) collective-permute-start(bf16[96,2048]{1,0:T(8,128)(2,1)S(1)} %get-tuple-element.85), channel_id=1, source_target_pairs={{4,8},{12,16},{20,24},{8,4},{16,12},{24,20},{5,9},{13,17},{21,25},... | collective-permute-start | bytes 1179656 | tf_op jit(solution)/shard_map/ppermute | solution.py:459
  41.6 4.2 %collective-permute-start.11 = (bf16[224,128]{1,0:T(8,128)(2,1)S(1)}, bf16[224,128]{1,0:T(8,128)(2,1)S(1)}, u32[]{:S(2)}, u32[]{:S(2)}) collective-permute-start(bf16[224,128]{1,0:T(8,128)(2,1)S(1)} %add_convert_fusion.1), channel_id=1, source_target_pairs={{0,3},{1,2},{2,1},{3,0},{4,7},{5,6},{6,5},{7,4},{8,11},{9,10},{10,... | collective-permute-start | bytes 172040 | tf_op jit(solution)/shard_map/ppermute | solution.py:431
  41.7 5.4 %collective-permute-start.10 = (bf16[224,128]{1,0:T(8,128)(2,1)S(1)}, bf16[224,128]{1,0:T(8,128)(2,1)S(1)}, u32[]{:S(2)}, u32[]{:S(2)}) collective-permute-start(bf16[224,128]{1,0:T(8,128)(2,1)S(1)} %add_convert_fusion.1), channel_id=1, source_target_pairs={{0,2},{1,3},{2,0},{3,1},{4,6},{5,7},{6,4},{7,5},{8,10},{9,11},{10,... | collective-permute-start | bytes 172040 | tf_op jit(solution)/shard_map/ppermute | solution.py:431
  43.2 3.9 %collective-permute-start.9 = (bf16[224,128]{1,0:T(8,128)(2,1)S(1)}, bf16[224,128]{1,0:T(8,128)(2,1)S(1)}, u32[]{:S(2)}, u32[]{:S(2)}) collective-permute-start(bf16[224,128]{1,0:T(8,128)(2,1)S(1)} %add_convert_fusion.1), channel_id=1, source_target_pairs={{0,1},{1,0},{2,3},{3,2},{4,5},{5,4},{6,7},{7,6},{8,9},{9,8},{10,11... | collective-permute-start | bytes 172040 | tf_op jit(solution)/shard_map/ppermute | solution.py:431
  47.2 4.2 %collective-permute-start.12 = (bf16[224,128]{1,0:T(8,128)(2,1)S(1)}, bf16[224,128]{1,0:T(8,128)(2,1)S(1)}, u32[]{:S(2)}, u32[]{:S(2)}) collective-permute-start(bf16[224,128]{1,0:T(8,128)(2,1)S(1)} %add_convert_fusion.refs_0_), channel_id=1, source_target_pairs={{0,4},{1,5},{2,6},{3,7},{4,0},{5,1},{6,2},{7,3},{8,12},{9,13},{10,... | collective-permute-start | bytes 172040 | tf_op jit(solution)/shard_map/ppermute | solution.py:431
